TPU v7x, 32 devices: a whole 2x2x4 slice. The times are simulated.
32 devices in a mesh: pipe: 4 (over y, x), dp: 2 (over core), rep: 4 (over z).
Axes of the slice: x: 2, y: 2, z: 4, core: 2. Of those that a mesh axis runs over, the one named last changes fastest.
Arguments:
- images: bfloat16 [64, 196, 1024], P(('dp', 'rep')), may hold values from -80 to 80
- section_weights: bfloat16 [4, 3407872], P('pipe'), may hold values from -3 to 3
- bn_gain: float32 [4, 4, 4096], P('pipe'), may hold values from 0.25 to 1.75
- bn_bias: float32 [4, 4, 4096], P('pipe'), may hold values from -3 to 3
- width: int32 [8, 2], replicated, may hold values from 128 to 512, as said below
- bn_set: int32 [8, 2], replicated, may hold values from 0 to 3
- gate: int32 [8], replicated, may hold values from 0 to 1, as said below
- cotangent: bfloat16 [64, 49, 2048], P(('dp', 'rep')), may hold values from -16 to 16
Outputs:
- output: bfloat16 [64, 49, 2048], P(('dp', 'rep'), None, 'pipe')
- grad_images: float32 [64, 196, 1024], P(('dp', 'rep'), None, 'pipe')
- grad_weights: float32 [4, 3407872], P('pipe')
- grad_gain: float32 [4, 4, 4096], P('pipe')
- grad_bias: float32 [4, 4, 4096], P('pipe')
Inputs may be any that keep to these rules, and one draw needn't show every extreme that they name: `width`: both bounds occur in every draw. `gate`: every draw has a micro-batch with 1 and one with 0.
All inputs are finite; a program needn't handle non-finite values.
Results may differ from a plain program's by a relative error of at most 0.035.
Values may be sent and summed in bfloat16 or wider, within the bound.
A program may use at most 256 MiB of HBM per device.

v0:
```python
import jax
import jax.numpy as jnp
from jax import lax
from jax.sharding import PartitionSpec as P

C_IN = 1024
C_MID = 512
C_OUT = 2048
SIDE = 14
NSETS = 4
MB = 8
IMG_B = 1
OSIDE = 7
PIX_IN = 196
PIX_OUT = 49
IMG_DEV = 8
P_SIZE = 3407872


EPSILON = 1e-05


def for_sending(array):

    def short(part):
        return part.astype(jnp.bfloat16) if part.dtype == jnp.float32 else part

    return jax.tree.map(short, array)


def shifted(value, axis, steps):
    count = lax.axis_size(axis)
    first, last = (max(0, -steps), min(count, count - steps))
    return lax.ppermute(value, axis, [(source, source + steps) for source in range(first, last)])


def smooth(inputs):
    return inputs * jax.nn.sigmoid(inputs)


def smooth_slope(inputs):
    gate_sig = jax.nn.sigmoid(inputs)
    return gate_sig * (1.0 + inputs * (1.0 - gate_sig))


def matmul(left_op, right_op):
    return jnp.dot(left_op, right_op, preferred_element_type=jnp.float32)


def matmul_left_t(left_op, right_op):
    return lax.dot_general(
        left_op, right_op, (((0,), (0,)), ((), ())), preferred_element_type=jnp.float32
    )


def matmul_right_t(left_op, right_op):
    return lax.dot_general(
        left_op, right_op, (((1,), (1,)), ((), ())), preferred_element_type=jnp.float32
    )


def patches(planes, stride):
    images, side_len, channels = (planes.shape[0], planes.shape[1], planes.shape[3])
    out_side = side_len // stride
    padded = jnp.pad(planes, ((0, 0), (1, 1), (1, 1), (0, 0)))
    pieces = []
    for row_off in range(3):
        for col_off in range(3):
            pieces.append(
                padded[
                    :,
                    row_off : row_off + stride * (out_side - 1) + 1 : stride,
                    col_off : col_off + stride * (out_side - 1) + 1 : stride,
                    :,
                ]
            )
    return jnp.concatenate(pieces, axis=3).reshape(images * out_side * out_side, 9 * channels)


def unpatch(columns, images, side_len, stride, channels):
    out_side = side_len // stride
    pieces = columns.reshape(images, out_side, out_side, 9, channels)
    padded = jnp.zeros((images, side_len + 2, side_len + 2, channels), jnp.float32)
    for row_off in range(3):
        for col_off in range(3):
            padded = padded.at[
                :,
                row_off : row_off + stride * (out_side - 1) + 1 : stride,
                col_off : col_off + stride * (out_side - 1) + 1 : stride,
                :,
            ].add(pieces[:, :, :, row_off * 3 + col_off, :])
    return padded[:, 1 : side_len + 1, 1 : side_len + 1, :]


def group_moments(sums_local, squares_local):
    return (
        lax.psum(sums_local.astype(jnp.bfloat16), "dp").astype(jnp.float32),
        lax.psum(squares_local.astype(jnp.bfloat16), "dp").astype(jnp.float32),
    )


def group_grad_sums(bias_local, gain_local):
    return (
        lax.psum(bias_local.astype(jnp.bfloat16), "dp").astype(jnp.float32),
        lax.psum(gain_local.astype(jnp.bfloat16), "dp").astype(jnp.float32),
    )


def stats_of(sum_all, square_all, start, count, row_total):
    center = sum_all[start : start + count] / row_total
    inv_std = lax.rsqrt(square_all[start : start + count] / row_total - center * center + EPSILON)
    return (center, inv_std)


def norm_grad(slope_in, normed, gain_vec, inv_std, sum_bias, sum_gain, row_total):
    return (
        gain_vec * inv_std * (slope_in - sum_bias / row_total - normed * (sum_gain / row_total))
    ).astype(jnp.bfloat16)


def on_device(images, section_weights, bn_gain, bn_bias, width, bn_set, gate, cotangent):
    section_idx = lax.axis_index("pipe")
    pipe_count = lax.axis_size("pipe")
    dp_count = lax.axis_size("dp")
    flat_weights = section_weights[0]
    gain_table = bn_gain[0]
    bias_table = bn_bias[0]
    rows_in = IMG_B * PIX_IN
    rows_out = IMG_B * PIX_OUT
    total_in = float(rows_in * dp_count)
    total_out = float(rows_out * dp_count)
    wide = 2 * C_OUT
    scr_len = IMG_B * max(PIX_IN * C_MID, PIX_OUT * wide)
    image_blocks = images.reshape(MB, IMG_B, PIX_IN, C_IN)
    pad_mid = jnp.zeros((wide - 2 * C_MID,), jnp.float32)
    zero_wide = jnp.zeros((wide,), jnp.float32)
    zero_scr = jnp.zeros((scr_len,), jnp.float32)
    zero_mid = jnp.zeros((rows_out, C_MID), jnp.bfloat16)
    zero_res = jnp.zeros((rows_out, C_OUT), jnp.bfloat16)
    zero_rows = jnp.zeros((rows_out, C_OUT), jnp.float32)
    zero_input = jnp.zeros((IMG_B, PIX_IN, C_IN), jnp.float32)

    def pack(values):
        flat = values.reshape(-1).astype(jnp.float32)
        return jnp.pad(flat, (0, scr_len - flat.shape[0]))

    def unpack(buffer, rows, cols):
        return buffer[: rows * cols].reshape(rows, cols)

    def place(vec, start):
        return jnp.pad(vec, (start, wide - start - vec.shape[0]))

    def add_weight(acc, grad, offset, valid):
        flat = grad.reshape(-1)
        return acc.at[offset : offset + flat.shape[0]].add(jnp.where(valid, flat, 0.0))

    def weights_zero():
        split_at = C_IN * C_MID
        return (
            flat_weights[:split_at].reshape(C_IN, C_MID),
            flat_weights[split_at : split_at + 9 * C_MID * C_MID].reshape(9 * C_MID, C_MID),
        )

    def weights_one():
        split_at = C_MID * C_OUT
        return (
            flat_weights[:split_at].reshape(C_MID, C_OUT),
            flat_weights[split_at : split_at + C_IN * C_OUT].reshape(C_IN, C_OUT),
        )

    def weights_two():
        split_at = C_OUT * C_MID
        return (
            flat_weights[:split_at].reshape(C_OUT, C_MID),
            flat_weights[split_at : split_at + 9 * C_MID * C_MID].reshape(9 * C_MID, C_MID),
        )

    def short_rows(image_block):
        return image_block.reshape(IMG_B, SIDE, SIDE, C_IN)[:, ::2, ::2, :].reshape(rows_out, C_IN)

    def local_stats(values, start):
        return (
            place(jnp.sum(values, axis=0), start),
            place(jnp.sum(values * values, axis=0), start),
        )

    def fwd_a_zero(ops):
        conv_a, conv_b = weights_zero()
        pre_one = matmul(ops[0].reshape(rows_in, C_IN), conv_a)
        sums_local, squares_local = local_stats(pre_one, 0)
        return (pack(pre_one), sums_local, squares_local)

    def fwd_a_one(ops):
        conv_a, conv_b = weights_one()
        pre_both = jnp.concatenate(
            [matmul(ops[1], conv_a), matmul(short_rows(ops[0]), conv_b)], axis=1
        )
        sums_local, squares_local = local_stats(pre_both, 0)
        return (pack(pre_both), sums_local, squares_local)

    def fwd_a_two(ops):
        conv_a, conv_b = weights_two()
        pre_four = matmul(ops[2], conv_a)
        sums_local, squares_local = local_stats(pre_four, 0)
        return (pack(pre_four), sums_local, squares_local)

    def fwd_a_three(ops):
        conv_a = flat_weights[: C_MID * C_OUT].reshape(C_MID, C_OUT)
        pre_six = matmul(ops[1], conv_a)
        sums_local, squares_local = local_stats(pre_six, 0)
        return (pack(pre_six), sums_local, squares_local)

    def fwd_b_zero(args):
        ops, scratch, sum_all, square_all = args
        conv_a, conv_b = weights_zero()
        gain_vec, bias_vec, mask_vec = (ops[3], ops[4], ops[5])
        pre_one = unpack(scratch, rows_in, C_MID)
        center_one, inv_one = stats_of(sum_all, square_all, 0, C_MID, total_in)
        hidden_one = (
            smooth((pre_one - center_one) * inv_one * gain_vec[:C_MID] + bias_vec[:C_MID])
            * mask_vec
        ).astype(jnp.bfloat16)
        pre_two = matmul(patches(hidden_one.reshape(IMG_B, SIDE, SIDE, C_MID), 2), conv_b)
        sums_local, squares_local = local_stats(pre_two, C_MID)
        return (pack(pre_two), sums_local, squares_local)

    def fwd_b_pass(args):
        return (args[1], zero_wide, zero_wide)

    def fwd_b_two(args):
        ops, scratch, sum_all, square_all = args
        conv_a, conv_b = weights_two()
        gain_vec, bias_vec, mask_vec = (ops[3], ops[4], ops[5])
        pre_four = unpack(scratch, rows_out, C_MID)
        center_four, inv_four = stats_of(sum_all, square_all, 0, C_MID, total_out)
        hidden_four = (
            smooth((pre_four - center_four) * inv_four * gain_vec[:C_MID] + bias_vec[:C_MID])
            * mask_vec
        ).astype(jnp.bfloat16)
        pre_five = matmul(patches(hidden_four.reshape(IMG_B, OSIDE, OSIDE, C_MID), 1), conv_b)
        sums_local, squares_local = local_stats(pre_five, C_MID)
        return (pack(pre_five), sums_local, squares_local)

    def fwd_c_double(args, first_total, send_res):
        ops, scratch, sum_all, square_all = args
        gain_vec, bias_vec, mask_vec = (ops[3], ops[4], ops[5])
        pre_two = unpack(scratch, rows_out, C_MID)
        center_one, inv_one = stats_of(sum_all, square_all, 0, C_MID, first_total)
        center_two, inv_two = stats_of(sum_all, square_all, C_MID, C_MID, total_out)
        hidden_two = (
            smooth(
                (pre_two - center_two) * inv_two * gain_vec[C_MID : 2 * C_MID]
                + bias_vec[C_MID : 2 * C_MID]
            )
            * mask_vec
        ).astype(jnp.bfloat16)
        centers = jnp.concatenate([center_one, center_two, pad_mid])
        scales = jnp.concatenate([inv_one, inv_two, pad_mid])
        return (hidden_two, send_res, centers, scales, zero_rows)

    def fwd_c_zero(args):
        return fwd_c_double(args, total_in, zero_res)

    def fwd_c_two(args):
        return fwd_c_double(args, total_out, args[0][2])

    def fwd_c_one(args):
        ops, scratch, sum_all, square_all = args
        gain_vec, bias_vec = (ops[3], ops[4])
        pre_both = unpack(scratch, rows_out, wide)
        centers, scales = stats_of(sum_all, square_all, 0, wide, total_out)
        activ = (pre_both - centers) * scales * gain_vec + bias_vec
        block_out = smooth(activ[:, :C_OUT] + activ[:, C_OUT:]).astype(jnp.bfloat16)
        return (zero_mid, block_out, centers, scales, zero_rows)

    def fwd_c_three(args):
        ops, scratch, sum_all, square_all = args
        gain_vec, bias_vec, gate_val = (ops[3], ops[4], ops[6])
        pre_six = unpack(scratch, rows_out, C_OUT)
        centers, scales = stats_of(sum_all, square_all, 0, wide, total_out)
        residual = ops[2].astype(jnp.float32)
        merged = smooth(
            residual
            + (pre_six - centers[:C_OUT]) * scales[:C_OUT] * gain_vec[:C_OUT]
            + bias_vec[:C_OUT]
        )
        result = gate_val * merged + (1.0 - gate_val) * residual
        return (zero_mid, zero_res, centers, scales, result)

    def bwd_a_double(ops, flat_in, conv_a, conv_b, side_len, stride):
        centers, scales, grad_mid = (ops[3], ops[4], ops[5])
        gain_vec, bias_vec, mask_vec = (ops[8], ops[9], ops[10])
        norm_one = (matmul(flat_in, conv_a) - centers[:C_MID]) * scales[:C_MID]
        hidden_one = (smooth(norm_one * gain_vec[:C_MID] + bias_vec[:C_MID]) * mask_vec).astype(
            jnp.bfloat16
        )
        columns = patches(hidden_one.reshape(IMG_B, side_len, side_len, C_MID), stride)
        norm_two = (matmul(columns, conv_b) - centers[C_MID : 2 * C_MID]) * scales[
            C_MID : 2 * C_MID
        ]
        act_two = norm_two * gain_vec[C_MID : 2 * C_MID] + bias_vec[C_MID : 2 * C_MID]
        slope_two = grad_mid.astype(jnp.float32) * mask_vec * smooth_slope(act_two)
        return (
            pack(slope_two),
            pack(norm_two),
            pack(norm_one),
            place(jnp.sum(slope_two, axis=0), C_MID),
            place(jnp.sum(slope_two * norm_two, axis=0), C_MID),
        )

    def bwd_a_zero(ops):
        conv_a, conv_b = weights_zero()
        return bwd_a_double(ops, ops[0].reshape(rows_in, C_IN), conv_a, conv_b, SIDE, 2)

    def bwd_a_two(ops):
        conv_a, conv_b = weights_two()
        return bwd_a_double(ops, ops[2], conv_a, conv_b, OSIDE, 1)

    def bwd_a_one(ops):
        conv_a, conv_b = weights_one()
        centers, scales, grad_res = (ops[3], ops[4], ops[6])
        gain_vec, bias_vec = (ops[8], ops[9])
        pre_both = jnp.concatenate(
            [matmul(ops[1], conv_a), matmul(short_rows(ops[0]), conv_b)], axis=1
        )
        normed = (pre_both - centers) * scales
        activ = normed * gain_vec + bias_vec
        slope_in = grad_res.astype(jnp.float32) * smooth_slope(activ[:, :C_OUT] + activ[:, C_OUT:])
        both = jnp.concatenate([slope_in, slope_in], axis=1)
        return (
            pack(both),
            pack(normed),
            zero_scr,
            jnp.sum(both, axis=0),
            jnp.sum(both * normed, axis=0),
        )

    def bwd_a_three(ops):
        conv_a = flat_weights[: C_MID * C_OUT].reshape(C_MID, C_OUT)
        centers, scales = (ops[3], ops[4])
        gain_vec, bias_vec, gate_val = (ops[8], ops[9], ops[11])
        normed = (matmul(ops[1], conv_a) - centers[:C_OUT]) * scales[:C_OUT]
        joined = ops[2].astype(jnp.float32) + normed * gain_vec[:C_OUT] + bias_vec[:C_OUT]
        through = ops[7].astype(jnp.float32) * gate_val * smooth_slope(joined)
        return (
            pack(through),
            pack(normed),
            zero_scr,
            place(jnp.sum(through, axis=0), 0),
            place(jnp.sum(through * normed, axis=0), 0),
        )

    def bwd_b_double(args, conv_b, rows_first, side_len, stride, offset):
        ops, first_buf, second_buf, third_buf, sum_bias, sum_gain, acc = args
        scales = ops[4]
        gain_vec, bias_vec, mask_vec, valid = (ops[8], ops[9], ops[10], ops[12])
        slope_two = unpack(first_buf, rows_out, C_MID)
        norm_two = unpack(second_buf, rows_out, C_MID)
        norm_one = unpack(third_buf, rows_first, C_MID)
        grad_two = norm_grad(
            slope_two,
            norm_two,
            gain_vec[C_MID : 2 * C_MID],
            scales[C_MID : 2 * C_MID],
            sum_bias[C_MID : 2 * C_MID],
            sum_gain[C_MID : 2 * C_MID],
            total_out,
        )
        act_one = norm_one * gain_vec[:C_MID] + bias_vec[:C_MID]
        hidden_one = (smooth(act_one) * mask_vec).astype(jnp.bfloat16)
        columns = patches(hidden_one.reshape(IMG_B, side_len, side_len, C_MID), stride)
        acc = add_weight(acc, matmul_left_t(columns, grad_two), offset, valid)
        hid_grad = unpatch(
            matmul_right_t(grad_two, conv_b), IMG_B, side_len, stride, C_MID
        ).reshape(rows_first, C_MID)
        slope_one = hid_grad * mask_vec * smooth_slope(act_one)
        return (
            pack(slope_one),
            second_buf,
            third_buf,
            place(jnp.sum(slope_one, axis=0), 0),
            place(jnp.sum(slope_one * norm_one, axis=0), 0),
            acc,
        )

    def bwd_b_zero(args):
        conv_a, conv_b = weights_zero()
        return bwd_b_double(args, conv_b, rows_in, SIDE, 2, C_IN * C_MID)

    def bwd_b_two(args):
        conv_a, conv_b = weights_two()
        return bwd_b_double(args, conv_b, rows_out, OSIDE, 1, C_OUT * C_MID)

    def bwd_b_pass(args):
        return (args[1], args[2], args[3], zero_wide, zero_wide, args[6])

    def side_none():
        return zero_input

    def bwd_c_zero(args):
        ops, first_buf, second_buf, third_buf, sum_bias, sum_gain, acc = args
        conv_a, conv_b = weights_zero()
        scales, gain_vec, valid = (ops[4], ops[8], ops[12])
        flat_in = ops[0].reshape(rows_in, C_IN)
        slope_one = unpack(first_buf, rows_in, C_MID)
        norm_one = unpack(third_buf, rows_in, C_MID)
        grad_one = norm_grad(
            slope_one,
            norm_one,
            gain_vec[:C_MID],
            scales[:C_MID],
            sum_bias[:C_MID],
            sum_gain[:C_MID],
            total_in,
        )
        acc = add_weight(acc, matmul_left_t(flat_in, grad_one), 0, valid)
        side_out = matmul_right_t(grad_one, conv_a).reshape(IMG_B, PIX_IN, C_IN)
        return (zero_mid, zero_res, acc, side_out)

    def bwd_c_one(args):
        ops, first_buf, second_buf, third_buf, sum_bias, sum_gain, acc = args
        conv_a, conv_b = weights_one()
        scales, gain_vec, valid = (ops[4], ops[8], ops[12])
        short_in = short_rows(ops[0])
        both = unpack(first_buf, rows_out, wide)
        normed = unpack(second_buf, rows_out, wide)
        grad_both = norm_grad(both, normed, gain_vec, scales, sum_bias, sum_gain, total_out)
        acc = add_weight(acc, matmul_left_t(ops[1], grad_both[:, :C_OUT]), 0, valid)
        acc = add_weight(acc, matmul_left_t(short_in, grad_both[:, C_OUT:]), C_MID * C_OUT, valid)
        mid_grad = matmul_right_t(grad_both[:, :C_OUT], conv_a).astype(jnp.bfloat16)
        short_grad = matmul_right_t(grad_both[:, C_OUT:], conv_b).reshape(
            IMG_B, OSIDE, 1, OSIDE, 1, C_IN
        )
        side_out = jnp.pad(short_grad, ((0, 0), (0, 0), (0, 1), (0, 0), (0, 1), (0, 0))).reshape(
            IMG_B, PIX_IN, C_IN
        )
        return (mid_grad, zero_res, acc, side_out)

    def bwd_c_two(args):
        ops, first_buf, second_buf, third_buf, sum_bias, sum_gain, acc = args
        conv_a, conv_b = weights_two()
        scales, grad_res, gain_vec, valid = (ops[4], ops[6], ops[8], ops[12])
        slope_four = unpack(first_buf, rows_out, C_MID)
        norm_four = unpack(third_buf, rows_out, C_MID)
        grad_four = norm_grad(
            slope_four,
            norm_four,
            gain_vec[:C_MID],
            scales[:C_MID],
            sum_bias[:C_MID],
            sum_gain[:C_MID],
            total_out,
        )
        acc = add_weight(acc, matmul_left_t(ops[2], grad_four), 0, valid)
        carried_grad = (grad_res.astype(jnp.float32) + matmul_right_t(grad_four, conv_a)).astype(
            jnp.bfloat16
        )
        return (zero_mid, carried_grad, acc, side_none())

    def bwd_c_three(args):
        ops, first_buf, second_buf, third_buf, sum_bias, sum_gain, acc = args
        conv_a = flat_weights[: C_MID * C_OUT].reshape(C_MID, C_OUT)
        scales, gain_vec, gate_val, valid = (ops[4], ops[8], ops[11], ops[12])
        through = unpack(first_buf, rows_out, C_OUT)
        normed = unpack(second_buf, rows_out, C_OUT)
        res_grad = (through + (1.0 - gate_val) * ops[7].astype(jnp.float32)).astype(jnp.bfloat16)
        grad_six = norm_grad(
            through,
            normed,
            gain_vec[:C_OUT],
            scales[:C_OUT],
            sum_bias[:C_OUT],
            sum_gain[:C_OUT],
            total_out,
        )
        acc = add_weight(acc, matmul_left_t(ops[1], grad_six), 0, valid)
        mid_grad = matmul_right_t(grad_six, conv_a).astype(jnp.bfloat16)
        return (mid_grad, res_grad, acc, side_none())

    def select_params(micro_idx):
        block_id = section_idx // 2
        width_val = width[micro_idx, block_id]
        set_val = bn_set[micro_idx, block_id]
        onehot = (jnp.arange(NSETS) == set_val).astype(jnp.float32)
        gain_vec = jnp.sum(onehot[:, None] * gain_table, axis=0)
        bias_vec = jnp.sum(onehot[:, None] * bias_table, axis=0)
        mask_vec = (jnp.arange(C_MID) < width_val).astype(jnp.float32)
        gate_val = gate[micro_idx].astype(jnp.float32)
        return (gain_vec, bias_vec, mask_vec, gate_val, onehot)

    fwd_first = [fwd_a_zero, fwd_a_one, fwd_a_two, fwd_a_three]
    fwd_second = [fwd_b_zero, fwd_b_pass, fwd_b_two, fwd_b_pass]
    fwd_third = [fwd_c_zero, fwd_c_one, fwd_c_two, fwd_c_three]
    bwd_first = [bwd_a_zero, bwd_a_one, bwd_a_two, bwd_a_three]
    bwd_second = [bwd_b_zero, bwd_b_pass, bwd_b_two, bwd_b_pass]
    bwd_third = [bwd_c_zero, bwd_c_one, bwd_c_two, bwd_c_three]

    def forward_tick(tick_no, state_in):
        recv_mid, recv_res, stash_mid, stash_res, stash_center, stash_scale, out_rows = state_in
        micro_raw = tick_no - section_idx
        is_valid = (micro_raw >= 0) & (micro_raw < MB)
        micro_idx = jnp.clip(micro_raw, 0, MB - 1)
        gain_vec, bias_vec, mask_vec, gate_val, onehot = select_params(micro_idx)
        ops = (image_blocks[micro_idx], recv_mid, recv_res, gain_vec, bias_vec, mask_vec, gate_val)
        scratch, sums_local, squares_local = lax.switch(section_idx, fwd_first, ops)
        sum_first, square_first = group_moments(sums_local, squares_local)
        scratch, sums_local, squares_local = lax.switch(
            section_idx, fwd_second, (ops, scratch, sum_first, square_first)
        )
        sum_second, square_second = group_moments(sums_local, squares_local)
        send_mid, send_res, centers, scales, result = lax.switch(
            section_idx,
            fwd_third,
            (ops, scratch, sum_first + sum_second, square_first + square_second),
        )
        stash_mid = stash_mid.at[micro_idx].set(jnp.where(is_valid, recv_mid, stash_mid[micro_idx]))
        stash_res = stash_res.at[micro_idx].set(jnp.where(is_valid, recv_res, stash_res[micro_idx]))
        stash_center = stash_center.at[micro_idx].set(
            jnp.where(is_valid, centers, stash_center[micro_idx])
        )
        stash_scale = stash_scale.at[micro_idx].set(
            jnp.where(is_valid, scales, stash_scale[micro_idx])
        )
        out_rows = out_rows.at[micro_idx].set(jnp.where(is_valid, result, out_rows[micro_idx]))
        recv_mid, recv_res = (
            shifted(for_sending(send_mid), "pipe", 1).astype(send_mid.dtype),
            shifted(for_sending(send_res), "pipe", 1).astype(send_res.dtype),
        )
        return (recv_mid, recv_res, stash_mid, stash_res, stash_center, stash_scale, out_rows)

    forward_init = (
        zero_mid,
        zero_res,
        jnp.zeros((MB, rows_out, C_MID), jnp.bfloat16),
        jnp.zeros((MB, rows_out, C_OUT), jnp.bfloat16),
        jnp.zeros((MB, wide), jnp.float32),
        jnp.zeros((MB, wide), jnp.float32),
        jnp.zeros((MB, rows_out, C_OUT), jnp.float32),
    )
    forward_state = lax.fori_loop(0, MB + pipe_count - 1, forward_tick, forward_init)
    unused_mid, unused_res, stash_mid, stash_res, stash_center, stash_scale, out_rows = (
        forward_state
    )

    def backward_tick(tick_no, state_in):
        grad_mid, grad_res, weight_acc, gain_acc, bias_acc, input_acc = state_in
        micro_raw = tick_no - (pipe_count - 1 - section_idx)
        is_valid = (micro_raw >= 0) & (micro_raw < MB)
        micro_idx = jnp.clip(micro_raw, 0, MB - 1)
        gain_vec, bias_vec, mask_vec, gate_val, onehot = select_params(micro_idx)
        ops = (
            image_blocks[micro_idx],
            stash_mid[micro_idx],
            stash_res[micro_idx],
            stash_center[micro_idx],
            stash_scale[micro_idx],
            grad_mid,
            grad_res,
            cotangent[micro_idx],
            gain_vec,
            bias_vec,
            mask_vec,
            gate_val,
            is_valid,
        )
        first_buf, second_buf, third_buf, bias_one, gain_one = lax.switch(
            section_idx, bwd_first, ops
        )
        sum_bias_one, sum_gain_one = group_grad_sums(bias_one, gain_one)
        first_buf, second_buf, third_buf, bias_two, gain_two, weight_acc = lax.switch(
            section_idx,
            bwd_second,
            (ops, first_buf, second_buf, third_buf, sum_bias_one, sum_gain_one, weight_acc),
        )
        sum_bias_two, sum_gain_two = group_grad_sums(bias_two, gain_two)
        send_mid, send_res, weight_acc, side_out = lax.switch(
            section_idx,
            bwd_third,
            (
                ops,
                first_buf,
                second_buf,
                third_buf,
                sum_bias_one + sum_bias_two,
                sum_gain_one + sum_gain_two,
                weight_acc,
            ),
        )
        gain_grad = gain_one + gain_two
        bias_grad = bias_one + bias_two
        gain_acc = jnp.where(is_valid, gain_acc + onehot[:, None] * gain_grad[None, :], gain_acc)
        bias_acc = jnp.where(is_valid, bias_acc + onehot[:, None] * bias_grad[None, :], bias_acc)
        input_acc = jax.tree.map(
            lambda stored, fresh: stored.at[micro_idx].set(
                jnp.where(is_valid, fresh, stored[micro_idx])
            ),
            input_acc,
            side_out,
        )
        grad_mid, grad_res = (
            shifted(for_sending(send_mid), "pipe", -1).astype(send_mid.dtype),
            shifted(for_sending(send_res), "pipe", -1).astype(send_res.dtype),
        )
        return (grad_mid, grad_res, weight_acc, gain_acc, bias_acc, input_acc)

    side_init = jnp.zeros((MB, IMG_B, PIX_IN, C_IN), jnp.float32)
    backward_init = (
        zero_mid,
        zero_res,
        jnp.zeros((P_SIZE,), jnp.float32),
        jnp.zeros((NSETS, wide), jnp.float32),
        jnp.zeros((NSETS, wide), jnp.float32),
        side_init,
    )
    backward_state = lax.fori_loop(0, MB + pipe_count - 1, backward_tick, backward_init)
    unused_gmid, unused_gres, weight_acc, gain_acc, bias_acc, input_acc = backward_state
    grad_images, output_sum = (
        lax.psum_scatter(
            input_acc.reshape(IMG_DEV, PIX_IN, C_IN).astype(jnp.bfloat16),
            "pipe",
            scatter_dimension=2,
            tiled=True,
        ).astype(jnp.float32),
        lax.psum_scatter(
            out_rows.astype(jnp.bfloat16), "pipe", scatter_dimension=2, tiled=True
        ).astype(jnp.float32),
    )
    output_part = output_sum.astype(jnp.bfloat16)
    norm_grads = jnp.concatenate([gain_acc.reshape(-1), bias_acc.reshape(-1)])
    weight_sum, norm_sum = lax.psum((weight_acc, norm_grads), ("dp", "rep"))
    grad_gain = norm_sum[: NSETS * wide].reshape(1, NSETS, wide)
    grad_bias = norm_sum[NSETS * wide :].reshape(1, NSETS, wide)
    return (output_part, grad_images, weight_sum.reshape(1, P_SIZE), grad_gain, grad_bias)


def solution(mesh):
    placed = (
        P(("dp", "rep"), None, None),
        P("pipe", None),
        P("pipe", None, None),
        P("pipe", None, None),
        P(),
        P(),
        P(),
        P(("dp", "rep"), None, None),
    )
    return jax.shard_map(
        on_device,
        mesh=mesh,
        in_specs=placed,
        out_specs=(
            P(("dp", "rep"), None, "pipe"),
            P(("dp", "rep"), None, "pipe"),
            P("pipe", None),
            P("pipe", None, None),
            P("pipe", None, None),
        ),
        check_vma=False,
    )
```

profile of v0, /device:TPU:5, one launch (start us, length us, event | category | flops | bytes accessed | tf_op | source)
XLA Modules:
  0.0 3535.0 jit_solution(16291322402475116286)
XLA Ops:
  15.7 145.3 %reduce.88 = bf16[3407872]{0:T(1024)(128)(2,1)} reduce(bf16[1,3407872]{1,0:T(2,128)(2,1)} %param.81, bf16[]{:T(256)} %constant.1340), dimensions={0}, to_apply=%param.81.reduce_sub_computation | reduce | bytes 13631490 | tf_op args[1]
  165.2 701.1 %while.77 = (s32[]{:T(128)}, bf16[49,512]{1,0:T(8,128)(2,1)S(1)}, bf16[49,2048]{1,0:T(8,128)(2,1)S(1)}, bf16[8,49,512]{2,1,0:T(8,128)(2,1)S(1)}, bf16[8,49,2048]...) while((s32[]{:T(128)}, bf16[49,512]{1,0:T(8,128)(2,1)S(1)}, ...), condition=%wide.region_33.34_spmd, body=%wide.region_0.33_spmd.sunk | while | flops 543368192 | bytes 78632848 | solution.py:540
  181.0 18.0 conditional.16
  243.7 18.0 conditional.16
  306.3 18.0 conditional.16
  370.4 18.0 conditional.16
  434.5 18.0 conditional.16
  498.5 18.0 conditional.16
  562.6 18.0 conditional.16
  626.7 18.0 conditional.16
  690.8 18.0 conditional.16
  754.8 18.0 conditional.16
  818.9 18.0 conditional.16
  874.4 2359.8 %while.78 = (s32[]{:T(128)}, bf16[49,512]{1,0:T(8,128)(2,1)S(1)}, bf16[49,2048]{1,0:T(8,128)(2,1)}, f32[3407872]{0:T(1024)}, f32[4,4096]{1,0:T(4,128)}, /*index=...) while((s32[]{:T(128)}, bf16[49,512]{1,0:T(8,128)(2,1)S(1)}, ...), condition=%wide.region_77.78_spmd.clone, body=%wide.region_35.77_spmd.clone.sunk | while | flops 1531920384 | bytes 303546656 | solution.py:615
  885.1 28.0 conditional.18
  918.6 91.9 %conditional.19 = (f32[200704]{0:T(1024)S(1)}, f32[4096]{0:T(1024)}, f32[4096]{0:T(1024)}, f32[3407872]{0:T(1024)}) conditional(s32[]{:T(128)} %get-tuple-element.2871, (f32[4096]{0:T(1024)S(1)}, f32[4096]{0:T(1024)S(1)}, f32[200704]{0:T(1024)S(1)}, f32[4096]{0:T(1024)S(1)}, f32[200704]{0:T(1024)S(1)}, ...), branch_computations={%region_52.63_spmd, %region_64.64_spmd, %region_65.68_spmd, %regio... | conditional | flops 469199872 | bytes 100038712 | solution.py:570
  1018.0 33.5 conditional.20
  1053.6 17.6 collective-permute-start.3
  1077.4 15.5 scatter.71
  1104.2 28.0 conditional.18
  1138.3 91.9 %conditional.19 = (f32[200704]{0:T(1024)S(1)}, f32[4096]{0:T(1024)}, f32[4096]{0:T(1024)}, f32[3407872]{0:T(1024)}) conditional(s32[]{:T(128)} %get-tuple-element.2871, (f32[4096]{0:T(1024)S(1)}, f32[4096]{0:T(1024)S(1)}, f32[200704]{0:T(1024)S(1)}, f32[4096]{0:T(1024)S(1)}, f32[200704]{0:T(1024)S(1)}, ...), branch_computations={%region_52.63_spmd, %region_64.64_spmd, %region_65.68_spmd, %regio... | conditional | flops 469199872 | bytes 100038712 | solution.py:570
  1237.7 33.3 conditional.20
  1273.1 11.7 collective-permute-start.3
  1291.4 15.5 scatter.71
  1318.5 28.0 conditional.18
  1352.5 91.7 %conditional.19 = (f32[200704]{0:T(1024)S(1)}, f32[4096]{0:T(1024)}, f32[4096]{0:T(1024)}, f32[3407872]{0:T(1024)}) conditional(s32[]{:T(128)} %get-tuple-element.2871, (f32[4096]{0:T(1024)S(1)}, f32[4096]{0:T(1024)S(1)}, f32[200704]{0:T(1024)S(1)}, f32[4096]{0:T(1024)S(1)}, f32[200704]{0:T(1024)S(1)}, ...), branch_computations={%region_52.63_spmd, %region_64.64_spmd, %region_65.68_spmd, %regio... | conditional | flops 469199872 | bytes 100038712 | solution.py:570
  1451.7 33.5 conditional.20
  1505.1 15.5 scatter.71
  1532.0 28.0 conditional.18
  1566.1 91.9 %conditional.19 = (f32[200704]{0:T(1024)S(1)}, f32[4096]{0:T(1024)}, f32[4096]{0:T(1024)}, f32[3407872]{0:T(1024)}) conditional(s32[]{:T(128)} %get-tuple-element.2871, (f32[4096]{0:T(1024)S(1)}, f32[4096]{0:T(1024)S(1)}, f32[200704]{0:T(1024)S(1)}, f32[4096]{0:T(1024)S(1)}, f32[200704]{0:T(1024)S(1)}, ...), branch_computations={%region_52.63_spmd, %region_64.64_spmd, %region_65.68_spmd, %regio... | conditional | flops 469199872 | bytes 100038712 | solution.py:570
  1665.5 33.5 conditional.20
  1718.9 15.5 scatter.71
  1745.7 28.0 conditional.18
  1779.8 91.9 %conditional.19 = (f32[200704]{0:T(1024)S(1)}, f32[4096]{0:T(1024)}, f32[4096]{0:T(1024)}, f32[3407872]{0:T(1024)}) conditional(s32[]{:T(128)} %get-tuple-element.2871, (f32[4096]{0:T(1024)S(1)}, f32[4096]{0:T(1024)S(1)}, f32[200704]{0:T(1024)S(1)}, f32[4096]{0:T(1024)S(1)}, f32[200704]{0:T(1024)S(1)}, ...), branch_computations={%region_52.63_spmd, %region_64.64_spmd, %region_65.68_spmd, %regio... | conditional | flops 469199872 | bytes 100038712 | solution.py:570
  1879.2 33.3 conditional.20
  1932.9 15.5 scatter.71
  1960.0 28.0 conditional.18
  1994.0 91.7 %conditional.19 = (f32[200704]{0:T(1024)S(1)}, f32[4096]{0:T(1024)}, f32[4096]{0:T(1024)}, f32[3407872]{0:T(1024)}) conditional(s32[]{:T(128)} %get-tuple-element.2871, (f32[4096]{0:T(1024)S(1)}, f32[4096]{0:T(1024)S(1)}, f32[200704]{0:T(1024)S(1)}, f32[4096]{0:T(1024)S(1)}, f32[200704]{0:T(1024)S(1)}, ...), branch_computations={%region_52.63_spmd, %region_64.64_spmd, %region_65.68_spmd, %regio... | conditional | flops 469199872 | bytes 100038712 | solution.py:570
  2093.2 33.5 conditional.20
  2146.9 15.5 scatter.71
  2173.8 28.0 conditional.18
  2207.8 91.9 %conditional.19 = (f32[200704]{0:T(1024)S(1)}, f32[4096]{0:T(1024)}, f32[4096]{0:T(1024)}, f32[3407872]{0:T(1024)}) conditional(s32[]{:T(128)} %get-tuple-element.2871, (f32[4096]{0:T(1024)S(1)}, f32[4096]{0:T(1024)S(1)}, f32[200704]{0:T(1024)S(1)}, f32[4096]{0:T(1024)S(1)}, f32[200704]{0:T(1024)S(1)}, ...), branch_computations={%region_52.63_spmd, %region_64.64_spmd, %region_65.68_spmd, %regio... | conditional | flops 469199872 | bytes 100038712 | solution.py:570
  2307.2 33.5 conditional.20
  2360.9 15.5 scatter.71
  2387.7 28.0 conditional.18
  2421.8 91.9 %conditional.19 = (f32[200704]{0:T(1024)S(1)}, f32[4096]{0:T(1024)}, f32[4096]{0:T(1024)}, f32[3407872]{0:T(1024)}) conditional(s32[]{:T(128)} %get-tuple-element.2871, (f32[4096]{0:T(1024)S(1)}, f32[4096]{0:T(1024)S(1)}, f32[200704]{0:T(1024)S(1)}, f32[4096]{0:T(1024)S(1)}, f32[200704]{0:T(1024)S(1)}, ...), branch_computations={%region_52.63_spmd, %region_64.64_spmd, %region_65.68_spmd, %regio... | conditional | flops 469199872 | bytes 100038712 | solution.py:570
  2521.2 33.3 conditional.20
  2556.6 11.7 collective-permute-start.3
  2574.9 15.5 scatter.71
  2602.0 28.0 conditional.18
  2636.0 91.7 %conditional.19 = (f32[200704]{0:T(1024)S(1)}, f32[4096]{0:T(1024)}, f32[4096]{0:T(1024)}, f32[3407872]{0:T(1024)}) conditional(s32[]{:T(128)} %get-tuple-element.2871, (f32[4096]{0:T(1024)S(1)}, f32[4096]{0:T(1024)S(1)}, f32[200704]{0:T(1024)S(1)}, f32[4096]{0:T(1024)S(1)}, f32[200704]{0:T(1024)S(1)}, ...), branch_computations={%region_52.63_spmd, %region_64.64_spmd, %region_65.68_spmd, %regio... | conditional | flops 469199872 | bytes 100038712 | solution.py:570
  2735.2 33.5 conditional.20
  2788.9 15.5 scatter.71
  2815.8 28.0 conditional.18
  2849.8 91.9 %conditional.19 = (f32[200704]{0:T(1024)S(1)}, f32[4096]{0:T(1024)}, f32[4096]{0:T(1024)}, f32[3407872]{0:T(1024)}) conditional(s32[]{:T(128)} %get-tuple-element.2871, (f32[4096]{0:T(1024)S(1)}, f32[4096]{0:T(1024)S(1)}, f32[200704]{0:T(1024)S(1)}, f32[4096]{0:T(1024)S(1)}, f32[200704]{0:T(1024)S(1)}, ...), branch_computations={%region_52.63_spmd, %region_64.64_spmd, %region_65.68_spmd, %regio... | conditional | flops 469199872 | bytes 100038712 | solution.py:570
  2949.2 33.5 conditional.20
  3002.6 15.5 scatter.71
  3029.5 28.0 conditional.18
  3063.5 91.9 %conditional.19 = (f32[200704]{0:T(1024)S(1)}, f32[4096]{0:T(1024)}, f32[4096]{0:T(1024)}, f32[3407872]{0:T(1024)}) conditional(s32[]{:T(128)} %get-tuple-element.2871, (f32[4096]{0:T(1024)S(1)}, f32[4096]{0:T(1024)S(1)}, f32[200704]{0:T(1024)S(1)}, f32[4096]{0:T(1024)S(1)}, f32[200704]{0:T(1024)S(1)}, ...), branch_computations={%region_52.63_spmd, %region_64.64_spmd, %region_65.68_spmd, %regio... | conditional | flops 469199872 | bytes 100038712 | solution.py:570
  3162.9 33.3 conditional.20
  3198.3 12.0 collective-permute-start.3
  3216.6 15.5 scatter.71
  3237.4 41.9 %reduce-scatter.5.cloned.1.call-done = bf16[8,196,256]{2,0,1:T(8,128)(2,1)} async-done(((bf16[8,196,1024]{2,0,1:T(8,128)(2,1)}), bf16[8,196,256]{2,0,1:T(8,128)(2,1)}) %reduce-scatter.5.cloned.1.call-update) | async-done | bytes 802832 | tf_op jit(solution)/shard_map/reduce_scatter | solution.py:618
  3281.7 233.1 %all-reduce.58.cloned.1.call-done = (f32[1,3407872]{1,0:T(1,128)}, f32[32768]{0:T(1024)}) async-done(((f32[1,3407872]{1,0:T(1,128)}, f32[32768]{0:T(1024)}), (f32[1,3407872]{1,0:T(1,128)}, f32[32768]{0:T(1024)})) %all-reduce.58.cloned.1.call-update) | async-done | bytes 13762576 | tf_op jit(solution)/shard_map/psum | solution.py:630
  (3006 shorter events, 2757.3 us)
Async XLA Ops:
  8.0 3271.3 %reduce-scatter.5.cloned.1.call-start = ((), (), s32[]{:S(2)}) async-start(), calls=%async_computation.3 | async-start | bytes 4014080 | tf_op jit(solution)/shard_map/reduce_scatter | solution.py:618
  203.2 25.2 collective-permute-start
  205.1 23.2 collective-permute-start.1
  265.9 25.2 collective-permute-start
  267.8 23.2 collective-permute-start.1
  328.5 26.6 collective-permute-start
  330.4 24.6 collective-permute-start.1
  392.6 26.6 collective-permute-start
  394.5 24.7 collective-permute-start.1
  456.7 26.6 collective-permute-start
  458.6 24.7 collective-permute-start.1
  520.7 26.6 collective-permute-start
  522.7 24.7 collective-permute-start.1
  584.8 26.6 collective-permute-start
  586.7 24.7 collective-permute-start.1
  648.9 26.6 collective-permute-start
  650.8 24.7 collective-permute-start.1
  713.0 26.6 collective-permute-start
  714.9 24.7 collective-permute-start.1
  777.0 26.6 collective-permute-start
  779.0 24.7 collective-permute-start.1
  841.1 25.2 collective-permute-start
  843.0 23.2 collective-permute-start.1
  1018.0 53.2 %copy-start.43 = (s32[4]{0:T(128)S(1)}, s32[4]{0:T(128)}, u32[]{:S(2)}) copy-start(s32[4]{0:T(128)} %get-tuple-element.2876) | copy-start | bytes 52 | tf_op jit(solution)/shard_map/while
  1018.0 53.9 %copy-start.42 = (f32[4]{0:T(128)S(1)}, f32[4]{0:T(128)}, u32[]{:S(2)}) copy-start(f32[4]{0:T(128)} %copy-done.41) | copy-start | bytes 52 | tf_op jit(solution)/shard_map/while
  1051.5 41.3 %collective-permute-start.2 = (bf16[49,512]{1,0:T(8,128)(2,1)}, bf16[49,512]{1,0:T(8,128)(2,1)S(1)}, u32[]{:S(2)}, u32[]{:S(2)}) collective-permute-start(bf16[49,512]{1,0:T(8,128)(2,1)} %get-tuple-element.2615), channel_id=1, source_target_pairs={{8,0},{16,8},{24,16},{9,1},{17,9},{25,17},{10,2},{18,10},{26,18},{... | collective-permute-start | bytes 150536 | tf_op jit(solution)/shard_map/while/body/eval_jaxpr/ppermute | solution.py:34
  1053.6 39.2 %collective-permute-start.3 = (bf16[49,2048]{1,0:T(8,128)(2,1)}, bf16[49,2048]{1,0:T(8,128)(2,1)S(1)}, u32[]{:S(2)}, u32[]{:S(2)}) collective-permute-start(bf16[49,2048]{1,0:T(8,128)(2,1)} %get-tuple-element.2616), channel_id=1, source_target_pairs={{8,0},{16,8},{24,16},{9,1},{17,9},{25,17},{10,2},{18,10},{26,18},{... | collective-permute-start | bytes 602120 | tf_op jit(solution)/shard_map/while/body/eval_jaxpr/ppermute | solution.py:34
  1237.7 47.1 %copy-start.43 = (s32[4]{0:T(128)S(1)}, s32[4]{0:T(128)}, u32[]{:S(2)}) copy-start(s32[4]{0:T(128)} %get-tuple-element.2876) | copy-start | bytes 52 | tf_op jit(solution)/shard_map/while
  1237.7 47.8 %copy-start.42 = (f32[4]{0:T(128)S(1)}, f32[4]{0:T(128)}, u32[]{:S(2)}) copy-start(f32[4]{0:T(128)} %copy-done.41) | copy-start | bytes 52 | tf_op jit(solution)/shard_map/while
  1271.0 35.8 %collective-permute-start.2 = (bf16[49,512]{1,0:T(8,128)(2,1)}, bf16[49,512]{1,0:T(8,128)(2,1)S(1)}, u32[]{:S(2)}, u32[]{:S(2)}) collective-permute-start(bf16[49,512]{1,0:T(8,128)(2,1)} %get-tuple-element.2615), channel_id=1, source_target_pairs={{8,0},{16,8},{24,16},{9,1},{17,9},{25,17},{10,2},{18,10},{26,18},{... | collective-permute-start | bytes 150536 | tf_op jit(solution)/shard_map/while/body/eval_jaxpr/ppermute | solution.py:34
  1273.1 33.8 collective-permute-start.3
  1451.7 47.6 %copy-start.42 = (f32[4]{0:T(128)S(1)}, f32[4]{0:T(128)}, u32[]{:S(2)}) copy-start(f32[4]{0:T(128)} %copy-done.41) | copy-start | bytes 52 | tf_op jit(solution)/shard_map/while
  1485.2 35.4 %collective-permute-start.2 = (bf16[49,512]{1,0:T(8,128)(2,1)}, bf16[49,512]{1,0:T(8,128)(2,1)S(1)}, u32[]{:S(2)}, u32[]{:S(2)}) collective-permute-start(bf16[49,512]{1,0:T(8,128)(2,1)} %get-tuple-element.2615), channel_id=1, source_target_pairs={{8,0},{16,8},{24,16},{9,1},{17,9},{25,17},{10,2},{18,10},{26,18},{... | collective-permute-start | bytes 150536 | tf_op jit(solution)/shard_map/while/body/eval_jaxpr/ppermute | solution.py:34
  1487.3 33.3 collective-permute-start.3
  1665.5 47.6 %copy-start.42 = (f32[4]{0:T(128)S(1)}, f32[4]{0:T(128)}, u32[]{:S(2)}) copy-start(f32[4]{0:T(128)} %copy-done.41) | copy-start | bytes 52 | tf_op jit(solution)/shard_map/while
  1699.0 35.4 %collective-permute-start.2 = (bf16[49,512]{1,0:T(8,128)(2,1)}, bf16[49,512]{1,0:T(8,128)(2,1)S(1)}, u32[]{:S(2)}, u32[]{:S(2)}) collective-permute-start(bf16[49,512]{1,0:T(8,128)(2,1)} %get-tuple-element.2615), channel_id=1, source_target_pairs={{8,0},{16,8},{24,16},{9,1},{17,9},{25,17},{10,2},{18,10},{26,18},{... | collective-permute-start | bytes 150536 | tf_op jit(solution)/shard_map/while/body/eval_jaxpr/ppermute | solution.py:34
  1701.0 33.3 collective-permute-start.3
  1879.2 47.1 %copy-start.43 = (s32[4]{0:T(128)S(1)}, s32[4]{0:T(128)}, u32[]{:S(2)}) copy-start(s32[4]{0:T(128)} %get-tuple-element.2876) | copy-start | bytes 52 | tf_op jit(solution)/shard_map/while
  1879.2 47.8 %copy-start.42 = (f32[4]{0:T(128)S(1)}, f32[4]{0:T(128)}, u32[]{:S(2)}) copy-start(f32[4]{0:T(128)} %copy-done.41) | copy-start | bytes 52 | tf_op jit(solution)/shard_map/while
  1912.5 35.8 %collective-permute-start.2 = (bf16[49,512]{1,0:T(8,128)(2,1)}, bf16[49,512]{1,0:T(8,128)(2,1)S(1)}, u32[]{:S(2)}, u32[]{:S(2)}) collective-permute-start(bf16[49,512]{1,0:T(8,128)(2,1)} %get-tuple-element.2615), channel_id=1, source_target_pairs={{8,0},{16,8},{24,16},{9,1},{17,9},{25,17},{10,2},{18,10},{26,18},{... | collective-permute-start | bytes 150536 | tf_op jit(solution)/shard_map/while/body/eval_jaxpr/ppermute | solution.py:34
  1914.6 33.8 collective-permute-start.3
  2093.2 47.8 %copy-start.42 = (f32[4]{0:T(128)S(1)}, f32[4]{0:T(128)}, u32[]{:S(2)}) copy-start(f32[4]{0:T(128)} %copy-done.41) | copy-start | bytes 52 | tf_op jit(solution)/shard_map/while
  2126.7 35.6 %collective-permute-start.2 = (bf16[49,512]{1,0:T(8,128)(2,1)}, bf16[49,512]{1,0:T(8,128)(2,1)S(1)}, u32[]{:S(2)}, u32[]{:S(2)}) collective-permute-start(bf16[49,512]{1,0:T(8,128)(2,1)} %get-tuple-element.2615), channel_id=1, source_target_pairs={{8,0},{16,8},{24,16},{9,1},{17,9},{25,17},{10,2},{18,10},{26,18},{... | collective-permute-start | bytes 150536 | tf_op jit(solution)/shard_map/while/body/eval_jaxpr/ppermute | solution.py:34
  2128.8 33.6 collective-permute-start.3
  2307.2 47.8 %copy-start.42 = (f32[4]{0:T(128)S(1)}, f32[4]{0:T(128)}, u32[]{:S(2)}) copy-start(f32[4]{0:T(128)} %copy-done.41) | copy-start | bytes 52 | tf_op jit(solution)/shard_map/while
  2340.7 35.6 %collective-permute-start.2 = (bf16[49,512]{1,0:T(8,128)(2,1)}, bf16[49,512]{1,0:T(8,128)(2,1)S(1)}, u32[]{:S(2)}, u32[]{:S(2)}) collective-permute-start(bf16[49,512]{1,0:T(8,128)(2,1)} %get-tuple-element.2615), channel_id=1, source_target_pairs={{8,0},{16,8},{24,16},{9,1},{17,9},{25,17},{10,2},{18,10},{26,18},{... | collective-permute-start | bytes 150536 | tf_op jit(solution)/shard_map/while/body/eval_jaxpr/ppermute | solution.py:34
  2342.8 33.6 collective-permute-start.3
  2521.2 47.1 %copy-start.43 = (s32[4]{0:T(128)S(1)}, s32[4]{0:T(128)}, u32[]{:S(2)}) copy-start(s32[4]{0:T(128)} %get-tuple-element.2876) | copy-start | bytes 52 | tf_op jit(solution)/shard_map/while
  2521.2 47.8 %copy-start.42 = (f32[4]{0:T(128)S(1)}, f32[4]{0:T(128)}, u32[]{:S(2)}) copy-start(f32[4]{0:T(128)} %copy-done.41) | copy-start | bytes 52 | tf_op jit(solution)/shard_map/while
  2554.5 35.8 %collective-permute-start.2 = (bf16[49,512]{1,0:T(8,128)(2,1)}, bf16[49,512]{1,0:T(8,128)(2,1)S(1)}, u32[]{:S(2)}, u32[]{:S(2)}) collective-permute-start(bf16[49,512]{1,0:T(8,128)(2,1)} %get-tuple-element.2615), channel_id=1, source_target_pairs={{8,0},{16,8},{24,16},{9,1},{17,9},{25,17},{10,2},{18,10},{26,18},{... | collective-permute-start | bytes 150536 | tf_op jit(solution)/shard_map/while/body/eval_jaxpr/ppermute | solution.py:34
  2556.6 33.8 collective-permute-start.3
  2735.2 47.8 %copy-start.42 = (f32[4]{0:T(128)S(1)}, f32[4]{0:T(128)}, u32[]{:S(2)}) copy-start(f32[4]{0:T(128)} %copy-done.41) | copy-start | bytes 52 | tf_op jit(solution)/shard_map/while
  2768.7 35.6 %collective-permute-start.2 = (bf16[49,512]{1,0:T(8,128)(2,1)}, bf16[49,512]{1,0:T(8,128)(2,1)S(1)}, u32[]{:S(2)}, u32[]{:S(2)}) collective-permute-start(bf16[49,512]{1,0:T(8,128)(2,1)} %get-tuple-element.2615), channel_id=1, source_target_pairs={{8,0},{16,8},{24,16},{9,1},{17,9},{25,17},{10,2},{18,10},{26,18},{... | collective-permute-start | bytes 150536 | tf_op jit(solution)/shard_map/while/body/eval_jaxpr/ppermute | solution.py:34
  2770.8 33.6 collective-permute-start.3
  2949.2 47.1 %copy-start.43 = (s32[4]{0:T(128)S(1)}, s32[4]{0:T(128)}, u32[]{:S(2)}) copy-start(s32[4]{0:T(128)} %get-tuple-element.2876) | copy-start | bytes 52 | tf_op jit(solution)/shard_map/while
  2949.2 47.8 %copy-start.42 = (f32[4]{0:T(128)S(1)}, f32[4]{0:T(128)}, u32[]{:S(2)}) copy-start(f32[4]{0:T(128)} %copy-done.41) | copy-start | bytes 52 | tf_op jit(solution)/shard_map/while
  2982.7 35.4 %collective-permute-start.2 = (bf16[49,512]{1,0:T(8,128)(2,1)}, bf16[49,512]{1,0:T(8,128)(2,1)S(1)}, u32[]{:S(2)}, u32[]{:S(2)}) collective-permute-start(bf16[49,512]{1,0:T(8,128)(2,1)} %get-tuple-element.2615), channel_id=1, source_target_pairs={{8,0},{16,8},{24,16},{9,1},{17,9},{25,17},{10,2},{18,10},{26,18},{... | collective-permute-start | bytes 150536 | tf_op jit(solution)/shard_map/while/body/eval_jaxpr/ppermute | solution.py:34
  2984.8 33.3 collective-permute-start.3
  3162.9 47.3 %copy-start.43 = (s32[4]{0:T(128)S(1)}, s32[4]{0:T(128)}, u32[]{:S(2)}) copy-start(s32[4]{0:T(128)} %get-tuple-element.2876) | copy-start | bytes 52 | tf_op jit(solution)/shard_map/while
  3162.9 48.1 %copy-start.42 = (f32[4]{0:T(128)S(1)}, f32[4]{0:T(128)}, u32[]{:S(2)}) copy-start(f32[4]{0:T(128)} %copy-done.41) | copy-start | bytes 52 | tf_op jit(solution)/shard_map/while
  3196.2 35.8 %collective-permute-start.2 = (bf16[49,512]{1,0:T(8,128)(2,1)}, bf16[49,512]{1,0:T(8,128)(2,1)S(1)}, u32[]{:S(2)}, u32[]{:S(2)}) collective-permute-start(bf16[49,512]{1,0:T(8,128)(2,1)} %get-tuple-element.2615), channel_id=1, source_target_pairs={{8,0},{16,8},{24,16},{9,1},{17,9},{25,17},{10,2},{18,10},{26,18},{... | collective-permute-start | bytes 150536 | tf_op jit(solution)/shard_map/while/body/eval_jaxpr/ppermute | solution.py:34
  3198.3 33.8 collective-permute-start.3
  3234.2 280.5 %all-reduce.58.cloned.1.call-start = ((), (), s32[]{:S(2)}) async-start(), calls=%async_computation.4 | async-start | bytes 27525120 | tf_op jit(solution)/shard_map/psum | solution.py:630
  3236.7 280.3 %reduce-scatter.3.cloned.1.call-start = ((), (), s32[]{:S(2)}) async-start(), calls=%async_computation.2 | async-start | bytes 2007040 | tf_op jit(solution)/shard_map/reduce_scatter | solution.py:624
  (219 other events, 2708.6 us)
Sparse Core Ops, SparseCore 0:
  3234.4 44.8 reduce-scatter.4
  3282.8 31.1 reduce-scatter.2
Sparse Core Ops, SparseCore 1:
  3237.7 277.0 all-reduce.57
where the time goes:
time: 3590 us; the launch traced here: 3530 us
  local copies, waits for them, and re-layouts  1760 us (49%)
  other arithmetic  693 us (19%)
  waiting for transfers between devices  276 us (8%)
  matrix products  235 us (7%)
  loops' own time  202 us (6%)
  starting transfers between devices  198 us (6%)
  blocking collectives  154 us (4%)
    slice x66, local copies, waits for them, and re-layouts, weights_two(): flat_weights[split_at:split_at + 9 * C_MID * C_MID]  461 us
    psum x1, waiting for transfers between devices, on_device(): weight_sum, norm_sum = lax.psum((weight_acc, norm_grads), ('dp', 'rep'))  233 us
    slice x66, local copies, waits for them, and re-layouts, weights_two(): flat_weights[:split_at].reshape(C_OUT, C_MID)  204 us
    ppermute x44, starting transfers between devices, shifted(): lax.ppermute(value, axis, [(source, source + steps) for source in range(f...  198 us
    cond x484, local copies, waits for them, and re-layouts  187 us
    scatter-add x22, other arithmetic, add_weight(): acc.at[offset:offset + flat.shape[0]].add(jnp.where(valid, flat, 0.0))  171 us
    scatter x11, local copies, waits for them, and re-layouts, backward_tick(): stored.at[micro_idx].set(jnp.where(is_valid, fresh, stored[micro_idx]))  170 us
    unnamed x3, other arithmetic  145 us
  transfers between devices with their start and end apart: 47, of which 2 were waited for; matrix products, arithmetic and copies ran while one was open for 14% of the time, Pallas kernels for 0%

commit v1 on v0

--- a/solution.py
+++ b/solution.py
@@ -1,6 +1,8 @@
 import jax
 import jax.numpy as jnp
 from jax import lax
+from jax.experimental import pallas as pl
+from jax.experimental.pallas import tpu as pltpu
 from jax.sharding import PartitionSpec as P
 
 C_IN = 1024
@@ -633,7 +635,909 @@
     return (output_part, grad_images, weight_sum.reshape(1, P_SIZE), grad_gain, grad_bias)
 
 
+PP = PIX_OUT + 1
+RW = 8 * PP
+RV = 8 * PIX_OUT
+BLK = 512
+SUB = 65536
+F32 = jnp.float32
+BF16 = jnp.bfloat16
+MESH = pl.DeviceIdType.MESH
+
+C_H2, C_O1, C_H4, C_H5, C_Z6, C_D5, C_D4, C_DH = range(8, 16)
+C_SHARE, C_GI, C_GP = 16, 19, 22
+C_WIN, C_WPEER, C_WZ, C_WFWD = 25, 30, 35, 40
+C_PAR2, C_PAR3, C_DG2, C_DG3 = 45, 46, 47, 48
+N_SEM = 49
+PIECES = ((0, 512), (2048, 384), (3584, 384), (5120, 384), (6656, 512))
+
+
+def nn(a, b):
+    return jnp.dot(a, b, preferred_element_type=F32)
+
+
+def nt(a, b):
+    return lax.dot_general(a, b, (((1,), (1,)), ((), ())), preferred_element_type=F32)
+
+
+def tn(a, b):
+    return lax.dot_general(a, b, (((0,), (0,)), ((), ())), preferred_element_type=F32)
+
+
+def rows(start, size):
+    return pl.ds(pl.multiple_of(start, 16), size)
+
+
+def whole_kernel(
+    img, wts, gain, bias, meta, cot,
+    out, gi, dw, dgb,
+    imgb, raw, st, wh, wx, f0, f1, f2, f3, fs, pb, pt, u0, u1, u2, u3, sx, cotb,
+    h2, h4, h5, d5, d4, dh, r0, r1, ob, tx, rx, inv, par, parx, dg, dgx, sb, ls, ss, rs,
+):
+    p, d, r = lax.axis_index("pipe"), lax.axis_index("dp"), lax.axis_index("rep")
+    peer = (p, 1 - d, r)
+    z_pair = r + 1 - 2 * lax.rem(r, 2)
+    quarter = 2 * lax.rem(r, 2) + d
+
+    def remote(src, dst, send, recv, device):
+        return pltpu.make_async_remote_copy(
+            src_ref=src, dst_ref=dst, send_sem=ss.at[send], recv_sem=rs.at[recv],
+            device_id=device, device_id_type=MESH,
+        )
+
+    def sync(event, first, count):
+        part = pl.ds(first, count)
+        copy = remote(tx.at[part], rx.at[part], event, event, peer)
+        copy.start()
+        copy.wait()
+
+    def both(slot):
+        return tx[slot] + rx[slot]
+
+    def moments(slot_sum, slot_square, total, inv_slot):
+        center = both(slot_sum) * (1.0 / total)
+        scale = lax.rsqrt(both(slot_square) * (1.0 / total) - center * center + EPSILON)
+        inv[inv_slot] = scale
+        return center, scale
+
+    def silu(v):
+        return v * jax.nn.sigmoid(v)
+
+    def slope(v):
+        s = jax.nn.sigmoid(v)
+        return s * (1.0 + v * (1.0 - s))
+
+    def clear_pad(ref, first):
+        tile = ref[rows(first + RW - 16, 16), :].astype(F32)
+        keep = lax.broadcasted_iota(jnp.int32, tile.shape, 0) < 8
+        ref[rows(first + RW - 16, 16), :] = jnp.where(keep, tile, 0.0).astype(BF16)
+
+    def mask_of(column):
+        lane = lax.broadcasted_iota(jnp.int32, (8, BLK), 1).astype(F32)
+        return (lane < meta[:, column : column + 1]).astype(F32)
+
+    def five(body, init=0):
+        return lax.fori_loop(0, 5, lambda c, carry: body(pl.ds(c * 10, 10), c, carry), init)
+
+    def add_stats(carry, a, b):
+        return carry[0] + jnp.sum(a, axis=0), carry[1] + jnp.sum(b, axis=0)
+
+    zero_stats = (jnp.zeros((8, BLK), F32), jnp.zeros((8, BLK), F32))
+
+    def store_z(ref, first, z, slot_sum, slot_square):
+        z3 = z.reshape(PP, 8, BLK)
+        ref[pl.ds(first, PP)] = z3
+        tx[slot_sum] = jnp.sum(z3, axis=0)
+        tx[slot_square] = jnp.sum(z3 * z3, axis=0)
+
+    def raw_copy(slot, element):
+        return pltpu.make_async_copy(
+            wts.at[:, pl.ds(pl.multiple_of(element, SUB), SUB)], raw.at[slot], ls.at[2 + slot]
+        )
+
+    def load_weights(count, element_of, put):
+        raw_copy(0, element_of(0)).start()
+
+        def body(i, carry):
+            slot = lax.rem(i, 2)
+
+            @pl.when(i + 1 < count)
+            def _():
+                raw_copy(1 - slot, element_of(i + 1)).start()
+
+            raw_copy(slot, element_of(i)).wait()
+            st[0:512] = raw[slot].astype(F32).reshape(512, 128)
+            put(i)
+            return carry
+
+        lax.fori_loop(0, count, body, 0)
+
+    def put_narrow(ref, row_of):
+        def put(i):
+            for j in range(4):
+                ref[rows(row_of(i), 128), j * 128 : (j + 1) * 128] = st[
+                    pl.ds(j, 128, stride=4), :
+                ].astype(BF16)
+
+        return put
+
+    def put_wide(ref, base, block_rows):
+        def put(i):
+            for n in range(4):
+                for j in range(4):
+                    ref[rows(base + n * block_rows + i * 32, 32), j * 128 : (j + 1) * 128] = st[
+                        pl.ds(4 * n + j, 32, stride=16), :
+                    ].astype(BF16)
+
+        return put
+
+    def img_copy(q, slot):
+        return pltpu.make_async_copy(img.at[pl.ds(q * 28, 28)], imgb.at[slot], ls.at[slot])
+
+    def over_images(body, init):
+        img_copy(0, 0).start()
+
+        def step(q, carry):
+            slot = lax.rem(q, 2)
+
+            @pl.when(q + 1 < 7)
+            def _():
+                img_copy(q + 1, 1 - slot).start()
+
+            img_copy(q, slot).wait()
+            return body(q, slot, carry)
+
+        return lax.fori_loop(0, 7, step, init)
+
+    def dw_copy(slot, chunk):
+        return pltpu.make_async_copy(
+            sb.at[slot], dw.at[pl.ds(pl.multiple_of(chunk * 2048, 2048), 2048)], ls.at[4 + slot]
+        )
+
+    def emit(turn, chunk):
+        slot = lax.rem(turn, 2)
+
+        @pl.when(turn >= 2)
+        def _():
+            dw_copy(slot, chunk).wait()
+
+        sb[slot] = st[...].astype(BF16)
+        dw_copy(slot, chunk).start()
+
+    def stage_narrow(block):
+        for j in range(4):
+            st[pl.ds(j, 512, stride=4), :] = block[:, j * 128 : (j + 1) * 128]
+
+    def stage_wide(n, block):
+        for j in range(4):
+            st[pl.ds(4 * n + j, 128, stride=16), :] = block[:, j * 128 : (j + 1) * 128]
+
+    def emit_wide(turn, chunk, left, left_rows, left_cols, right):
+        for n in range(4):
+            stage_wide(n, tn(left[left_rows, left_cols], right[n * RW : (n + 1) * RW, :]))
+        emit(turn, chunk)
+
+    def emit_zeros(turn, first):
+        st[...] = jnp.zeros_like(st)
+
+        def body(i, carry):
+            emit(turn + i, first + i)
+            return carry
+
+        lax.fori_loop(0, 13 - first, body, 0)
+        dw_copy(0, 0).wait()
+        dw_copy(1, 0).wait()
+
+    barrier = pltpu.get_barrier_semaphore()
+    for device in (peer, (p, d, z_pair)) + tuple((lax.rem(p + k, 4), d, r) for k in (1, 2, 3)):
+        pl.semaphore_signal(barrier, inc=1, device_id=device, device_id_type=MESH)
+
+    block_two = p >= 2
+    set_col = jnp.where(block_two, meta[:, 3:4], meta[:, 2:3])
+    for k in range(NSETS):
+        hot = (set_col == float(k)).astype(F32)
+        for n in range(8):
+            g = hot * gain[k : k + 1, n * BLK : (n + 1) * BLK]
+            b = hot * bias[k : k + 1, n * BLK : (n + 1) * BLK]
+            if k == 0:
+                par[n] = g
+                par[8 + n] = b
+            else:
+                par[n] += g
+                par[8 + n] += b
+    dg[...] = jnp.zeros_like(dg)
+    pl.semaphore_wait(barrier, 5)
+
+    total_in, total_out = 2.0 * PIX_IN, 2.0 * PIX_OUT
+
+    def build_patches(base):
+        def body(tap, carry):
+            row, col = base(tap)
+            window = pb[pl.ds(row, 7), pl.ds(col, 7)].reshape(RV, BLK)
+            pt[tap, 0:RV, :] = window.astype(BF16)
+            return carry
+
+        lax.fori_loop(0, 9, body, 0)
+
+    def clear_patch_pad():
+        def body(tap, carry):
+            pt[tap, RW - 16 : RW, :] = jnp.zeros((16, BLK), BF16)
+            return carry
+
+        lax.fori_loop(0, 9, body, 0)
+
+    def strided_base(tap):
+        di, dj = tap // 3, lax.rem(tap, 3)
+        return lax.rem(di, 2) * 8 + di // 2, lax.rem(dj, 2) * 8 + dj // 2
+
+    def plain_base(tap):
+        return tap // 3, lax.rem(tap, 3)
+
+    def conv(ref, first, target):
+        target[...] = jnp.zeros_like(target)
+
+        def body(tap, carry):
+            z = nn(pt[tap], ref[rows(first + tap * BLK, BLK), :])
+            target[...] += z.reshape(PP, 8, BLK)
+            return carry
+
+        lax.fori_loop(0, 9, body, 0)
+
+    def conv_back(dz, ref, first, base):
+        pb[...] = jnp.zeros_like(pb)
+
+        def body(tap, carry):
+            row, col = base(tap)
+            part = nt(dz[0:RV, :], ref[rows(first + tap * BLK, BLK), :])
+            pb[pl.ds(row, 7), pl.ds(col, 7)] += part.reshape(7, 7, 8, BLK)
+            return carry
+
+        lax.fori_loop(0, 9, body, 0)
+
+    def stats_of_map(ref, slot_sum, slot_square):
+        def body(c, _, carry):
+            z = ref[c]
+            return add_stats(carry, z, z * z)
+
+        tx[slot_sum], tx[slot_square] = five(body, zero_stats)
+
+    def act_to(ref, target, center, scale, g, b, mask):
+        def body(c, i, carry):
+            zhat = (ref[c] - center) * scale
+            ref[c] = zhat
+            h = silu(zhat * g + b) * mask
+            target[rows(i * 80, 80), :] = h.reshape(80, BLK).astype(BF16)
+            return carry
+
+        five(body)
+        clear_pad(target, 0)
+
+    def upstream(target, grad, zhat_ref, g, b, mask, slot_sum, slot_gain):
+        def body(c, i, carry):
+            zhat = zhat_ref[c]
+            du = grad[rows(i * 80, 80), :].astype(F32).reshape(10, 8, BLK) * mask * slope(zhat * g + b)
+            target[c] = du
+            return add_stats(carry, du, du * zhat)
+
+        tx[slot_sum], tx[slot_gain] = five(body, zero_stats)
+
+    def norm_back(target, first, du_ref, du_first, zhat_ref, zhat_first, gscale, mean_du, mean_dg):
+        def body(c, i, carry):
+            du = du_ref[pl.ds(du_first + i * 10, 10)]
+            zhat = zhat_ref[pl.ds(zhat_first + i * 10, 10)]
+            dz = gscale * (du - mean_du - zhat * mean_dg)
+            target[rows(first + i * 80, 80), :] = dz.reshape(80, BLK).astype(BF16)
+            return carry
+
+        five(body)
+        clear_pad(target, first)
+
+    @pl.when(p == 0)
+    def _():
+        mask = mask_of(0)
+        load_weights(8, lambda i: i * SUB, put_narrow(wh, lambda i: i * 128))
+
+        def first_conv(q, slot, carry):
+            rows_q = imgb[slot].astype(F32).reshape(224, 1024).astype(BF16)
+            wx[rows(q * 224, 224), :] = rows_q[:, 0:512]
+            wx[rows(1568 + q * 224, 224), :] = rows_q[:, 512:1024]
+            z = nn(rows_q, wh[0:1024, :]).reshape(28, 8, BLK)
+            f0[pl.ds(q * 28, 28)] = z
+            return add_stats(carry, z, z * z)
+
+        tx[0], tx[1] = over_images(first_conv, zero_stats)
+        exchange = remote(tx.at[pl.ds(0, 2)], rx.at[pl.ds(0, 2)], 0, 0, peer)
+        exchange.start()
+        pb[...] = jnp.zeros_like(pb)
+        clear_patch_pad()
+        load_weights(36, lambda i: (8 + i) * SUB, put_narrow(wh, lambda i: 1024 + i * 128))
+        exchange.wait()
+
+        center, scale = moments(0, 1, total_in, 0)
+        g1, b1, g2, b2 = par[0], par[8], par[1], par[9]
+
+        def hidden(i, carry):
+            zhat = (f0[pl.ds(i * 14, 14)] - center) * scale
+            f0[pl.ds(i * 14, 14)] = zhat
+            h = (silu(zhat * g1 + b1) * mask).astype(BF16).astype(F32).reshape(7, 2, 8, BLK)
+            u = i + 1
+            row = lax.rem(u, 2) * 8 + u // 2
+            pb[row, 8:15] = h[:, 0]
+            pb[row, 1:8] = h[:, 1]
+            return carry
+
+        lax.fori_loop(0, 14, hidden, 0)
+        build_patches(strided_base)
+        conv(wh, 1024, fs.at[0])
+        stats_of_map(fs.at[0], 2, 3)
+        sync(1, 2, 2)
+        center, scale = moments(2, 3, total_out, 1)
+        act_to(fs.at[0], h2, center, scale, g2, b2, mask)
+        send = remote(h2, h2, C_H2, C_H2, (1, d, r))
+        send.start()
+        send.wait_send()
+
+        remote(dh, dh, C_DH, C_DH, (0, d, r)).wait_recv()
+        upstream(fs.at[1], dh, fs.at[0], g2, b2, mask, 4, 5)
+        sync(2, 4, 2)
+        s_du, s_dg = both(4), both(5)
+        dg[1], dg[9] = s_dg, s_du
+        norm_back(d5, 0, fs.at[1], 0, fs.at[0], 0, g2 * inv[1], s_du * (1.0 / total_out), s_dg * (1.0 / total_out))
+        conv_back(d5, wh, 1024, strided_base)
+
+        def slopes(i, carry):
+            u = i + 1
+            row = lax.rem(u, 2) * 8 + u // 2
+            grad = jnp.stack([pb[row, 8:15], pb[row, 1:8]], axis=1).reshape(14, 8, BLK)
+            zhat = f0[pl.ds(i * 14, 14)]
+            du = grad * mask * slope(zhat * g1 + b1)
+            f1[pl.ds(i * 14, 14)] = du
+            return add_stats(carry, du, du * zhat)
+
+        tx[6], tx[7] = lax.fori_loop(0, 14, slopes, zero_stats)
+        sync(3, 6, 2)
+        s_du, s_dg = both(6), both(7)
+        dg[0], dg[8] = s_dg, s_du
+        gscale, m_du, m_dg = g1 * inv[0], s_du * (1.0 / total_in), s_dg * (1.0 / total_in)
+
+        def first_back(q, carry):
+            part = pl.ds(q * 28, 28)
+            dz = gscale * (f1[part] - m_du - f0[part] * m_dg)
+            u1[rows(q * 224, 224), :] = dz.reshape(224, BLK).astype(BF16)
+            return carry
+
+        lax.fori_loop(0, 7, first_back, 0)
+
+        def share(target, column, k):
+            def body(q, carry):
+                g = nt(u1[rows(q * 224, 224), :], wh[k * 256 : (k + 1) * 256, :])
+                target[rows(q * 224, 224), column : column + 256] = g.astype(BF16)
+                return carry
+
+            lax.fori_loop(0, 7, body, 0)
+
+        sends = []
+        for k, (target, column) in enumerate(((u0, 0), (u0, 256), (u2, 0)), 1):
+            share(target, column, k)
+            send = remote(target.at[0:1568, column : column + 256], r0, C_GI + k - 1, C_GI, (k, d, r))
+            send.start()
+            sends.append(send)
+        share(r0, 0, 0)
+
+        def second_weights(tap, carry):
+            stage_narrow(tn(pt[tap], d5[...]))
+            emit(tap, tap + 2)
+            return carry
+
+        lax.fori_loop(0, 9, second_weights, 0)
+
+        def first_weights(k, carry):
+            stage_narrow(tn(wx[rows(k * 1568, 1568), :], u1[0:1568, :]))
+            emit(9 + k, k)
+            return carry
+
+        lax.fori_loop(0, 2, first_weights, 0)
+        emit_zeros(11, 11)
+        for send in sends:
+            send.wait_send()
+
+    @pl.when(p == 1)
+    def _():
+        mask = mask_of(1)
+        gate_col = meta[:, 4:5]
+        cot_copy = pltpu.make_async_copy(cot, cotb.at[0:PIX_OUT], ls.at[6])
+        cot_copy.start()
+        cotb[PIX_OUT] = jnp.zeros((8, C_OUT), BF16)
+        clear_patch_pad()
+        load_weights(32, lambda i: (16 + i) * SUB, put_wide(wh, 2048, 1024))
+
+        def shorten(a, slot, carry):
+            v = imgb[slot, 0:14].astype(F32).reshape(7, 2, 8, 1024)[:, 0]
+            f0[pl.ds(a * 7, 7)] = v[:, :, 0:512]
+            f0[pl.ds(PP + a * 7, 7)] = v[:, :, 512:1024]
+            return carry
+
+        over_images(shorten, 0)
+        f0[PIX_OUT] = jnp.zeros((8, BLK), F32)
+        f0[PP + PIX_OUT] = jnp.zeros((8, BLK), F32)
+        sx[...] = f0[0 : 2 * PP].reshape(2 * RW, BLK).astype(BF16)
+
+        def shortcut(n, carry):
+            z = nn(sx[0:RW, :], wh[rows(2048 + n * 1024, 512), :]) + nn(
+                sx[RW : 2 * RW, :], wh[rows(2560 + n * 1024, 512), :]
+            )
+            store_z(f1, n * PP, z, 8 + n, 12 + n)
+            return carry
+
+        lax.fori_loop(0, 4, shortcut, 0)
+        load_weights(16, lambda i: i * SUB, put_wide(wh, 0, 512))
+
+        sends = []
+
+        def piece(i, q):
+            first, size = PIECES[i]
+            return wx.at[rows(first + q * size, size)]
+
+        other_z = 2 * (1 - lax.rem(r, 2))
+
+        def pass_own(i):
+            mine = piece(i, quarter)
+            remote(mine, mine, C_WIN + i, C_WIN + i, (1, d, r)).wait_recv()
+            for base, device in ((C_WPEER, peer), (C_WZ, (p, d, z_pair))):
+                copy = remote(mine, mine, base + i, base + i, device)
+                copy.start()
+                sends.append(copy)
+
+        def pass_on(i):
+            theirs = piece(i, other_z + d)
+            remote(theirs, theirs, C_WZ + i, C_WZ + i, peer).wait_recv()
+            copy = remote(theirs, theirs, C_WFWD + i, C_WFWD + i, peer)
+            copy.start()
+            sends.append(copy)
+
+        def have(i):
+            a = piece(i, 2 * lax.rem(r, 2) + 1 - d)
+            b = piece(i, other_z + 1 - d)
+            remote(a, a, C_WPEER + i, C_WPEER + i, peer).wait_recv()
+            remote(b, b, C_WFWD + i, C_WFWD + i, peer).wait_recv()
+
+        pass_own(0)
+        remote(h2, h2, C_H2, C_H2, (1, d, r)).wait_recv()
+
+        def third_conv(n, carry):
+            store_z(f0, n * PP, nn(h2[...], wh[rows(n * 512, 512), :]), n, 4 + n)
+            return carry
+
+        lax.fori_loop(0, 4, third_conv, 0)
+        sync(0, 0, 16)
+
+        def join(n, carry):
+            c3, s3 = moments(n, 4 + n, total_out, 2 + n)
+            cp, sp = moments(8 + n, 12 + n, total_out, 6 + n)
+            g3, gp, b = par[n], par[4 + n], par[8 + n] + par[12 + n]
+
+            def body(_, i, carry):
+                part = pl.ds(n * PP + i * 10, 10)
+                a = (f0[part] - c3) * s3
+                b_ = (f1[part] - cp) * sp
+                f0[part] = a
+                f1[part] = b_
+                o = silu(a * g3 + b_ * gp + b)
+                u0[rows(n * RW + i * 80, 80), :] = o.reshape(80, BLK).astype(BF16)
+                return carry
+
+            five(body)
+            clear_pad(u0, n * RW)
+            return carry
+
+        lax.fori_loop(0, 4, join, 0)
+        copy = remote(u0, u0, C_O1, C_O1, (2, d, r))
+        copy.start()
+        sends.append(copy)
+        pass_on(0)
+        have(0)
+
+        zhat4, zhat5 = fs.at[0], fs.at[1]
+        z = nn(u0[0:RW, :], wx[0:512, :])
+        for n in range(1, 4):
+            z += nn(u0[n * RW : (n + 1) * RW, :], wx[n * 512 : (n + 1) * 512, :])
+        store_z(zhat4, 0, z, 16, 17)
+        sync(1, 16, 2)
+        remote(parx.at[0:4], parx.at[0:4], C_PAR2, C_PAR2, (1, d, r)).wait_recv()
+        center, scale = moments(16, 17, total_out, 10)
+        g4, g5, b4, b5 = parx[0], parx[1], parx[2], parx[3]
+        pb[...] = jnp.zeros_like(pb)
+
+        def hidden(a, carry):
+            part = pl.ds(a * 7, 7)
+            zhat = (zhat4[part] - center) * scale
+            zhat4[part] = zhat
+            h = silu(zhat * g4 + b4) * mask
+            pb[a + 1, 1:8] = h.astype(BF16).astype(F32)
+            return carry
+
+        lax.fori_loop(0, 7, hidden, 0)
+        h4[0:RV, :] = pb[1:8, 1:8].reshape(RV, BLK).astype(BF16)
+        copy = remote(h4, h4, C_H4, C_H4, (2, d, r))
+        copy.start()
+        sends.append(copy)
+        build_patches(plain_base)
+        pass_own(1)
+        pass_own(2)
+        pass_on(1)
+        pass_own(3)
+        pass_on(2)
+        pass_on(3)
+        pass_own(4)
+        for i in (1, 2, 3):
+            have(i)
+        conv(wx, 2048, zhat5)
+        stats_of_map(zhat5, 18, 19)
+        sync(2, 18, 2)
+        center, scale = moments(18, 19, total_out, 11)
+        act_to(zhat5, h5, center, scale, g5, b5, mask)
+        copy = remote(h5, h5, C_H5, C_H5, (3, d, r))
+        copy.start()
+        sends.append(copy)
+        pass_on(4)
+        have(4)
+
+        def sixth_conv(n, carry):
+            store_z(f2, n * PP, nn(h5[...], wx[rows(6656 + n * 512, 512), :]), 20 + n, 24 + n)
+            return carry
+
+        lax.fori_loop(0, 4, sixth_conv, 0)
+        sync(3, 20, 8)
+        remote(parx.at[4:12], parx.at[4:12], C_PAR3, C_PAR3, (1, d, r)).wait_recv()
+        cot_copy.wait()
+
+        def finish(n, carry):
+            center, scale = moments(20 + n, 24 + n, total_out, 12 + n)
+            g6, b6 = parx[4 + n], parx[8 + n]
+            gate_v = jnp.broadcast_to(gate_col, (8, BLK))
+
+            def body(c, i, carry):
+                part = pl.ds(n * PP + i * 10, 10)
+                part_rows = rows(n * RW + i * 80, 80)
+                zhat = (f2[part] - center) * scale
+                f2[part] = zhat
+                o = u0[part_rows, :].astype(F32).reshape(10, 8, BLK)
+                q = o + zhat * g6 + b6
+                s = jax.nn.sigmoid(q)
+                merged = gate_v * (q * s) + (1.0 - gate_v) * o
+                u3[part_rows, :] = merged.reshape(80, BLK).astype(BF16)
+                ct = cotb[c, :, pl.ds(pl.multiple_of(n * BLK, BLK), BLK)].astype(F32)
+                dq = ct * gate_v * (s * (1.0 + q * (1.0 - s)))
+                f3[part] = dq
+                dres = dq + (1.0 - gate_v) * ct
+                u2[part_rows, :] = dres.reshape(80, BLK).astype(BF16)
+                return add_stats(carry, dq, dq * zhat)
+
+            tx[28 + n], tx[32 + n] = five(body, zero_stats)
+            return carry
+
+        lax.fori_loop(0, 4, finish, 0)
+        out_sends = []
+        for slot, k in enumerate((0, 2, 3)):
+            copy = remote(u3.at[k * RW : (k + 1) * RW], ob, C_SHARE + slot, C_SHARE, (k, d, r))
+            copy.start()
+            out_sends.append(copy)
+        ob[...] = u3[RW : 2 * RW, :]
+
+        sync(4, 28, 8)
+
+        def sixth_back(n, carry):
+            s_du, s_dg = both(28 + n), both(32 + n)
+            dgx[4 + n] = s_dg
+            dgx[8 + n] = s_du
+            norm_back(u1, n * RW, f3, n * PP, f2, n * PP, parx[4 + n] * inv[12 + n], s_du * (1.0 / total_out), s_dg * (1.0 / total_out))
+            return carry
+
+        lax.fori_loop(0, 4, sixth_back, 0)
+        z6_send = remote(u1, u1, C_Z6, C_Z6, (3, d, r))
+        z6_send.start()
+        grad = nt(u1[0:RW, :], wx[6656:7168, :])
+        for n in range(1, 4):
+            grad += nt(u1[n * RW : (n + 1) * RW, :], wx[6656 + n * 512 : 7168 + n * 512, :])
+        dh[...] = grad.astype(BF16)
+
+        upstream(f2, dh, zhat5, g5, b5, mask, 36, 37)
+        sync(5, 36, 2)
+        s_du, s_dg = both(36), both(37)
+        dgx[1] = s_dg
+        dgx[3] = s_du
+        norm_back(d5, 0, f2, 0, zhat5, 0, g5 * inv[11], s_du * (1.0 / total_out), s_dg * (1.0 / total_out))
+        copy = remote(d5, d5, C_D5, C_D5, (2, d, r))
+        copy.start()
+        sends.append(copy)
+        conv_back(d5, wx, 2048, plain_base)
+
+        def fourth_slopes(a, carry):
+            part = pl.ds(a * 7, 7)
+            zhat = zhat4[part]
+            du = pb[a + 1, 1:8] * mask * slope(zhat * g4 + b4)
+            f2[part] = du
+            return add_stats(carry, du, du * zhat)
+
+        tx[38], tx[39] = lax.fori_loop(0, 7, fourth_slopes, zero_stats)
+        sync(6, 38, 2)
+        s_du, s_dg = both(38), both(39)
+        dgx[0] = s_dg
+        dgx[2] = s_du
+        norm_back(d4, 0, f2, 0, zhat4, 0, g4 * inv[10], s_du * (1.0 / total_out), s_dg * (1.0 / total_out))
+        copy = remote(d4, d4, C_D4, C_D4, (2, d, r))
+        copy.start()
+        sends.append(copy)
+        for first, last, sem, chip in ((0, 4, C_DG2, 2), (4, 12, C_DG3, 3)):
+            copy = remote(dgx.at[first:last], dgx.at[first:last], sem, sem, (chip, d, r))
+            copy.start()
+            sends.append(copy)
+
+        def first_block_slopes(n, carry):
+            f3[pl.ds(n * PP, PP)] = nt(d4[...], wx[rows(n * 512, 512), :]).reshape(PP, 8, BLK)
+            g3, gp, b = par[n], par[4 + n], par[8 + n] + par[12 + n]
+
+            def body(_, i, carry):
+                part = pl.ds(n * PP + i * 10, 10)
+                do = u2[rows(n * RW + i * 80, 80), :].astype(F32).reshape(10, 8, BLK) + f3[part]
+                a, b_ = f0[part], f1[part]
+                dp = do.astype(BF16).astype(F32) * slope(a * g3 + b_ * gp + b)
+                f3[part] = dp
+                s0, s1, s2 = carry
+                return s0 + jnp.sum(dp, axis=0), s1 + jnp.sum(dp * a, axis=0), s2 + jnp.sum(dp * b_, axis=0)
+
+            tx[40 + n], tx[44 + n], tx[48 + n] = five(body, zero_stats + zero_stats[:1])
+            return carry
+
+        lax.fori_loop(0, 4, first_block_slopes, 0)
+        z6_send.wait_send()
+        for copy in out_sends:
+            copy.wait_send()
+        sync(7, 40, 12)
+
+        def third_back(n, carry):
+            s_du, s_d3, s_dp = both(40 + n), both(44 + n), both(48 + n)
+            dg[n] = s_d3
+            dg[4 + n] = s_dp
+            dg[8 + n] = s_du
+            dg[12 + n] = s_du
+            m_du = s_du * (1.0 / total_out)
+            norm_back(u1, n * RW, f3, n * PP, f0, n * PP, par[n] * inv[2 + n], m_du, s_d3 * (1.0 / total_out))
+            norm_back(u3, n * RW, f3, n * PP, f1, n * PP, par[4 + n] * inv[6 + n], m_du, s_dp * (1.0 / total_out))
+            return carry
+
+        lax.fori_loop(0, 4, third_back, 0)
+        grad = nt(u1[0:RW, :], wh[0:512, :])
+        for n in range(1, 4):
+            grad += nt(u1[n * RW : (n + 1) * RW, :], wh[n * 512 : (n + 1) * 512, :])
+        dh[...] = grad.astype(BF16)
+        copy = remote(dh, dh, C_DH, C_DH, (0, d, r))
+        copy.start()
+        sends.append(copy)
+
+        def shortcut_share(k):
+            g = nt(u3[0:RW, :], wh[2048 + k * 256 : 2304 + k * 256, :])
+            for n in range(1, 4):
+                g += nt(u3[n * RW : (n + 1) * RW, :], wh[2048 + n * 1024 + k * 256 : 2304 + n * 1024 + k * 256, :])
+            return g.astype(BF16)
+
+        for slot, k in enumerate((0, 2, 3)):
+            u2[slot * RW : (slot + 1) * RW, 0:256] = shortcut_share(k)
+            copy = remote(u2.at[slot * RW : (slot + 1) * RW, 0:256], r1, C_GP + slot, C_GP, (k, d, r))
+            copy.start()
+            sends.append(copy)
+        r1[...] = shortcut_share(1)
+
+        def third_weights(m, carry):
+            emit_wide(m, m, h2, slice(None), pl.ds(pl.multiple_of(m * 128, 128), 128), u1)
+            return carry
+
+        lax.fori_loop(0, 4, third_weights, 0)
+
+        def shortcut_weights(m, carry):
+            emit_wide(4 + m, 4 + m, sx, rows((m // 4) * RW, RW), pl.ds(pl.multiple_of(lax.rem(m, 4) * 128, 128), 128), u3)
+            return carry
+
+        lax.fori_loop(0, 8, shortcut_weights, 0)
+        emit_zeros(12, 12)
+        for copy in sends:
+            copy.wait_send()
+
+    @pl.when(p == 2)
+    def _():
+        for k, slot in ((0, 0), (1, 1), (2, 8), (3, 9)):
+            parx[k] = par[slot]
+        sends = [remote(parx.at[0:4], parx.at[0:4], C_PAR2, C_PAR2, (1, d, r))]
+        sends[0].start()
+        load_weights(4, lambda i: (quarter * 4 + i) * SUB, put_narrow(wx, lambda i: quarter * 512 + i * 128))
+        for i in range(4):
+            first, size = PIECES[i]
+            if i > 0:
+                load_weights(
+                    3,
+                    lambda k, i=i: (16 + (i - 1) * 12 + quarter * 3 + k) * SUB,
+                    put_narrow(wx, lambda k, first=first: first + quarter * 384 + k * 128),
+                )
+            part = wx.at[rows(first + quarter * size, size)]
+            copy = remote(part, part, C_WIN + i, C_WIN + i, (1, d, r))
+            copy.start()
+            sends.append(copy)
+        pb[...] = jnp.zeros_like(pb)
+        clear_patch_pad()
+        remote(h4, h4, C_H4, C_H4, (2, d, r)).wait_recv()
+        pb[1:8, 1:8] = h4[0:RV, :].astype(F32).reshape(7, 7, 8, BLK)
+        build_patches(plain_base)
+        remote(d5, d5, C_D5, C_D5, (2, d, r)).wait_recv()
+
+        def fifth_weights(tap, carry):
+            stage_narrow(tn(pt[tap], d5[...]))
+            emit(tap, tap + 4)
+            return carry
+
+        lax.fori_loop(0, 9, fifth_weights, 0)
+        remote(u0, u0, C_O1, C_O1, (2, d, r)).wait_recv()
+        remote(d4, d4, C_D4, C_D4, (2, d, r)).wait_recv()
+
+        def fourth_weights(n, carry):
+            stage_narrow(tn(u0[rows(n * RW, RW), :], d4[...]))
+            emit(9 + n, n)
+            return carry
+
+        lax.fori_loop(0, 4, fourth_weights, 0)
+        dw_copy(0, 0).wait()
+        dw_copy(1, 0).wait()
+        remote(dgx.at[0:4], dgx.at[0:4], C_DG2, C_DG2, (2, d, r)).wait_recv()
+        dg[0], dg[1], dg[8], dg[9] = dgx[0], dgx[1], dgx[2], dgx[3]
+        for copy in sends:
+            copy.wait_send()
+
+    @pl.when(p == 3)
+    def _():
+        for k in range(4):
+            parx[4 + k] = par[k]
+            parx[8 + k] = par[8 + k]
+        sends = [remote(parx.at[4:12], parx.at[4:12], C_PAR3, C_PAR3, (1, d, r))]
+        sends[0].start()
+
+        def put(i):
+            for j in range(4):
+                wx[rows(6656 + quarter * 512 + i * 32, 32), j * 128 : (j + 1) * 128] = st[
+                    pl.ds(4 * quarter + j, 32, stride=16), :
+                ].astype(BF16)
+
+        load_weights(16, lambda i: i * SUB, put)
+        part = wx.at[rows(6656 + quarter * 512, 512)]
+        copy = remote(part, part, C_WIN + 4, C_WIN + 4, (1, d, r))
+        copy.start()
+        sends.append(copy)
+        remote(h5, h5, C_H5, C_H5, (3, d, r)).wait_recv()
+        remote(u1, u1, C_Z6, C_Z6, (3, d, r)).wait_recv()
+
+        def sixth_weights(m, carry):
+            emit_wide(m, m, h5, slice(None), pl.ds(pl.multiple_of(m * 128, 128), 128), u1)
+            return carry
+
+        lax.fori_loop(0, 4, sixth_weights, 0)
+        emit_zeros(4, 4)
+        remote(dgx.at[4:12], dgx.at[4:12], C_DG3, C_DG3, (3, d, r)).wait_recv()
+        for k in range(4):
+            dg[k] = dgx[4 + k]
+            dg[8 + k] = dgx[8 + k]
+        for copy in sends:
+            copy.wait_send()
+
+    @pl.when(p != 1)
+    def _():
+        remote(ob, ob, C_SHARE, C_SHARE, (p, d, r)).wait_recv()
+        remote(r1, r1, C_GP, C_GP, (p, d, r)).wait_recv()
+
+    @pl.when(p != 0)
+    def _():
+        remote(r0, r0, C_GI, C_GI, (p, d, r)).wait_recv()
+
+    out[...] = ob[0:RV, :].astype(F32).reshape(PIX_OUT, 8, BLK).astype(BF16)
+    f0[0:PP, :, 0:256] = r1[...].astype(F32).reshape(PP, 8, 256)
+
+    def place(a, carry):
+        m = r0[rows(a * 224, 224), :].astype(F32).reshape(28, 8, 256)
+        first = m[0:14].reshape(7, 2, 8, 256)
+        even = first[:, 0] + f0[pl.ds(a * 7, 7), :, 0:256]
+        f3[pl.ds(a * 28, 14), :, 0:256] = jnp.stack([even, first[:, 1]], axis=1).reshape(14, 8, 256)
+        f3[pl.ds(a * 28 + 14, 14), :, 0:256] = m[14:28]
+        return carry
+
+    lax.fori_loop(0, 7, place, 0)
+    gi_copy = pltpu.make_async_copy(f3.at[0:PIX_IN, :, 0:256], gi, ls.at[7])
+    gi_copy.start()
+    for k in range(NSETS):
+        hot = (set_col == float(k)).astype(F32)
+        for n in range(8):
+            dgb[k : k + 1, n * BLK : (n + 1) * BLK] = jnp.sum(dg[n] * hot, axis=0, keepdims=True)
+            dgb[4 + k : 5 + k, n * BLK : (n + 1) * BLK] = jnp.sum(dg[8 + n] * hot, axis=0, keepdims=True)
+    gi_copy.wait()
+
+
+def one_kernel(images, section_weights, bn_gain, bn_bias, width, bn_set, gate, cotangent):
+    meta = jnp.concatenate(
+        [width.astype(F32), bn_set.astype(F32), gate.astype(F32)[:, None], jnp.zeros((MB, 123), F32)], axis=1
+    )
+    any_space = pl.BlockSpec(memory_space=pl.ANY)
+    vmem = pl.BlockSpec(memory_space=pltpu.VMEM)
+    out, gi, dw, dgb = pl.pallas_call(
+        whole_kernel,
+        out_shape=(
+            jax.ShapeDtypeStruct((PIX_OUT, 8, BLK), BF16),
+            jax.ShapeDtypeStruct((PIX_IN, 8, 256), F32),
+            jax.ShapeDtypeStruct((P_SIZE // 128, 128), BF16),
+            jax.ShapeDtypeStruct((8, 4096), F32),
+        ),
+        in_specs=[any_space, any_space, vmem, vmem, vmem, any_space],
+        out_specs=(vmem, any_space, any_space, vmem),
+        scratch_shapes=[
+            pltpu.VMEM((2, 28, 8, 1024), BF16),
+            pltpu.VMEM((2, 1, SUB), BF16),
+            pltpu.VMEM((2048, 128), F32),
+            pltpu.VMEM((6144, BLK), BF16),
+            pltpu.VMEM((8704, BLK), BF16),
+            pltpu.VMEM((4 * PP, 8, BLK), F32),
+            pltpu.VMEM((4 * PP, 8, BLK), F32),
+            pltpu.VMEM((4 * PP, 8, BLK), F32),
+            pltpu.VMEM((4 * PP, 8, BLK), F32),
+            pltpu.VMEM((2, PP, 8, BLK), F32),
+            pltpu.VMEM((16, 16, 8, BLK), F32),
+            pltpu.VMEM((9, RW, BLK), BF16),
+            pltpu.VMEM((4 * RW, BLK), BF16),
+            pltpu.VMEM((4 * RW, BLK), BF16),
+            pltpu.VMEM((4 * RW, BLK), BF16),
+            pltpu.VMEM((4 * RW, BLK), BF16),
+            pltpu.VMEM((2 * RW, BLK), BF16),
+            pltpu.VMEM((PP, 8, C_OUT), BF16),
+            pltpu.VMEM((RW, BLK), BF16),
+            pltpu.VMEM((RW, BLK), BF16),
+            pltpu.VMEM((RW, BLK), BF16),
+            pltpu.VMEM((RW, BLK), BF16),
+            pltpu.VMEM((RW, BLK), BF16),
+            pltpu.VMEM((RW, BLK), BF16),
+            pltpu.VMEM((8 * PIX_IN, 256), BF16),
+            pltpu.VMEM((RW, 256), BF16),
+            pltpu.VMEM((RW, BLK), BF16),
+            pltpu.VMEM((52, 8, BLK), F32),
+            pltpu.VMEM((52, 8, BLK), F32),
+            pltpu.VMEM((16, 8, BLK), F32),
+            pltpu.VMEM((16, 8, BLK), F32),
+            pltpu.VMEM((12, 8, BLK), F32),
+            pltpu.VMEM((16, 8, BLK), F32),
+            pltpu.VMEM((12, 8, BLK), F32),
+            pltpu.VMEM((2, 2048, 128), BF16),
+            pltpu.SemaphoreType.DMA((8,)),
+            pltpu.SemaphoreType.DMA((N_SEM,)),
+            pltpu.SemaphoreType.DMA((N_SEM,)),
+        ],
+        compiler_params=pltpu.CompilerParams(
+            collective_id=0, has_side_effects=True, vmem_limit_bytes=64 * 1024 * 1024
+        ),
+    )(
+        jnp.transpose(images, (1, 0, 2)),
+        section_weights,
+        bn_gain[0],
+        bn_bias[0],
+        meta,
+        jnp.transpose(cotangent, (1, 0, 2)),
+    )
+    dw = lax.psum(dw, ("dp", "rep")).astype(F32).reshape(1, P_SIZE)
+    dgb = lax.psum(dgb, "rep")
+    return (
+        jnp.transpose(out, (1, 0, 2)),
+        jnp.transpose(gi, (1, 0, 2)),
+        dw,
+        dgb[None, :4],
+        dgb[None, 4:],
+    )
+
+
 def solution(mesh):
+    sizes = dict(mesh.shape)
+    fits = sizes["pipe"] == 4 and sizes["dp"] == 2 and sizes["rep"] % 2 == 0
     placed = (
         P(("dp", "rep"), None, None),
         P("pipe", None),
@@ -645,7 +1549,7 @@
         P(("dp", "rep"), None, None),
     )
     return jax.shard_map(
-        on_device,
+        one_kernel if fits else on_device,
         mesh=mesh,
         in_specs=placed,
         out_specs=(

time: 3590 us -> 567 us (0.16); the launches traced: 3530 us -> 564 us
  local copies, waits for them, and re-layouts: 1760 us -> 18.1 us
  other arithmetic: 693 us -> 17.8 us
  matrix products: 235 us -> 0 us
  loops' own time: 202 us -> 0 us
  Pallas kernels: 0 us -> 201 us
  starting transfers between devices: 198 us -> 0.08 us
  blocking collectives: 154 us -> 0 us
  waiting for transfers between devices: 276 us -> 314 us
    slice x410 -> x0, local copies, waits for them, and re-layouts: 714 us -> none  [the longest x66 461 us: weights_two(): flat_weights[split_at:split_at + 9 * C_MID * C_MID]]
    scatter x55 -> x0, local copies, waits for them, and re-layouts: 300 us -> none  [the longest x11 170 us: backward_tick(): stored.at[micro_idx].set(jnp.where(is_valid, fresh, stored[micro_idx]))]
    dot_general x88 -> x0, matrix products: 235 us -> none  [the longest x44 90 us: matmul(): return jnp.dot(left_op, right_op, preferred_element_type=jnp.float32)]
    another operation x68 -> x0, loops' own time: 202 us -> none  [the longest x11 94.8 us: backward_tick(): lax.switch(section_idx, bwd_second, (ops, first_buf, second_buf, third_bu...]
    pallas_call x0 -> x1, Pallas kernels: none -> 201 us  [one_kernel(): pl.pallas_call(whole_kernel, out_shape=(jax.ShapeDtypeStruct((PIX_OUT, 8,...]
    ppermute x44 -> x0, starting transfers between devices: 198 us -> none  [shifted(): lax.ppermute(value, axis, [(source, source + steps) for source in range(f...]
    cond x484 -> x0, local copies, waits for them, and re-layouts: 187 us -> none
    scatter-add x22 -> x0, other arithmetic: 171 us -> none  [add_weight(): acc.at[offset:offset + flat.shape[0]].add(jnp.where(valid, flat, 0.0))]
  transfers between devices with their start and end apart: 47 -> 2, of which waited for: 2 -> 2; matrix products, arithmetic and copies ran while one was open for 14% -> 3% of each run, Pallas kernels for 0% -> 0%
where the time goes in v1:
time: 567 us; the launch traced here: 564 us
  waiting for transfers between devices  314 us (55%)
  Pallas kernels  201 us (35%)
  local copies, waits for them, and re-layouts  18.1 us (3%)
  other arithmetic  17.8 us (3%)
  between operations  14.1 us (2%)
    psum x1, waiting for transfers between devices, one_kernel(): dw = lax.psum(dw, ('dp', 'rep')).astype(F32).reshape(1, P_SIZE)  277 us
    pallas_call x1, Pallas kernels, one_kernel(): pl.pallas_call(whole_kernel, out_shape=(jax.ShapeDtypeStruct((PIX_OUT, 8,...  201 us
    psum x1, waiting for transfers between devices, one_kernel(): dgb = lax.psum(dgb, 'rep')  36.3 us
    reshape x1, other arithmetic, one_kernel(): dw = lax.psum(dw, ('dp', 'rep')).astype(F32).reshape(1, P_SIZE)  16.4 us
    unnamed x9, local copies, waits for them, and re-layouts  16.3 us
  transfers between devices with their start and end apart: 2, of which 2 were waited for; matrix products, arithmetic and copies ran while one was open for 3% of the time, Pallas kernels for 0%

profile of v1, /device:TPU:5, one launch (start us, length us, event | category | flops | bytes accessed | tf_op | source)
XLA Modules:
  0.0 564.2 jit_solution(9811591997322673983)
XLA Ops:
  7.2 0.0 all-reduce.5.cloned.1.call-start
  7.2 0.7 convert_bitcast_fusion
  7.9 0.1 copy.15
  8.0 0.8 copy.13
  8.7 0.8 copy.14
  9.5 0.1 pad.3.clone
  9.6 0.7 maximum_maximum_fusion.meta
  10.2 200.5 %shard_map.119 = (bf16[49,8,512]{2,1,0:T(8,128)(2,1)}, f32[196,8,256]{2,1,0:T(8,128)}, bf16[26624,128]{1,0:T(8,128)(2,1)}, f32[8,4096]{1,0:T(8,128)}) custom-call(bf16[196,8,1024]{2,1,0:T(8,128)(2,1)} %bitcast.19, bf16[1,3407872]{1,0:T(2,128)(2,1)} %wts.1, f32[4,4096]{1,0:T(4,128)} %bitcast.23, f32[4,4096]{1,0:T(4,128)} %bitcast.24, ...), custom_call_target="tpu_custom_call" | custom-call | tf_op jit(solution)/shard_map/pallas_call | solution.py:1466
  210.7 0.0 all-reduce.5.cloned.1.call-update
  210.8 0.0 all-reduce.3.cloned.1.call-start
  210.8 12.9 %copy.18 = bf16[1,1,26624,128]{3,1,2,0:T(2,128)(2,1)} copy(bf16[1,1,26624,128]{3,2,1,0:T(8,128)(2,1)} %bitcast.18) | data formatting | bytes 13631488
  223.7 0.0 all-reduce.3.cloned.1.call-update
  223.7 36.3 %all-reduce.5.cloned.1.call-done = f32[8,4096]{1,0:T(8,128)} async-done(((f32[8,4096]{1,0:T(8,128)}), f32[8,4096]{1,0:T(8,128)}) %all-reduce.5.cloned.1.call-update) | async-done | bytes 131088 | tf_op jit(solution)/shard_map/psum | solution.py:1528
  260.1 1.7 slice_bitcast_fusion
  261.7 0.0 copy-start.1
  261.7 0.0 copy-start
  261.7 277.3 %all-reduce.3.cloned.1.call-done = bf16[1,3407872]{1,0:T(2,128)(2,1)} async-done(((bf16[1,3407872]{1,0:T(2,128)(2,1)}), bf16[1,3407872]{1,0:T(2,128)(2,1)}) %all-reduce.3.cloned.1.call-update) | async-done | bytes 6815760 | tf_op jit(solution)/shard_map/psum | solution.py:1527
  539.0 16.4 %reshape.17 = f32[1,3407872]{1,0:T(1,128)} convert(bf16[1,3407872]{1,0:T(2,128)(2,1)} %all-reduce.3.cloned.1.call-done) | non-fusion elementwise | flops 3407872 | bytes 20447232 | tf_op jit(solution)/shard_map/reshape | solution.py:1527
  555.4 0.0 copy-done.1
  555.4 0.8 copy.23
  556.2 0.0 copy-done
  556.2 1.2 copy.24
  (3 shorter events, 0.0 us)
Async XLA Ops:
  7.2 252.9 %all-reduce.5.cloned.1.call-start = ((), (), s32[]{:S(2)}) async-start(), calls=%async_computation.1 | async-start | bytes 262144 | tf_op jit(solution)/shard_map/psum | solution.py:1528
  210.8 328.2 %all-reduce.3.cloned.1.call-start = ((), (), s32[]{:S(2)}) async-start(), calls=%async_computation | async-start | bytes 27262976 | tf_op jit(solution)/shard_map/psum | solution.py:1527
  261.7 293.7 %copy-start.1 = (bf16[49,8,512]{2,1,0:T(8,128)(2,1)S(1)}, bf16[49,8,512]{2,1,0:T(8,128)(2,1)}, u32[]{:S(2)}) copy-start(bf16[49,8,512]{2,1,0:T(8,128)(2,1)} %get-tuple-element.9) | copy-start | bytes 1204228
  261.7 294.5 %copy-start = (f32[196,8,256]{2,1,0:T(8,128)S(1)}, f32[196,8,256]{2,1,0:T(8,128)}, u32[]{:S(2)}) copy-start(f32[196,8,256]{2,1,0:T(8,128)} %get-tuple-element.10) | copy-start | bytes 4816900
Sparse Core Ops, SparseCore 0:
  210.9 49.1 all-reduce.4
  263.1 275.7 all-reduce.2

commit v2 on v1

--- a/solution.py
+++ b/solution.py
@@ -644,12 +644,14 @@
 BF16 = jnp.bfloat16
 MESH = pl.DeviceIdType.MESH
 
-C_H2, C_O1, C_H4, C_H5, C_Z6, C_D5, C_D4, C_DH = range(8, 16)
-C_SHARE, C_GI, C_GP = 16, 19, 22
-C_WIN, C_WPEER, C_WZ, C_WFWD = 25, 30, 35, 40
-C_PAR2, C_PAR3, C_DG2, C_DG3 = 45, 46, 47, 48
-N_SEM = 49
-PIECES = ((0, 512), (2048, 384), (3584, 384), (5120, 384), (6656, 512))
+C_H2, C_H4, C_H5, C_Z6, C_D5, C_D4, C_DH = range(8, 15)
+C_O1, C_SHARE, C_GI, C_GP = 15, 19, 22, 25
+C_PAR2, C_PAR3, C_DG2, C_DG3, C_BN1, C_BN2, C_BN3 = range(28, 35)
+N_SEM = 35
+N_PIECE = 17
+W_OWN, W_PEER, W_Z, W_ON = range(4)
+G_CORE, G_IN, G_ACROSS, G_OUT, G_DONE = range(5)
+RING = 8
 
 
 def nn(a, b):
@@ -671,8 +673,9 @@
 def whole_kernel(
     img, wts, gain, bias, meta, cot,
     out, gi, dw, dgb,
-    imgb, raw, st, wh, wx, f0, f1, f2, f3, fs, pb, pt, u0, u1, u2, u3, sx, cotb,
-    h2, h4, h5, d5, d4, dh, r0, r1, ob, tx, rx, inv, par, parx, dg, dgx, sb, ls, ss, rs,
+    imgb, raw, st, wh, wx, f0, f1, f2, f3, fs, pb, pt, u0, u1, u2, sx, cotb,
+    h2, h4, h5, d5, d4, dh, r0, r1, ob, tx, rx, inv, par, parx, dg, dgx, sb, rd, bz, dgs,
+    ls, ss, rs, wss, wrs, ass, ars, ready, go,
 ):
     p, d, r = lax.axis_index("pipe"), lax.axis_index("dp"), lax.axis_index("rep")
     peer = (p, 1 - d, r)
@@ -730,24 +733,27 @@
         tx[slot_sum] = jnp.sum(z3, axis=0)
         tx[slot_square] = jnp.sum(z3 * z3, axis=0)
 
-    def raw_copy(slot, element):
+    def raw_copy(turn, element_of):
+        slot = lax.rem(turn, RING)
         return pltpu.make_async_copy(
-            wts.at[:, pl.ds(pl.multiple_of(element, SUB), SUB)], raw.at[slot], ls.at[2 + slot]
-        )
-
-    def load_weights(count, element_of, put):
-        raw_copy(0, element_of(0)).start()
-
-        def body(i, carry):
-            slot = lax.rem(i, 2)
-
-            @pl.when(i + 1 < count)
-            def _():
-                raw_copy(1 - slot, element_of(i + 1)).start()
-
-            raw_copy(slot, element_of(i)).wait()
-            st[0:512] = raw[slot].astype(F32).reshape(512, 128)
-            put(i)
+            wts.at[:, pl.ds(pl.multiple_of(element_of(turn) * SUB, SUB), SUB)], raw.at[slot], ls.at[8 + slot]
+        )
+
+    def open_weights(element_of, total):
+        for turn in range(min(RING - 1, total)):
+            raw_copy(turn, element_of).start()
+
+    def load_weights(element_of, total, first, count, put):
+        def body(k, carry):
+            turn = first + k
+
+            @pl.when(turn + RING - 1 < total)
+            def _():
+                raw_copy(turn + RING - 1, element_of).start()
+
+            raw_copy(turn, element_of).wait()
+            st[0:512] = raw[lax.rem(turn, RING)].astype(F32).reshape(512, 128)
+            put(turn)
             return carry
 
         lax.fori_loop(0, count, body, 0)
@@ -761,75 +767,284 @@
 
         return put
 
-    def put_wide(ref, base, block_rows):
+    def put_wide(ref, base, block_rows, first):
         def put(i):
             for n in range(4):
                 for j in range(4):
-                    ref[rows(base + n * block_rows + i * 32, 32), j * 128 : (j + 1) * 128] = st[
+                    ref[rows(base + n * block_rows + (i - first) * 32, 32), j * 128 : (j + 1) * 128] = st[
                         pl.ds(4 * n + j, 32, stride=16), :
                     ].astype(BF16)
 
         return put
 
+    def put_chunk(t, n, block):
+        wh[rows(t * 512 + n * 64, 64), :] = block[0:64].astype(BF16)
+        wh[rows(t * 512 + 256 + n * 64, 64), :] = block[64:128].astype(BF16)
+
+    def plain(turn):
+        return turn
+
+    def every_fourth(turn):
+        return 4 * turn + quarter
+
+    def four_rows(turn):
+        return 4 * quarter + turn
+
     def img_copy(q, slot):
         return pltpu.make_async_copy(img.at[pl.ds(q * 28, 28)], imgb.at[slot], ls.at[slot])
 
+    def open_images():
+        for q in range(3):
+            img_copy(q, q).start()
+
     def over_images(body, init):
-        img_copy(0, 0).start()
-
         def step(q, carry):
-            slot = lax.rem(q, 2)
-
-            @pl.when(q + 1 < 7)
-            def _():
-                img_copy(q + 1, 1 - slot).start()
+            slot = lax.rem(q, 4)
+
+            @pl.when(q + 3 < 7)
+            def _():
+                img_copy(q + 3, lax.rem(q + 3, 4)).start()
 
             img_copy(q, slot).wait()
             return body(q, slot, carry)
 
         return lax.fori_loop(0, 7, step, init)
 
-    def dw_copy(slot, chunk):
-        return pltpu.make_async_copy(
-            sb.at[slot], dw.at[pl.ds(pl.multiple_of(chunk * 2048, 2048), 2048)], ls.at[4 + slot]
-        )
-
-    def emit(turn, chunk):
-        slot = lax.rem(turn, 2)
-
-        @pl.when(turn >= 2)
+    outer = (r == 0) | (r == 3)
+    inner = jnp.logical_not(outer)
+    z_dev, across = (p, d, z_pair), (p, d, 3 - r)
+
+    def grad_copy(kind, t, src, dst, device):
+        return pltpu.make_async_remote_copy(
+            src_ref=src, dst_ref=dst, send_sem=ass.at[kind, t], recv_sem=ars.at[kind, t],
+            device_id=device, device_id_type=MESH,
+        )
+
+    def chunk_rows(chunk, half):
+        return dw.at[pl.ds(pl.multiple_of(chunk * 2048 + half * 1024, 1024), 1024)]
+
+    def zero_rest(first):
+        sb[0] = jnp.zeros((1024, 128), BF16)
+
+        def body(i, carry):
+            for half in range(2):
+                copy = pltpu.make_async_copy(sb.at[0], chunk_rows(first + i, half), ls.at[4])
+                copy.start()
+                copy.wait()
+            return carry
+
+        lax.fori_loop(0, 13 - first, body, 0)
+
+    def bn_sums():
+        for k in range(NSETS):
+            hot = (set_col == float(k)).astype(F32)
+            for n in range(8):
+                cols = slice(n * BLK, (n + 1) * BLK)
+                dgs[k : k + 1, cols] = jnp.sum(dg[n] * hot, axis=0, keepdims=True)
+                dgs[4 + k : 5 + k, cols] = jnp.sum(dg[8 + n] * hot, axis=0, keepdims=True)
+
+    def bn_in():
+        return remote(dgs, bz.at[0], C_BN1, C_BN1, z_dev)
+
+    def bn_across():
+        return remote(dgs, bz.at[1], C_BN2, C_BN2, across)
+
+    def bn_out():
+        return remote(dgb, bz.at[0], C_BN3, C_BN3, z_dev)
+
+    def say_ready():
+        pl.semaphore_signal(ready.at[0], inc=1, device_id=z_dev, device_id_type=MESH)
+
+        @pl.when(inner)
         def _():
-            dw_copy(slot, chunk).wait()
-
-        sb[slot] = st[...].astype(BF16)
-        dw_copy(slot, chunk).start()
-
-    def stage_narrow(block):
-        for j in range(4):
-            st[pl.ds(j, 512, stride=4), :] = block[:, j * 128 : (j + 1) * 128]
-
-    def stage_wide(n, block):
-        for j in range(4):
-            st[pl.ds(4 * n + j, 128, stride=16), :] = block[:, j * 128 : (j + 1) * 128]
-
-    def emit_wide(turn, chunk, left, left_rows, left_cols, right):
-        for n in range(4):
-            stage_wide(n, tn(left[left_rows, left_cols], right[n * RW : (n + 1) * RW, :]))
-        emit(turn, chunk)
-
-    def emit_zeros(turn, first):
-        st[...] = jnp.zeros_like(st)
-
-        def body(i, carry):
-            emit(turn + i, first + i)
-            return carry
-
-        lax.fori_loop(0, 13 - first, body, 0)
-        dw_copy(0, 0).wait()
-        dw_copy(1, 0).wait()
+            pl.semaphore_signal(ready.at[1], inc=1, device_id=across, device_id_type=MESH)
+
+    def sum_gradients(count, compute, at_row, chunk_of, wide, z1, extra):
+        z2 = z1 + count * 256
+
+        def half(t, which):
+            return wh.at[rows(at_row(t) + which * 256, 256)]
+
+        def from_z(t):
+            return wx.at[rows(z1 + t * 256, 256)]
+
+        def from_across(t):
+            return wx.at[rows(z2 + t * 256, 256)]
+
+        def to_core(t):
+            return grad_copy(G_CORE, t, half(t, 1 - d), rd.at[rows(t * 256, 256)], peer)
+
+        def inwards(t):
+            return grad_copy(G_IN, t, half(t, d), from_z(t), z_dev)
+
+        def exchange(t):
+            return grad_copy(G_ACROSS, t, half(t, d), from_across(t), across)
+
+        def outwards(t):
+            return grad_copy(G_OUT, t, half(t, d), from_z(t), z_dev)
+
+        def done_core(t):
+            part = chunk_rows(chunk_of(t), d)
+            return grad_copy(G_DONE, t, sb.at[lax.rem(t, 4)], part, peer)
+
+        def done_here(t):
+            return pltpu.make_async_copy(sb.at[lax.rem(t, 4)], chunk_rows(chunk_of(t), d), ls.at[4 + lax.rem(t, 4)])
+
+        def add(t, other):
+            total = half(t, d)[...].astype(F32) + other[...].astype(F32)
+            half(t, d)[...] = total.astype(BF16)
+
+        def finish(t, ref):
+            @pl.when(t >= 4)
+            def _():
+                done_here(t - 4).wait()
+                done_core(t - 4).wait_send()
+
+            value = ref[...].astype(F32)
+            for j in range(4):
+                cols = slice(j * 128, (j + 1) * 128)
+                if wide:
+                    for n in range(4):
+                        st[pl.ds(4 * n + j, 64, stride=16), :] = value[n * 64 : (n + 1) * 64, cols]
+                else:
+                    st[pl.ds(j, 256, stride=4), :] = value[:, cols]
+            sb[lax.rem(t, 4)] = st[...].astype(BF16)
+            done_here(t).start()
+            done_core(t).start()
+
+        def step(it, carry):
+            for when, work in extra.items():
+                pl.when(it == when)(work)
+
+            @pl.when(it < count)
+            def _():
+                compute(it)
+                to_core(it).start()
+
+            t1 = it - 1
+
+            @pl.when((t1 >= 0) & (t1 < count))
+            def _():
+                to_core(t1).wait_recv()
+                add(t1, rd.at[rows(t1 * 256, 256)])
+
+                @pl.when(outer & (t1 == 0))
+                def _():
+                    pl.semaphore_wait(ready.at[0], 1)
+
+                @pl.when(outer)
+                def _():
+                    inwards(t1).start()
+
+            t2 = it - 2
+
+            @pl.when(inner & (t2 >= 0) & (t2 < count))
+            def _():
+                @pl.when(t2 == 0)
+                def _():
+                    pl.semaphore_wait(ready.at[1], 1)
+
+                inwards(t2).wait_recv()
+                add(t2, from_z(t2))
+                exchange(t2).start()
+
+            t3 = it - 3
+
+            @pl.when(inner & (t3 >= 0) & (t3 < count))
+            def _():
+                @pl.when(t3 == 0)
+                def _():
+                    pl.semaphore_wait(ready.at[0], 1)
+
+                exchange(t3).wait()
+                add(t3, from_across(t3))
+                outwards(t3).start()
+                finish(t3, half(t3, d))
+
+            t5 = it - 5
+
+            @pl.when(outer & (t5 >= 0) & (t5 < count))
+            def _():
+                outwards(t5).wait_recv()
+                finish(t5, from_z(t5))
+
+            @pl.when(it == count - 3)
+            def _():
+                bn_sums()
+
+                @pl.when(outer)
+                def _():
+                    bn_in().start()
+
+            @pl.when(inner & (it == count))
+            def _():
+                bn_in().wait_recv()
+                dgs[...] += bz[0]
+                bn_across().start()
+
+            @pl.when(inner & (it == count + 3))
+            def _():
+                bn_across().wait()
+                dgb[...] = dgs[...] + bz[1]
+                bn_out().start()
+
+            return carry
+
+        lax.fori_loop(0, count + 5, step, 0)
+
+        @pl.when(outer)
+        def _():
+            bn_in().wait_send()
+            bn_out().wait_recv()
+            dgb[...] = bz[0]
+
+        @pl.when(inner)
+        def _():
+            bn_out().wait_send()
+
+        def drain(t, carry):
+            to_core(t).wait_send()
+
+            @pl.when(outer)
+            def _():
+                inwards(t).wait_send()
+
+            @pl.when(inner)
+            def _():
+                outwards(t).wait_send()
+
+            @pl.when(t >= count - 4)
+            def _():
+                done_here(t).wait()
+                done_core(t).wait_send()
+
+            theirs = chunk_rows(chunk_of(t), 1 - d)
+            grad_copy(G_DONE, t, sb.at[0], theirs, peer).wait_recv()
+            return carry
+
+        lax.fori_loop(0, count, drain, 0)
+
+    @pl.when(p == 0)
+    def _():
+        open_weights(plain, 44)
+        open_images()
+
+    @pl.when(p == 1)
+    def _():
+        open_weights(plain, 48)
+        open_images()
+        pltpu.make_async_copy(cot, cotb.at[0:PIX_OUT], ls.at[16]).start()
+
+    @pl.when(p == 2)
+    def _():
+        open_weights(every_fourth, 13)
+
+    @pl.when(p == 3)
+    def _():
+        open_weights(four_rows, 4)
 
     barrier = pltpu.get_barrier_semaphore()
-    for device in (peer, (p, d, z_pair)) + tuple((lax.rem(p + k, 4), d, r) for k in (1, 2, 3)):
+    for device in (peer, (p, d, z_pair), (p, d, 3 - r)) + tuple((lax.rem(p + k, 4), d, r) for k in (1, 2, 3)):
         pl.semaphore_signal(barrier, inc=1, device_id=device, device_id_type=MESH)
 
     block_two = p >= 2
@@ -846,7 +1061,7 @@
                 par[n] += g
                 par[8 + n] += b
     dg[...] = jnp.zeros_like(dg)
-    pl.semaphore_wait(barrier, 5)
+    pl.semaphore_wait(barrier, 6)
 
     total_in, total_out = 2.0 * PIX_IN, 2.0 * PIX_OUT
 
@@ -935,7 +1150,9 @@
     @pl.when(p == 0)
     def _():
         mask = mask_of(0)
-        load_weights(8, lambda i: i * SUB, put_narrow(wh, lambda i: i * 128))
+        say_ready()
+        put_w = put_narrow(wh, lambda i: i * 128)
+        load_weights(plain, 44, 0, 8, put_w)
 
         def first_conv(q, slot, carry):
             rows_q = imgb[slot].astype(F32).reshape(224, 1024).astype(BF16)
@@ -943,6 +1160,7 @@
             wx[rows(1568 + q * 224, 224), :] = rows_q[:, 512:1024]
             z = nn(rows_q, wh[0:1024, :]).reshape(28, 8, BLK)
             f0[pl.ds(q * 28, 28)] = z
+            load_weights(plain, 44, 8 + 5 * q, 5, put_w)
             return add_stats(carry, z, z * z)
 
         tx[0], tx[1] = over_images(first_conv, zero_stats)
@@ -950,7 +1168,7 @@
         exchange.start()
         pb[...] = jnp.zeros_like(pb)
         clear_patch_pad()
-        load_weights(36, lambda i: (8 + i) * SUB, put_narrow(wh, lambda i: 1024 + i * 128))
+        load_weights(plain, 44, 43, 1, put_w)
         exchange.wait()
 
         center, scale = moments(0, 1, total_in, 0)
@@ -975,6 +1193,7 @@
         act_to(fs.at[0], h2, center, scale, g2, b2, mask)
         send = remote(h2, h2, C_H2, C_H2, (1, d, r))
         send.start()
+        zero_rest(11)
         send.wait_send()
 
         remote(dh, dh, C_DH, C_DH, (0, d, r)).wait_recv()
@@ -983,7 +1202,8 @@
         s_du, s_dg = both(4), both(5)
         dg[1], dg[9] = s_dg, s_du
         norm_back(d5, 0, fs.at[1], 0, fs.at[0], 0, g2 * inv[1], s_du * (1.0 / total_out), s_dg * (1.0 / total_out))
-        conv_back(d5, wh, 1024, strided_base)
+        def back_conv():
+            conv_back(d5, wh, 1024, strided_base)
 
         def slopes(i, carry):
             u = i + 1
@@ -994,19 +1214,22 @@
             f1[pl.ds(i * 14, 14)] = du
             return add_stats(carry, du, du * zhat)
 
-        tx[6], tx[7] = lax.fori_loop(0, 14, slopes, zero_stats)
-        sync(3, 6, 2)
-        s_du, s_dg = both(6), both(7)
-        dg[0], dg[8] = s_dg, s_du
-        gscale, m_du, m_dg = g1 * inv[0], s_du * (1.0 / total_in), s_dg * (1.0 / total_in)
-
-        def first_back(q, carry):
-            part = pl.ds(q * 28, 28)
-            dz = gscale * (f1[part] - m_du - f0[part] * m_dg)
-            u1[rows(q * 224, 224), :] = dz.reshape(224, BLK).astype(BF16)
-            return carry
-
-        lax.fori_loop(0, 7, first_back, 0)
+        def first_slopes():
+            tx[6], tx[7] = lax.fori_loop(0, 14, slopes, zero_stats)
+            sync(3, 6, 2)
+            dg[0], dg[8] = both(7), both(6)
+
+        def first_back():
+            s_du, s_dg = both(6), both(7)
+            gscale, m_du, m_dg = g1 * inv[0], s_du * (1.0 / total_in), s_dg * (1.0 / total_in)
+
+            def body(q, carry):
+                part = pl.ds(q * 28, 28)
+                dz = gscale * (f1[part] - m_du - f0[part] * m_dg)
+                u1[rows(q * 224, 224), :] = dz.reshape(224, BLK).astype(BF16)
+                return carry
+
+            lax.fori_loop(0, 7, body, 0)
 
         def share(target, column, k):
             def body(q, carry):
@@ -1016,40 +1239,55 @@
 
             lax.fori_loop(0, 7, body, 0)
 
-        sends = []
-        for k, (target, column) in enumerate(((u0, 0), (u0, 256), (u2, 0)), 1):
-            share(target, column, k)
-            send = remote(target.at[0:1568, column : column + 256], r0, C_GI + k - 1, C_GI, (k, d, r))
-            send.start()
-            sends.append(send)
-        share(r0, 0, 0)
-
-        def second_weights(tap, carry):
-            stage_narrow(tn(pt[tap], d5[...]))
-            emit(tap, tap + 2)
-            return carry
-
-        lax.fori_loop(0, 9, second_weights, 0)
-
-        def first_weights(k, carry):
-            stage_narrow(tn(wx[rows(k * 1568, 1568), :], u1[0:1568, :]))
-            emit(9 + k, k)
-            return carry
-
-        lax.fori_loop(0, 2, first_weights, 0)
-        emit_zeros(11, 11)
-        for send in sends:
-            send.wait_send()
+        places = {1: (u0, 0), 2: (u0, 256), 3: (u2, 0)}
+
+        def share_copy(k):
+            target, column = places[k]
+            return remote(target.at[0:1568, column : column + 256], r0, C_GI + k - 1, C_GI, (k, d, r))
+
+        def share_out(k):
+            share(*places[k], k)
+            share_copy(k).start()
+
+        def back_and_share():
+            first_back()
+            share_out(3)
+
+        def compute(t):
+            @pl.when(t < 9)
+            def _():
+                wh[rows(at_row(t), 512), :] = tn(pt[t], d5[...]).astype(BF16)
+
+            @pl.when(t >= 9)
+            def _():
+                block = tn(wx[rows((t - 9) * 1568, 1568), :], u1[0:1568, :])
+                wh[rows(at_row(t), 512), :] = block.astype(BF16)
+
+        def at_row(t):
+            return jnp.where(t < 2, 5632 + t * 512, t * 512)
+
+        sum_gradients(
+            11, compute, at_row, lambda t: lax.rem(t + 2, 11), False, 3136,
+            {
+                2: back_conv,
+                3: first_slopes,
+                4: back_and_share,
+                5: lambda: share_out(1),
+                6: lambda: share_out(2),
+                7: lambda: share(r0, 0, 0),
+            },
+        )
+        for k in (1, 2, 3):
+            share_copy(k).wait_send()
 
     @pl.when(p == 1)
     def _():
         mask = mask_of(1)
         gate_col = meta[:, 4:5]
-        cot_copy = pltpu.make_async_copy(cot, cotb.at[0:PIX_OUT], ls.at[6])
-        cot_copy.start()
         cotb[PIX_OUT] = jnp.zeros((8, C_OUT), BF16)
         clear_patch_pad()
-        load_weights(32, lambda i: (16 + i) * SUB, put_wide(wh, 2048, 1024))
+        load_weights(plain, 48, 0, 16, put_wide(wh, 0, 512, 0))
+        load_weights(plain, 48, 16, 32, put_wide(wh, 2048, 1024, 16))
 
         def shorten(a, slot, carry):
             v = imgb[slot, 0:14].astype(F32).reshape(7, 2, 8, 1024)[:, 0]
@@ -1070,38 +1308,43 @@
             return carry
 
         lax.fori_loop(0, 4, shortcut, 0)
-        load_weights(16, lambda i: i * SUB, put_wide(wh, 0, 512))
-
-        sends = []
+
+        other_z = 2 * (1 - lax.rem(r, 2))
+        this_z = 2 * lax.rem(r, 2)
 
         def piece(i, q):
-            first, size = PIECES[i]
-            return wx.at[rows(first + q * size, size)]
-
-        other_z = 2 * (1 - lax.rem(r, 2))
+            return wx.at[rows(i * 512 + q * 128, 128)]
+
+        def piece_copy(kind, i, q, device):
+            part = piece(i, q)
+            return pltpu.make_async_remote_copy(
+                src_ref=part, dst_ref=part, send_sem=wss.at[kind, i], recv_sem=wrs.at[kind, i],
+                device_id=device, device_id_type=MESH,
+            )
 
         def pass_own(i):
-            mine = piece(i, quarter)
-            remote(mine, mine, C_WIN + i, C_WIN + i, (1, d, r)).wait_recv()
-            for base, device in ((C_WPEER, peer), (C_WZ, (p, d, z_pair))):
-                copy = remote(mine, mine, base + i, base + i, device)
-                copy.start()
-                sends.append(copy)
+            piece_copy(W_OWN, i, quarter, (1, d, r)).wait_recv()
+            piece_copy(W_PEER, i, quarter, peer).start()
+            piece_copy(W_Z, i, quarter, z_dev).start()
 
         def pass_on(i):
-            theirs = piece(i, other_z + d)
-            remote(theirs, theirs, C_WZ + i, C_WZ + i, peer).wait_recv()
-            copy = remote(theirs, theirs, C_WFWD + i, C_WFWD + i, peer)
-            copy.start()
-            sends.append(copy)
+            piece_copy(W_Z, i, other_z + d, peer).wait_recv()
+            piece_copy(W_ON, i, other_z + d, peer).start()
 
         def have(i):
-            a = piece(i, 2 * lax.rem(r, 2) + 1 - d)
-            b = piece(i, other_z + 1 - d)
-            remote(a, a, C_WPEER + i, C_WPEER + i, peer).wait_recv()
-            remote(b, b, C_WFWD + i, C_WFWD + i, peer).wait_recv()
-
-        pass_own(0)
+            piece_copy(W_PEER, i, this_z + 1 - d, peer).wait_recv()
+            piece_copy(W_ON, i, other_z + 1 - d, peer).wait_recv()
+
+        def each(work, first, last):
+            def body(i, carry):
+                work(i)
+                return carry
+
+            lax.fori_loop(first, last, body, 0)
+
+        zero_rest(12)
+        each(pass_own, 0, 7)
+        each(pass_on, 0, 4)
         remote(h2, h2, C_H2, C_H2, (1, d, r)).wait_recv()
 
         def third_conv(n, carry):
@@ -1110,6 +1353,8 @@
 
         lax.fori_loop(0, 4, third_conv, 0)
         sync(0, 0, 16)
+        pass_own(7)
+        pass_on(4)
 
         def join(n, carry):
             c3, s3 = moments(n, 4 + n, total_out, 2 + n)
@@ -1131,12 +1376,9 @@
             return carry
 
         lax.fori_loop(0, 4, join, 0)
-        copy = remote(u0, u0, C_O1, C_O1, (2, d, r))
-        copy.start()
-        sends.append(copy)
-        pass_on(0)
-        have(0)
-
+        pass_own(8)
+        pass_on(5)
+        each(have, 0, 4)
         zhat4, zhat5 = fs.at[0], fs.at[1]
         z = nn(u0[0:RW, :], wx[0:512, :])
         for n in range(1, 4):
@@ -1158,38 +1400,54 @@
 
         lax.fori_loop(0, 7, hidden, 0)
         h4[0:RV, :] = pb[1:8, 1:8].reshape(RV, BLK).astype(BF16)
-        copy = remote(h4, h4, C_H4, C_H4, (2, d, r))
-        copy.start()
-        sends.append(copy)
+        h4_send = remote(h4, h4, C_H4, C_H4, (2, d, r))
+        h4_send.start()
+
+        def o1_copy(n):
+            part = u0.at[n * RW : (n + 1) * RW]
+            return remote(part, part, C_O1 + n, C_O1 + n, (2, d, r))
+
+        o1_copy(0).start()
+        o1_copy(1).start()
         build_patches(plain_base)
-        pass_own(1)
-        pass_own(2)
-        pass_on(1)
-        pass_own(3)
-        pass_on(2)
-        pass_on(3)
-        pass_own(4)
-        for i in (1, 2, 3):
-            have(i)
-        conv(wx, 2048, zhat5)
+        each(pass_own, 9, 11)
+        pl.semaphore_signal(go, inc=1, device_id=(3, d, r), device_id_type=MESH)
+        pass_on(6)
+        pass_own(11)
+        pass_on(7)
+        pass_own(12)
+        pass_on(8)
+        zhat5[...] = jnp.zeros_like(zhat5)
+
+        def fifth_conv(t, carry):
+            @pl.when(t >= 5)
+            def _():
+                pass_on(4 + t)
+
+            have(4 + t)
+            z = nn(pt[t], wx[rows(2048 + t * 512, 512), :])
+            zhat5[...] += z.reshape(PP, 8, BLK)
+            return carry
+
+        lax.fori_loop(0, 9, fifth_conv, 0)
+        each(pass_own, 13, 17)
         stats_of_map(zhat5, 18, 19)
         sync(2, 18, 2)
         center, scale = moments(18, 19, total_out, 11)
         act_to(zhat5, h5, center, scale, g5, b5, mask)
-        copy = remote(h5, h5, C_H5, C_H5, (3, d, r))
-        copy.start()
-        sends.append(copy)
-        pass_on(4)
-        have(4)
+        h5_send = remote(h5, h5, C_H5, C_H5, (3, d, r))
+        h5_send.start()
+        each(pass_on, 13, 17)
 
         def sixth_conv(n, carry):
+            have(13 + n)
             store_z(f2, n * PP, nn(h5[...], wx[rows(6656 + n * 512, 512), :]), 20 + n, 24 + n)
             return carry
 
         lax.fori_loop(0, 4, sixth_conv, 0)
         sync(3, 20, 8)
         remote(parx.at[4:12], parx.at[4:12], C_PAR3, C_PAR3, (1, d, r)).wait_recv()
-        cot_copy.wait()
+        pltpu.make_async_copy(cot, cotb.at[0:PIX_OUT], ls.at[16]).wait()
 
         def finish(n, carry):
             center, scale = moments(20 + n, 24 + n, total_out, 12 + n)
@@ -1205,7 +1463,7 @@
                 q = o + zhat * g6 + b6
                 s = jax.nn.sigmoid(q)
                 merged = gate_v * (q * s) + (1.0 - gate_v) * o
-                u3[part_rows, :] = merged.reshape(80, BLK).astype(BF16)
+                pt[n, rows(i * 80, 80), :] = merged.reshape(80, BLK).astype(BF16)
                 ct = cotb[c, :, pl.ds(pl.multiple_of(n * BLK, BLK), BLK)].astype(F32)
                 dq = ct * gate_v * (s * (1.0 + q * (1.0 - s)))
                 f3[part] = dq
@@ -1217,12 +1475,7 @@
             return carry
 
         lax.fori_loop(0, 4, finish, 0)
-        out_sends = []
-        for slot, k in enumerate((0, 2, 3)):
-            copy = remote(u3.at[k * RW : (k + 1) * RW], ob, C_SHARE + slot, C_SHARE, (k, d, r))
-            copy.start()
-            out_sends.append(copy)
-        ob[...] = u3[RW : 2 * RW, :]
+        ob[...] = pt[1]
 
         sync(4, 28, 8)
 
@@ -1247,9 +1500,8 @@
         dgx[1] = s_dg
         dgx[3] = s_du
         norm_back(d5, 0, f2, 0, zhat5, 0, g5 * inv[11], s_du * (1.0 / total_out), s_dg * (1.0 / total_out))
-        copy = remote(d5, d5, C_D5, C_D5, (2, d, r))
-        copy.start()
-        sends.append(copy)
+        d5_send = remote(d5, d5, C_D5, C_D5, (2, d, r))
+        d5_send.start()
         conv_back(d5, wx, 2048, plain_base)
 
         def fourth_slopes(a, carry):
@@ -1265,13 +1517,6 @@
         dgx[0] = s_dg
         dgx[2] = s_du
         norm_back(d4, 0, f2, 0, zhat4, 0, g4 * inv[10], s_du * (1.0 / total_out), s_dg * (1.0 / total_out))
-        copy = remote(d4, d4, C_D4, C_D4, (2, d, r))
-        copy.start()
-        sends.append(copy)
-        for first, last, sem, chip in ((0, 4, C_DG2, 2), (4, 12, C_DG3, 3)):
-            copy = remote(dgx.at[first:last], dgx.at[first:last], sem, sem, (chip, d, r))
-            copy.start()
-            sends.append(copy)
 
         def first_block_slopes(n, carry):
             f3[pl.ds(n * PP, PP)] = nt(d4[...], wx[rows(n * 512, 512), :]).reshape(PP, 8, BLK)
@@ -1290,9 +1535,6 @@
             return carry
 
         lax.fori_loop(0, 4, first_block_slopes, 0)
-        z6_send.wait_send()
-        for copy in out_sends:
-            copy.wait_send()
         sync(7, 40, 12)
 
         def third_back(n, carry):
@@ -1302,129 +1544,187 @@
             dg[8 + n] = s_du
             dg[12 + n] = s_du
             m_du = s_du * (1.0 / total_out)
-            norm_back(u1, n * RW, f3, n * PP, f0, n * PP, par[n] * inv[2 + n], m_du, s_d3 * (1.0 / total_out))
-            norm_back(u3, n * RW, f3, n * PP, f1, n * PP, par[4 + n] * inv[6 + n], m_du, s_dp * (1.0 / total_out))
+            norm_back(pt.at[4 + n], 0, f3, n * PP, f0, n * PP, par[n] * inv[2 + n], m_du, s_d3 * (1.0 / total_out))
+            norm_back(u2, n * RW, f3, n * PP, f1, n * PP, par[4 + n] * inv[6 + n], m_du, s_dp * (1.0 / total_out))
             return carry
 
         lax.fori_loop(0, 4, third_back, 0)
-        grad = nt(u1[0:RW, :], wh[0:512, :])
+        grad = nt(pt[4], wh[0:512, :])
         for n in range(1, 4):
-            grad += nt(u1[n * RW : (n + 1) * RW, :], wh[n * 512 : (n + 1) * 512, :])
+            grad += nt(pt[4 + n], wh[n * 512 : (n + 1) * 512, :])
         dh[...] = grad.astype(BF16)
-        copy = remote(dh, dh, C_DH, C_DH, (0, d, r))
-        copy.start()
-        sends.append(copy)
-
-        def shortcut_share(k):
-            g = nt(u3[0:RW, :], wh[2048 + k * 256 : 2304 + k * 256, :])
-            for n in range(1, 4):
-                g += nt(u3[n * RW : (n + 1) * RW, :], wh[2048 + n * 1024 + k * 256 : 2304 + n * 1024 + k * 256, :])
-            return g.astype(BF16)
-
-        for slot, k in enumerate((0, 2, 3)):
-            u2[slot * RW : (slot + 1) * RW, 0:256] = shortcut_share(k)
-            copy = remote(u2.at[slot * RW : (slot + 1) * RW, 0:256], r1, C_GP + slot, C_GP, (k, d, r))
+        dh_send = remote(dh, dh, C_DH, C_DH, (0, d, r))
+        dh_send.start()
+
+        d4_send = remote(d4, d4, C_D4, C_D4, (2, d, r))
+        d4_send.start()
+        def drain_pieces(i, carry):
+            piece_copy(W_PEER, i, quarter, peer).wait_send()
+            piece_copy(W_Z, i, quarter, z_dev).wait_send()
+            piece_copy(W_ON, i, other_z + d, peer).wait_send()
+            return carry
+
+        lax.fori_loop(0, N_PIECE, drain_pieces, 0)
+        say_ready()
+        o1_copy(2).start()
+        o1_copy(3).start()
+        sends = [d4_send, dh_send, d5_send, h5_send, z6_send] + [o1_copy(n) for n in range(4)]
+        for first, last, sem, chip in ((0, 4, C_DG2, 2), (4, 12, C_DG3, 3)):
+            copy = remote(dgx.at[first:last], dgx.at[first:last], sem, sem, (chip, d, r))
             copy.start()
             sends.append(copy)
-        r1[...] = shortcut_share(1)
-
-        def third_weights(m, carry):
-            emit_wide(m, m, h2, slice(None), pl.ds(pl.multiple_of(m * 128, 128), 128), u1)
-            return carry
-
-        lax.fori_loop(0, 4, third_weights, 0)
-
-        def shortcut_weights(m, carry):
-            emit_wide(4 + m, 4 + m, sx, rows((m // 4) * RW, RW), pl.ds(pl.multiple_of(lax.rem(m, 4) * 128, 128), 128), u3)
-            return carry
-
-        lax.fori_loop(0, 8, shortcut_weights, 0)
-        emit_zeros(12, 12)
+        for slot, k in enumerate((0, 2, 3)):
+            copy = remote(pt.at[k], ob, C_SHARE + slot, C_SHARE, (k, d, r))
+            copy.start()
+            sends.append(copy)
+
+        def shortcut_share(k):
+            g = nt(u2[0:RW, :], wh[2048 + k * 256 : 2304 + k * 256, :])
+            for n in range(1, 4):
+                g += nt(u2[n * RW : (n + 1) * RW, :], wh[2048 + n * 1024 + k * 256 : 2304 + n * 1024 + k * 256, :])
+            return g.astype(BF16)
+
+        places = ((h4.at[:, 0:256], 0), (h4.at[:, 256:512], 2), (pt.at[8, :, 0:256], 3))
+
+        def share_copy(slot):
+            place, k = places[slot]
+            return remote(place, r1, C_GP + slot, C_GP, (k, d, r))
+
+        def shortcut_shares():
+            h4_send.wait_send()
+            for slot, (place, k) in enumerate(places):
+                place[...] = shortcut_share(k)
+                share_copy(slot).start()
+            r1[...] = shortcut_share(1)
+
+        def compute(t):
+            @pl.when(t < 4)
+            def _():
+                left = h2[:, pl.ds(pl.multiple_of(t * 128, 128), 128)]
+                for n in range(4):
+                    put_chunk(t, n, tn(left, pt[4 + n]))
+
+            @pl.when(t >= 4)
+            def _():
+                m = t - 4
+                left = sx[rows((m // 4) * RW, RW), pl.ds(pl.multiple_of(lax.rem(m, 4) * 128, 128), 128)]
+                for n in range(4):
+                    put_chunk(t, n, tn(left, u2[n * RW : (n + 1) * RW, :]))
+
+        sum_gradients(12, compute, lambda t: t * 512, lambda t: t, True, 0, {1: shortcut_shares})
         for copy in sends:
             copy.wait_send()
+        for slot in range(3):
+            share_copy(slot).wait_send()
+
 
     @pl.when(p == 2)
     def _():
         for k, slot in ((0, 0), (1, 1), (2, 8), (3, 9)):
             parx[k] = par[slot]
-        sends = [remote(parx.at[0:4], parx.at[0:4], C_PAR2, C_PAR2, (1, d, r))]
-        sends[0].start()
-        load_weights(4, lambda i: (quarter * 4 + i) * SUB, put_narrow(wx, lambda i: quarter * 512 + i * 128))
-        for i in range(4):
-            first, size = PIECES[i]
-            if i > 0:
-                load_weights(
-                    3,
-                    lambda k, i=i: (16 + (i - 1) * 12 + quarter * 3 + k) * SUB,
-                    put_narrow(wx, lambda k, first=first: first + quarter * 384 + k * 128),
-                )
-            part = wx.at[rows(first + quarter * size, size)]
-            copy = remote(part, part, C_WIN + i, C_WIN + i, (1, d, r))
-            copy.start()
-            sends.append(copy)
+        par_send = remote(parx.at[0:4], parx.at[0:4], C_PAR2, C_PAR2, (1, d, r))
+        par_send.start()
+
+        def piece_copy(i):
+            part = wx.at[rows(i * 512 + quarter * 128, 128)]
+            return pltpu.make_async_remote_copy(
+                src_ref=part, dst_ref=part, send_sem=wss.at[W_OWN, i], recv_sem=wrs.at[W_OWN, i],
+                device_id=(1, d, r), device_id_type=MESH,
+            )
+
+        put_w = put_narrow(wx, lambda i: i * 512 + quarter * 128)
+
+        def put(i):
+            put_w(i)
+            piece_copy(i).start()
+
+        load_weights(every_fourth, 13, 0, 13, put)
         pb[...] = jnp.zeros_like(pb)
         clear_patch_pad()
+
+        def drain(i, carry):
+            piece_copy(i).wait_send()
+            return carry
+
+        lax.fori_loop(0, 13, drain, 0)
+        say_ready()
         remote(h4, h4, C_H4, C_H4, (2, d, r)).wait_recv()
         pb[1:8, 1:8] = h4[0:RV, :].astype(F32).reshape(7, 7, 8, BLK)
         build_patches(plain_base)
         remote(d5, d5, C_D5, C_D5, (2, d, r)).wait_recv()
 
-        def fifth_weights(tap, carry):
-            stage_narrow(tn(pt[tap], d5[...]))
-            emit(tap, tap + 4)
-            return carry
-
-        lax.fori_loop(0, 9, fifth_weights, 0)
-        remote(u0, u0, C_O1, C_O1, (2, d, r)).wait_recv()
-        remote(d4, d4, C_D4, C_D4, (2, d, r)).wait_recv()
-
-        def fourth_weights(n, carry):
-            stage_narrow(tn(u0[rows(n * RW, RW), :], d4[...]))
-            emit(9 + n, n)
-            return carry
-
-        lax.fori_loop(0, 4, fourth_weights, 0)
-        dw_copy(0, 0).wait()
-        dw_copy(1, 0).wait()
-        remote(dgx.at[0:4], dgx.at[0:4], C_DG2, C_DG2, (2, d, r)).wait_recv()
-        dg[0], dg[1], dg[8], dg[9] = dgx[0], dgx[1], dgx[2], dgx[3]
-        for copy in sends:
-            copy.wait_send()
+        def compute(t):
+            @pl.when(t < 9)
+            def _():
+                wh[rows(t * 512, 512), :] = tn(pt[t], d5[...]).astype(BF16)
+
+            @pl.when(t == 9)
+            def _():
+                remote(d4, d4, C_D4, C_D4, (2, d, r)).wait_recv()
+                for n in range(4):
+                    part = u0.at[n * RW : (n + 1) * RW]
+                    remote(part, part, C_O1 + n, C_O1 + n, (2, d, r)).wait_recv()
+
+            @pl.when(t >= 9)
+            def _():
+                wh[rows(t * 512, 512), :] = tn(u0[rows((t - 9) * RW, RW), :], d4[...]).astype(BF16)
+
+        def norm_grads():
+            remote(dgx.at[0:4], dgx.at[0:4], C_DG2, C_DG2, (2, d, r)).wait_recv()
+            dg[0], dg[1], dg[8], dg[9] = dgx[0], dgx[1], dgx[2], dgx[3]
+
+        sum_gradients(
+            13, compute, lambda t: t * 512, lambda t: lax.rem(t + 4, 13), False, 0, {10: norm_grads}
+        )
+        par_send.wait_send()
 
     @pl.when(p == 3)
     def _():
         for k in range(4):
             parx[4 + k] = par[k]
             parx[8 + k] = par[8 + k]
-        sends = [remote(parx.at[4:12], parx.at[4:12], C_PAR3, C_PAR3, (1, d, r))]
-        sends[0].start()
+        par_send = remote(parx.at[4:12], parx.at[4:12], C_PAR3, C_PAR3, (1, d, r))
+        par_send.start()
+        say_ready()
 
         def put(i):
-            for j in range(4):
-                wx[rows(6656 + quarter * 512 + i * 32, 32), j * 128 : (j + 1) * 128] = st[
-                    pl.ds(4 * quarter + j, 32, stride=16), :
-                ].astype(BF16)
-
-        load_weights(16, lambda i: i * SUB, put)
-        part = wx.at[rows(6656 + quarter * 512, 512)]
-        copy = remote(part, part, C_WIN + 4, C_WIN + 4, (1, d, r))
-        copy.start()
-        sends.append(copy)
+            for n in range(4):
+                for j in range(4):
+                    wx[rows(6656 + n * 512 + quarter * 128 + i * 32, 32), j * 128 : (j + 1) * 128] = st[
+                        pl.ds(4 * n + j, 32, stride=16), :
+                    ].astype(BF16)
+
+        load_weights(four_rows, 4, 0, 4, put)
+        zero_rest(4)
+        pl.semaphore_wait(go, 1)
+
+        def piece_copy(n):
+            part = wx.at[rows(6656 + n * 512 + quarter * 128, 128)]
+            return pltpu.make_async_remote_copy(
+                src_ref=part, dst_ref=part, send_sem=wss.at[W_OWN, 13 + n], recv_sem=wrs.at[W_OWN, 13 + n],
+                device_id=(1, d, r), device_id_type=MESH,
+            )
+
+        for n in range(4):
+            piece_copy(n).start()
         remote(h5, h5, C_H5, C_H5, (3, d, r)).wait_recv()
         remote(u1, u1, C_Z6, C_Z6, (3, d, r)).wait_recv()
 
-        def sixth_weights(m, carry):
-            emit_wide(m, m, h5, slice(None), pl.ds(pl.multiple_of(m * 128, 128), 128), u1)
-            return carry
-
-        lax.fori_loop(0, 4, sixth_weights, 0)
-        emit_zeros(4, 4)
-        remote(dgx.at[4:12], dgx.at[4:12], C_DG3, C_DG3, (3, d, r)).wait_recv()
-        for k in range(4):
-            dg[k] = dgx[4 + k]
-            dg[8 + k] = dgx[8 + k]
-        for copy in sends:
-            copy.wait_send()
+        def compute(t):
+            left = h5[:, pl.ds(pl.multiple_of(t * 128, 128), 128)]
+            for n in range(4):
+                put_chunk(t, n, tn(left, u1[n * RW : (n + 1) * RW, :]))
+
+        def norm_grads():
+            remote(dgx.at[4:12], dgx.at[4:12], C_DG3, C_DG3, (3, d, r)).wait_recv()
+            for k in range(4):
+                dg[k] = dgx[4 + k]
+                dg[8 + k] = dgx[8 + k]
+
+        sum_gradients(4, compute, lambda t: t * 512, lambda t: t, True, 0, {1: norm_grads})
+        for n in range(4):
+            piece_copy(n).wait_send()
+        par_send.wait_send()
 
     @pl.when(p != 1)
     def _():
@@ -1447,13 +1747,8 @@
         return carry
 
     lax.fori_loop(0, 7, place, 0)
-    gi_copy = pltpu.make_async_copy(f3.at[0:PIX_IN, :, 0:256], gi, ls.at[7])
+    gi_copy = pltpu.make_async_copy(f3.at[0:PIX_IN, :, 0:256], gi, ls.at[17])
     gi_copy.start()
-    for k in range(NSETS):
-        hot = (set_col == float(k)).astype(F32)
-        for n in range(8):
-            dgb[k : k + 1, n * BLK : (n + 1) * BLK] = jnp.sum(dg[n] * hot, axis=0, keepdims=True)
-            dgb[4 + k : 5 + k, n * BLK : (n + 1) * BLK] = jnp.sum(dg[8 + n] * hot, axis=0, keepdims=True)
     gi_copy.wait()
 
 
@@ -1474,11 +1769,11 @@
         in_specs=[any_space, any_space, vmem, vmem, vmem, any_space],
         out_specs=(vmem, any_space, any_space, vmem),
         scratch_shapes=[
-            pltpu.VMEM((2, 28, 8, 1024), BF16),
-            pltpu.VMEM((2, 1, SUB), BF16),
-            pltpu.VMEM((2048, 128), F32),
-            pltpu.VMEM((6144, BLK), BF16),
-            pltpu.VMEM((8704, BLK), BF16),
+            pltpu.VMEM((4, 28, 8, 1024), BF16),
+            pltpu.VMEM((RING, 1, SUB), BF16),
+            pltpu.VMEM((1024, 128), F32),
+            pltpu.VMEM((6656, BLK), BF16),
+            pltpu.VMEM((8768, BLK), BF16),
             pltpu.VMEM((4 * PP, 8, BLK), F32),
             pltpu.VMEM((4 * PP, 8, BLK), F32),
             pltpu.VMEM((4 * PP, 8, BLK), F32),
@@ -1486,7 +1781,6 @@
             pltpu.VMEM((2, PP, 8, BLK), F32),
             pltpu.VMEM((16, 16, 8, BLK), F32),
             pltpu.VMEM((9, RW, BLK), BF16),
-            pltpu.VMEM((4 * RW, BLK), BF16),
             pltpu.VMEM((4 * RW, BLK), BF16),
             pltpu.VMEM((4 * RW, BLK), BF16),
             pltpu.VMEM((4 * RW, BLK), BF16),
@@ -1508,10 +1802,19 @@
             pltpu.VMEM((12, 8, BLK), F32),
             pltpu.VMEM((16, 8, BLK), F32),
             pltpu.VMEM((12, 8, BLK), F32),
-            pltpu.VMEM((2, 2048, 128), BF16),
-            pltpu.SemaphoreType.DMA((8,)),
+            pltpu.VMEM((4, 1024, 128), BF16),
+            pltpu.VMEM((3328, BLK), BF16),
+            pltpu.VMEM((2, 8, 4096), F32),
+            pltpu.VMEM((8, 4096), F32),
+            pltpu.SemaphoreType.DMA((18,)),
             pltpu.SemaphoreType.DMA((N_SEM,)),
             pltpu.SemaphoreType.DMA((N_SEM,)),
+            pltpu.SemaphoreType.DMA((4, N_PIECE)),
+            pltpu.SemaphoreType.DMA((4, N_PIECE)),
+            pltpu.SemaphoreType.DMA((5, 13)),
+            pltpu.SemaphoreType.DMA((5, 13)),
+            pltpu.SemaphoreType.REGULAR((2,)),
+            pltpu.SemaphoreType.REGULAR,
         ],
         compiler_params=pltpu.CompilerParams(
             collective_id=0, has_side_effects=True, vmem_limit_bytes=64 * 1024 * 1024
@@ -1524,8 +1827,7 @@
         meta,
         jnp.transpose(cotangent, (1, 0, 2)),
     )
-    dw = lax.psum(dw, ("dp", "rep")).astype(F32).reshape(1, P_SIZE)
-    dgb = lax.psum(dgb, "rep")
+    dw = dw.astype(F32).reshape(1, P_SIZE)
     return (
         jnp.transpose(out, (1, 0, 2)),
         jnp.transpose(gi, (1, 0, 2)),
@@ -1537,7 +1839,7 @@
 
 def solution(mesh):
     sizes = dict(mesh.shape)
-    fits = sizes["pipe"] == 4 and sizes["dp"] == 2 and sizes["rep"] % 2 == 0
+    fits = sizes["pipe"] == 4 and sizes["dp"] == 2 and sizes["rep"] == 4
     placed = (
         P(("dp", "rep"), None, None),
         P("pipe", None),

time: 567 us -> 217 us (0.38)
  waiting for transfers between devices: 314 us -> 0 us
  between operations: 14.1 us -> 0.65 us
  local copies, waits for them, and re-layouts: 18.1 us -> 5.23 us
  other arithmetic: 17.8 us -> 9.74 us
    psum x2 -> x0, waiting for transfers between devices: 314 us -> none  [the longest x1 277 us: one_kernel(): dw = lax.psum(dw, ('dp', 'rep')).astype(F32).reshape(1, P_SIZE)]
    unnamed x9 -> x8, local copies, waits for them, and re-layouts: 16.3 us -> 3.41 us
    reshape x1, other arithmetic: 16.4 us -> 8.4 us  [one_kernel(): dw = dw.astype(F32).reshape(1, P_SIZE)]
  transfers between devices with their start and end apart: 2 -> 0, of which waited for: 2 -> 0; matrix products, arithmetic and copies ran while one was open for 3% -> 0% of each run, Pallas kernels for 0% -> 0%
where the time goes in v2:
time: 217 us; the launch traced here: 213 us
  Pallas kernels  197 us (91%)
  other arithmetic  9.74 us (4%)
  local copies, waits for them, and re-layouts  5.23 us (2%)
    pallas_call x1, Pallas kernels, one_kernel(): pl.pallas_call(whole_kernel, out_shape=(jax.ShapeDtypeStruct((PIX_OUT, 8,...  197 us
    reshape x1, other arithmetic, one_kernel(): dw = dw.astype(F32).reshape(1, P_SIZE)  8.4 us

profile of v2, /device:TPU:5, one launch (start us, length us, event | category | flops | bytes accessed | tf_op | source)
XLA Modules:
  0.0 212.7 jit_solution(3339081743232824990)
XLA Ops:
  0.6 0.7 convert_bitcast_fusion
  1.3 0.1 pad.3.clone
  1.4 0.1 copy.15
  1.4 0.8 copy.13
  2.2 0.8 copy.14
  3.0 0.7 maximum_maximum_fusion.meta
  3.6 197.1 %shard_map.119 = (bf16[49,8,512]{2,1,0:T(8,128)(2,1)}, f32[196,8,256]{2,1,0:T(8,128)}, bf16[26624,128]{1,0:T(8,128)(2,1)}, f32[8,4096]{1,0:T(8,128)}) custom-call(bf16[196,8,1024]{2,1,0:T(8,128)(2,1)} %bitcast.14, bf16[1,3407872]{1,0:T(2,128)(2,1)} %wts.1, f32[4,4096]{1,0:T(4,128)} %bitcast.18, f32[4,4096]{1,0:T(4,128)} %bitcast.19, ...), custom_call_target="tpu_custom_call" | custom-call | tf_op jit(solution)/shard_map/pallas_call | solution.py:1761
  200.8 1.7 slice_bitcast_fusion
  202.4 0.0 copy-start.1
  202.4 0.0 copy-start
  202.4 8.4 %reshape.18 = f32[26624,128]{1,0:T(8,128)} convert(bf16[26624,128]{1,0:T(8,128)(2,1)} %get-tuple-element.11) | non-fusion elementwise | flops 3407872 | bytes 20447232 | tf_op jit(solution)/shard_map/reshape | solution.py:1830
  210.8 0.0 copy-done.1
  210.8 0.7 copy.18
  211.6 0.0 copy-done
  211.6 1.2 copy.19
  (3 shorter events, 0.0 us)
Async XLA Ops:
  202.4 8.4 %copy-start.1 = (bf16[49,8,512]{2,1,0:T(8,128)(2,1)S(1)}, bf16[49,8,512]{2,1,0:T(8,128)(2,1)}, u32[]{:S(2)}) copy-start(bf16[49,8,512]{2,1,0:T(8,128)(2,1)} %get-tuple-element.9) | copy-start | bytes 1204228
  202.4 9.2 %copy-start = (f32[196,8,256]{2,1,0:T(8,128)S(1)}, f32[196,8,256]{2,1,0:T(8,128)}, u32[]{:S(2)}) copy-start(f32[196,8,256]{2,1,0:T(8,128)} %get-tuple-element.10) | copy-start | bytes 4816900

commit v3 on v2

--- a/solution.py
+++ b/solution.py
@@ -644,14 +644,24 @@
 BF16 = jnp.bfloat16
 MESH = pl.DeviceIdType.MESH
 
-C_H2, C_H4, C_H5, C_Z6, C_D5, C_D4, C_DH = range(8, 15)
+E_WIDE, E_WIDE_NEXT = 2, 6
+C_H2, C_H4, C_D5, C_D4, C_DH = range(10, 15)
 C_O1, C_SHARE, C_GI, C_GP = 15, 19, 22, 25
 C_PAR2, C_PAR3, C_DG2, C_DG3, C_BN1, C_BN2, C_BN3 = range(28, 35)
 N_SEM = 35
 N_PIECE = 17
-W_OWN, W_PEER, W_Z, W_ON = range(4)
-G_CORE, G_IN, G_ACROSS, G_OUT, G_DONE = range(5)
+W_OWN, W_PEER, W_Z, W_ON, W_VIA = range(5)
+VIA, HALF = 8, 11
+W_BASE = (0, 17, 34, 45, 56 - VIA)
+S_CORE, S_IN, S_OUT, S_HAND, S_BACK, S_DONE, S_ACROSS, N_SUM_SEND = 0, 1, 2, 3, 4, 5, 9, 17
+R_CORE, R_IN, R_ACROSS, R_OUT, R_GIVE = (0, 8), (8, 12), (20, 8), (28, 12), (40, 4)
+R_DONE, R_BACK, R_HAND, N_SUM_RECV = 44, 45, 46, 64
 RING = 8
+SUBS = 2
+SUB_ROWS = 256 // SUBS
+Z1_ZERO = 3136
+ACROSS_LAG, OUT_LAG = 3 * SUBS // 2 + 1, 4 * SUBS
+LAST_TURN = OUT_LAG - 2
 
 
 def nn(a, b):
@@ -666,12 +676,16 @@
     return lax.dot_general(a, b, (((0,), (0,)), ((), ())), preferred_element_type=F32)
 
 
+def sigmoid(v):
+    return 0.5 + 0.5 * jnp.tanh(0.5 * v)
+
+
 def rows(start, size):
     return pl.ds(pl.multiple_of(start, 16), size)
 
 
 def whole_kernel(
-    img, wts, gain, bias, meta, cot,
+    img, wts, gain, bias, width, sets, gates, cot,
     out, gi, dw, dgb,
     imgb, raw, st, wh, wx, f0, f1, f2, f3, fs, pb, pt, u0, u1, u2, sx, cotb,
     h2, h4, h5, d5, d4, dh, r0, r1, ob, tx, rx, inv, par, parx, dg, dgx, sb, rd, bz, dgs,
@@ -694,6 +708,10 @@
         copy.start()
         copy.wait()
 
+    def exchange_of(event, first, count):
+        part = pl.ds(first, count)
+        return remote(tx.at[part], rx.at[part], event, event, peer)
+
     def both(slot):
         return tx[slot] + rx[slot]
 
@@ -704,10 +722,10 @@
         return center, scale
 
     def silu(v):
-        return v * jax.nn.sigmoid(v)
+        return v * sigmoid(v)
 
     def slope(v):
-        s = jax.nn.sigmoid(v)
+        s = sigmoid(v)
         return s * (1.0 + v * (1.0 - s))
 
     def clear_pad(ref, first):
@@ -715,9 +733,16 @@
         keep = lax.broadcasted_iota(jnp.int32, tile.shape, 0) < 8
         ref[rows(first + RW - 16, 16), :] = jnp.where(keep, tile, 0.0).astype(BF16)
 
-    def mask_of(column):
-        lane = lax.broadcasted_iota(jnp.int32, (8, BLK), 1).astype(F32)
-        return (lane < meta[:, column : column + 1]).astype(F32)
+    def per_row(value_of):
+        row = lax.broadcasted_iota(jnp.int32, (8, BLK), 0)
+        out = jnp.zeros((8, BLK), jnp.int32)
+        for m in range(MB):
+            out = jnp.where(row == m, value_of(m), out)
+        return out
+
+    def mask_of(block):
+        lane = lax.broadcasted_iota(jnp.int32, (8, BLK), 1)
+        return (lane < per_row(lambda m: width[block, m])).astype(F32)
 
     def five(body, init=0):
         return lax.fori_loop(0, 5, lambda c, carry: body(pl.ds(c * 10, 10), c, carry), init)
@@ -778,17 +803,55 @@
         return put
 
     def put_chunk(t, n, block):
-        wh[rows(t * 512 + n * 64, 64), :] = block[0:64].astype(BF16)
-        wh[rows(t * 512 + 256 + n * 64, 64), :] = block[64:128].astype(BF16)
+        size = SUB_ROWS // 4
+        for part in range(2 * SUBS):
+            wh[rows(t * 512 + part * SUB_ROWS + n * size, size), :] = block[part * size : (part + 1) * size].astype(BF16)
 
     def plain(turn):
         return turn
 
-    def every_fourth(turn):
-        return 4 * turn + quarter
-
-    def four_rows(turn):
-        return 4 * quarter + turn
+    def own_parts(turn):
+        late = turn - HALF
+        return jnp.where(late < 0, 4 * turn + quarter, 4 * HALF + (late // 2) * 4 + 2 * d + lax.rem(late, 2))
+
+    def half_rows(turn):
+        return 8 * d + turn
+
+    def piece_copy(kind, i, q, device):
+        part = wx.at[rows(i * 512 + q * 128, 128)]
+        return pltpu.make_async_remote_copy(
+            src_ref=part, dst_ref=part, send_sem=wss.at[kind], recv_sem=wrs.at[W_BASE[kind] + i],
+            device_id=device, device_id_type=MESH,
+        )
+
+    def half_copy(kind, i, which, device):
+        part = wx.at[rows(i * 512 + which * 256, 256)]
+        order = min(i, 13) if kind == W_VIA else i
+        return pltpu.make_async_remote_copy(
+            src_ref=part, dst_ref=part, send_sem=wss.at[kind], recv_sem=wrs.at[W_BASE[kind] + order],
+            device_id=device, device_id_type=MESH,
+        )
+
+    def all_sent(semaphore, ref):
+        pltpu.make_async_remote_copy(
+            src_ref=ref, dst_ref=ref, send_sem=semaphore, recv_sem=rs.at[0], device_id=peer, device_id_type=MESH
+        ).wait_send()
+
+    def all_here(semaphore, ref):
+        pltpu.make_async_remote_copy(
+            src_ref=ref, dst_ref=ref, send_sem=ss.at[0], recv_sem=semaphore, device_id=peer, device_id_type=MESH
+        ).wait_recv()
+
+    def o1_copy(n, chip):
+        part = u0.at[n * RW : (n + 1) * RW]
+        return remote(part, part, C_O1 + n, C_O1 + n, (chip, d, r))
+
+    def each(work, first, last):
+        def body(i, carry):
+            work(i)
+            return carry
+
+        lax.fori_loop(first, last, body, 0)
 
     def img_copy(q, slot):
         return pltpu.make_async_copy(img.at[pl.ds(q * 28, 28)], imgb.at[slot], ls.at[slot])
@@ -814,30 +877,29 @@
     inner = jnp.logical_not(outer)
     z_dev, across = (p, d, z_pair), (p, d, 3 - r)
 
-    def grad_copy(kind, t, src, dst, device):
+    def grad_copy(send, recv, src, dst, device):
         return pltpu.make_async_remote_copy(
-            src_ref=src, dst_ref=dst, send_sem=ass.at[kind, t], recv_sem=ars.at[kind, t],
+            src_ref=src, dst_ref=dst, send_sem=ass.at[send], recv_sem=ars.at[recv],
             device_id=device, device_id_type=MESH,
         )
 
-    def chunk_rows(chunk, half):
-        return dw.at[pl.ds(pl.multiple_of(chunk * 2048 + half * 1024, 1024), 1024)]
-
-    def zero_rest(first):
-        sb[0] = jnp.zeros((1024, 128), BF16)
+    def in_turn(ring, u):
+        return ring[0] + lax.rem(u, ring[1])
+
+    def zero_rest(first, source):
+        source[...] = jnp.zeros(source.shape, BF16)
 
         def body(i, carry):
-            for half in range(2):
-                copy = pltpu.make_async_copy(sb.at[0], chunk_rows(first + i, half), ls.at[4])
-                copy.start()
-                copy.wait()
+            copy = pltpu.make_async_copy(source, dw.at[pl.ds((first + i) * 4, 4)], ls.at[18])
+            copy.start()
+            copy.wait()
             return carry
 
         lax.fori_loop(0, 13 - first, body, 0)
 
     def bn_sums():
         for k in range(NSETS):
-            hot = (set_col == float(k)).astype(F32)
+            hot = (set_of == k).astype(F32)
             for n in range(8):
                 cols = slice(n * BLK, (n + 1) * BLK)
                 dgs[k : k + 1, cols] = jnp.sum(dg[n] * hot, axis=0, keepdims=True)
@@ -859,116 +921,194 @@
         def _():
             pl.semaphore_signal(ready.at[1], inc=1, device_id=across, device_id_type=MESH)
 
-    def sum_gradients(count, compute, at_row, chunk_of, wide, z1, extra):
-        z2 = z1 + count * 256
-
-        def half(t, which):
-            return wh.at[rows(at_row(t) + which * 256, 256)]
-
-        def from_z(t):
-            return wx.at[rows(z1 + t * 256, 256)]
-
-        def from_across(t):
-            return wx.at[rows(z2 + t * 256, 256)]
-
-        def to_core(t):
-            return grad_copy(G_CORE, t, half(t, 1 - d), rd.at[rows(t * 256, 256)], peer)
-
-        def inwards(t):
-            return grad_copy(G_IN, t, half(t, d), from_z(t), z_dev)
-
-        def exchange(t):
-            return grad_copy(G_ACROSS, t, half(t, d), from_across(t), across)
-
-        def outwards(t):
-            return grad_copy(G_OUT, t, half(t, d), from_z(t), z_dev)
-
-        def done_core(t):
-            part = chunk_rows(chunk_of(t), d)
-            return grad_copy(G_DONE, t, sb.at[lax.rem(t, 4)], part, peer)
-
-        def done_here(t):
-            return pltpu.make_async_copy(sb.at[lax.rem(t, 4)], chunk_rows(chunk_of(t), d), ls.at[4 + lax.rem(t, 4)])
-
-        def add(t, other):
-            total = half(t, d)[...].astype(F32) + other[...].astype(F32)
-            half(t, d)[...] = total.astype(BF16)
-
-        def finish(t, ref):
-            @pl.when(t >= 4)
-            def _():
-                done_here(t - 4).wait()
-                done_core(t - 4).wait_send()
+    def sum_gradients(
+        count, compute, at_row, chunk_of, wide, z1, extra,
+        lend=(), passed=(), helper=0, helper_turn=None, handed_in=None, lent_by=None, computed=None, packed_here=None,
+    ):
+        turns = SUBS * count
+        last_lent = SUBS * (count + len(lend))
+        last_given = last_lent + SUBS * len(passed)
+        computed = (0, count) if computed is None else computed
+        packed_here = (0, count) if packed_here is None else packed_here
+        first_own, own_turns = packed_here[0] * SUBS, packed_here[1] * SUBS
+        z2 = z1 + last_given * SUB_ROWS
+
+        def when_own(u, work):
+            if handed_in is None:
+                work()
+            else:
+                pl.when(jnp.logical_not(handed_in(u // SUBS)))(work)
+
+        def when_handed(u, work):
+            if handed_in is not None:
+                pl.when(handed_in(u // SUBS))(work)
+
+        def when_kept(u, work):
+            if lent_by is None:
+                work()
+            else:
+                pl.when(jnp.logical_not(lent_by[0](u // SUBS)))(work)
+
+        def when_lent(u, work):
+            if lent_by is not None:
+                pl.when(lent_by[0](u // SUBS))(work)
+
+        def half(u, which):
+            return wh.at[rows(at_row(u // SUBS) + which * 256 + lax.rem(u, SUBS) * SUB_ROWS, SUB_ROWS)]
+
+        def from_z(u):
+            return wx.at[rows(z1 + u * SUB_ROWS, SUB_ROWS)]
+
+        def from_across(u):
+            return wx.at[rows(z2 + u * SUB_ROWS, SUB_ROWS)]
+
+        def from_core(u):
+            return rd.at[rows(u * SUB_ROWS, SUB_ROWS)]
+
+        def to_core(u):
+            recv = jnp.where(u < turns, in_turn(R_CORE, u), in_turn(R_GIVE, u))
+            return grad_copy(S_CORE, recv, half(u, 1 - d), from_core(u), peer)
+
+        def inwards(u):
+            return grad_copy(S_IN, in_turn(R_IN, u), half(u, d), from_z(u), z_dev)
+
+        def exchange(u):
+            return grad_copy(S_ACROSS + lax.rem(u, 8), in_turn(R_ACROSS, u), half(u, d), from_across(u), across)
+
+        def outwards(u):
+            return grad_copy(S_OUT, in_turn(R_OUT, u), half(u, d), from_z(u), z_dev)
+
+        def packed(u, which):
+            return dw.at[chunk_of(u // SUBS) * 4 + which * 2 + lax.rem(u, SUBS)]
+
+        def done_core(u, turn):
+            slot = lax.rem(turn, 4)
+            return grad_copy(S_DONE + slot, R_DONE, sb.at[slot], packed(u, d), peer)
+
+        def done_here(u, turn):
+            slot = lax.rem(turn, 4)
+            return pltpu.make_async_copy(sb.at[slot], packed(u, d), ls.at[4 + slot])
+
+        def add(u, other):
+            sums = half(u, d)[...].astype(F32) + other[...].astype(F32)
+            half(u, d)[...] = sums.astype(BF16)
+
+        def pack(u, turn, ref):
+            @pl.when(turn >= 4)
+            def _():
+                done_here(u, turn).wait()
+                done_core(u, turn).wait_send()
 
             value = ref[...].astype(F32)
             for j in range(4):
                 cols = slice(j * 128, (j + 1) * 128)
                 if wide:
                     for n in range(4):
-                        st[pl.ds(4 * n + j, 64, stride=16), :] = value[n * 64 : (n + 1) * 64, cols]
+                        part = SUB_ROWS // 4
+                        st[pl.ds(4 * n + j, part, stride=16), :] = value[n * part : (n + 1) * part, cols]
                 else:
-                    st[pl.ds(j, 256, stride=4), :] = value[:, cols]
-            sb[lax.rem(t, 4)] = st[...].astype(BF16)
-            done_here(t).start()
-            done_core(t).start()
+                    st[pl.ds(j, SUB_ROWS, stride=4), :] = value[:, cols]
+            sb[lax.rem(turn, 4)] = st[...].astype(BF16)
+            done_here(u, turn).start()
+            done_core(u, turn).start()
+
+        def hand(u):
+            theirs = helper_turn(u // SUBS) * SUBS + lax.rem(u, SUBS)
+            place = wh.at[rows(theirs * SUB_ROWS + (theirs // SUBS + d) * 256, SUB_ROWS)]
+            return grad_copy(S_HAND, R_HAND + theirs, half(u, d), place, (helper, d, r))
+
+        def handed(u):
+            return grad_copy(S_HAND, R_HAND + u, half(u, d), half(u, d), (p, d, r))
+
+        def give_back(u, ref):
+            t = u // SUBS
+            theirs = lent_by[2](t) * SUBS + lax.rem(u, SUBS)
+            place = wx.at[rows(jnp.where(lent_by[1](t) == 0, Z1_ZERO, 0) + theirs * SUB_ROWS, SUB_ROWS)]
+            return grad_copy(S_BACK, R_BACK, ref, place, (lent_by[1](t), d, r))
+
+        def finish(u, ref):
+            when_kept(u, lambda: pack(u, u - first_own, ref))
+            when_lent(u, lambda: give_back(u, ref).start())
+
+        def give(t):
+            compute(t)
+            for k in range(SUBS):
+                to_core(t * SUBS + k).start()
+            for k in range(SUBS):
+                u = t * SUBS + k
+                to_core(u).wait_recv()
+                add(u, from_core(u))
+                hand(u).start()
 
         def step(it, carry):
             for when, work in extra.items():
                 pl.when(it == when)(work)
-
-            @pl.when(it < count)
-            def _():
-                compute(it)
+            for k, when in enumerate(lend + passed):
+                pl.when(it == when)(lambda k=k: give(jnp.int32(count + k)))
+
+            def start():
+                @pl.when(lax.rem(it, SUBS) == 0)
+                def _():
+                    compute(it // SUBS)
+
                 to_core(it).start()
 
-            t1 = it - 1
-
-            @pl.when((t1 >= 0) & (t1 < count))
-            def _():
-                to_core(t1).wait_recv()
-                add(t1, rd.at[rows(t1 * 256, 256)])
-
-                @pl.when(outer & (t1 == 0))
+            @pl.when(it < turns)
+            def _():
+                when_own(it, start)
+
+            u1 = it - 1
+
+            @pl.when((u1 >= 0) & (u1 < turns))
+            def _():
+                def join_cores():
+                    to_core(u1).wait_recv()
+                    add(u1, from_core(u1))
+
+                when_own(u1, join_cores)
+                when_handed(u1, lambda: handed(u1).wait_recv())
+
+                @pl.when(outer & (u1 == 0))
                 def _():
                     pl.semaphore_wait(ready.at[0], 1)
 
                 @pl.when(outer)
                 def _():
-                    inwards(t1).start()
-
-            t2 = it - 2
-
-            @pl.when(inner & (t2 >= 0) & (t2 < count))
-            def _():
-                @pl.when(t2 == 0)
+                    inwards(u1).start()
+
+            u2 = it - 2
+
+            @pl.when(inner & (u2 >= 0) & (u2 < turns))
+            def _():
+                @pl.when(u2 == 0)
                 def _():
                     pl.semaphore_wait(ready.at[1], 1)
 
-                inwards(t2).wait_recv()
-                add(t2, from_z(t2))
-                exchange(t2).start()
-
-            t3 = it - 3
-
-            @pl.when(inner & (t3 >= 0) & (t3 < count))
-            def _():
-                @pl.when(t3 == 0)
+                inwards(u2).wait_recv()
+                add(u2, from_z(u2))
+                exchange(u2).start()
+
+            u4 = it - ACROSS_LAG
+
+            @pl.when(inner & (u4 >= 0) & (u4 < turns))
+            def _():
+                @pl.when(u4 == 0)
                 def _():
                     pl.semaphore_wait(ready.at[0], 1)
 
-                exchange(t3).wait()
-                add(t3, from_across(t3))
-                outwards(t3).start()
-                finish(t3, half(t3, d))
-
-            t5 = it - 5
-
-            @pl.when(outer & (t5 >= 0) & (t5 < count))
-            def _():
-                outwards(t5).wait_recv()
-                finish(t5, from_z(t5))
-
-            @pl.when(it == count - 3)
+                exchange(u4).wait()
+                add(u4, from_across(u4))
+                outwards(u4).start()
+                finish(u4, half(u4, d))
+
+            u8 = it - OUT_LAG
+
+            @pl.when(outer & (u8 >= 0) & (u8 < turns))
+            def _():
+                outwards(u8).wait_recv()
+                finish(u8, from_z(u8))
+
+            @pl.when(it == turns - 2 * SUBS)
             def _():
                 bn_sums()
 
@@ -976,13 +1116,13 @@
                 def _():
                     bn_in().start()
 
-            @pl.when(inner & (it == count))
+            @pl.when(inner & (it == turns))
             def _():
                 bn_in().wait_recv()
                 dgs[...] += bz[0]
                 bn_across().start()
 
-            @pl.when(inner & (it == count + 3))
+            @pl.when(inner & (it == turns + 2 * SUBS))
             def _():
                 bn_across().wait()
                 dgb[...] = dgs[...] + bz[1]
@@ -990,7 +1130,7 @@
 
             return carry
 
-        lax.fori_loop(0, count + 5, step, 0)
+        lax.fori_loop(0, turns + OUT_LAG, step, 0)
 
         @pl.when(outer)
         def _():
@@ -1002,27 +1142,37 @@
         def _():
             bn_out().wait_send()
 
-        def drain(t, carry):
-            to_core(t).wait_send()
-
-            @pl.when(outer)
-            def _():
-                inwards(t).wait_send()
-
-            @pl.when(inner)
-            def _():
-                outwards(t).wait_send()
-
-            @pl.when(t >= count - 4)
-            def _():
-                done_here(t).wait()
-                done_core(t).wait_send()
-
-            theirs = chunk_rows(chunk_of(t), 1 - d)
-            grad_copy(G_DONE, t, sb.at[0], theirs, peer).wait_recv()
-            return carry
-
-        lax.fori_loop(0, count, drain, 0)
+        def unit_rows(units):
+            return wh.at[0 : units * SUB_ROWS]
+
+        if lend:
+            all_here(ars.at[R_BACK], unit_rows(last_lent - turns))
+
+            def take(u, carry):
+                pack(u, own_turns + u - turns, from_z(u))
+                return carry
+
+            lax.fori_loop(turns, last_lent, take, 0)
+
+        @pl.when(outer)
+        def _():
+            all_sent(ass.at[S_IN], unit_rows(turns))
+
+        @pl.when(inner)
+        def _():
+            all_sent(ass.at[S_OUT], unit_rows(turns))
+
+        made = computed[1] * SUBS + last_given - turns
+        if made:
+            all_sent(ass.at[S_CORE], unit_rows(made))
+        if last_given > turns:
+            all_sent(ass.at[S_HAND], unit_rows(last_given - turns))
+        if lent_by is not None:
+            all_sent(ass.at[S_BACK], unit_rows(lent_by[3] * SUBS))
+        all_here(ars.at[R_DONE], dw.at[pl.ds(0, own_turns + last_lent - turns)])
+        for slot in range(4):
+            done_here(first_own, jnp.int32(slot)).wait()
+            done_core(first_own, jnp.int32(slot)).wait_send()
 
     @pl.when(p == 0)
     def _():
@@ -1037,20 +1187,20 @@
 
     @pl.when(p == 2)
     def _():
-        open_weights(every_fourth, 13)
+        open_weights(own_parts, 15)
 
     @pl.when(p == 3)
     def _():
-        open_weights(four_rows, 4)
+        open_weights(half_rows, 8)
 
     barrier = pltpu.get_barrier_semaphore()
     for device in (peer, (p, d, z_pair), (p, d, 3 - r)) + tuple((lax.rem(p + k, 4), d, r) for k in (1, 2, 3)):
         pl.semaphore_signal(barrier, inc=1, device_id=device, device_id_type=MESH)
 
     block_two = p >= 2
-    set_col = jnp.where(block_two, meta[:, 3:4], meta[:, 2:3])
+    set_of = per_row(lambda m: jnp.where(block_two, sets[1, m], sets[0, m]))
     for k in range(NSETS):
-        hot = (set_col == float(k)).astype(F32)
+        hot = (set_of == k).astype(F32)
         for n in range(8):
             g = hot * gain[k : k + 1, n * BLK : (n + 1) * BLK]
             b = hot * bias[k : k + 1, n * BLK : (n + 1) * BLK]
@@ -1147,10 +1297,45 @@
         five(body)
         clear_pad(target, first)
 
+    def gi_copy():
+        return pltpu.make_async_copy(f3.at[0:PIX_IN, :, 0:256], gi, ls.at[17])
+
+    def final_part():
+        @pl.when(p != 1)
+        def _():
+            remote(ob, ob, C_SHARE, C_SHARE, (p, d, r)).wait_recv()
+            remote(r1, r1, C_GP, C_GP, (p, d, r)).wait_recv()
+
+        @pl.when(p != 0)
+        def _():
+            remote(r0, r0, C_GI, C_GI, (p, d, r)).wait_recv()
+
+        out[...] = ob[0:RV, :].astype(F32).reshape(PIX_OUT, 8, BLK).astype(BF16)
+        f0[0:PP, :, 0:256] = r1[...].astype(F32).reshape(PP, 8, 256)
+
+        def place(a, carry):
+            m = r0[rows(a * 224, 224), :].astype(F32).reshape(28, 8, 256)
+            first = m[0:14].reshape(7, 2, 8, 256)
+            even = first[:, 0] + f0[pl.ds(a * 7, 7), :, 0:256]
+            f3[pl.ds(a * 28, 14), :, 0:256] = jnp.stack([even, first[:, 1]], axis=1).reshape(14, 8, 256)
+            f3[pl.ds(a * 28 + 14, 14), :, 0:256] = m[14:28]
+            return carry
+
+        lax.fori_loop(0, 7, place, 0)
+        gi_copy().start()
+
     @pl.when(p == 0)
     def _():
         mask = mask_of(0)
-        say_ready()
+
+        def relay(i):
+            piece_copy(W_VIA, i, quarter, (0, d, r)).wait_recv()
+            piece_copy(W_OWN, i, quarter, (1, d, r)).start()
+
+        def relay_half(i):
+            half_copy(W_VIA, i, d, (0, d, r)).wait_recv()
+            half_copy(W_OWN, i, d, (1, d, r)).start()
+
         put_w = put_narrow(wh, lambda i: i * 128)
         load_weights(plain, 44, 0, 8, put_w)
 
@@ -1164,6 +1349,7 @@
             return add_stats(carry, z, z * z)
 
         tx[0], tx[1] = over_images(first_conv, zero_stats)
+        relay(VIA)
         exchange = remote(tx.at[pl.ds(0, 2)], rx.at[pl.ds(0, 2)], 0, 0, peer)
         exchange.start()
         pb[...] = jnp.zeros_like(pb)
@@ -1185,20 +1371,26 @@
             return carry
 
         lax.fori_loop(0, 14, hidden, 0)
+        relay(VIA + 1)
         build_patches(strided_base)
         conv(wh, 1024, fs.at[0])
+        relay(VIA + 2)
         stats_of_map(fs.at[0], 2, 3)
         sync(1, 2, 2)
         center, scale = moments(2, 3, total_out, 1)
         act_to(fs.at[0], h2, center, scale, g2, b2, mask)
         send = remote(h2, h2, C_H2, C_H2, (1, d, r))
         send.start()
-        zero_rest(11)
+        for i in (HALF, HALF + 1, 16):
+            relay_half(i)
+        zero_rest(11, sb)
         send.wait_send()
+        all_sent(wss.at[W_OWN], wx.at[0 : 3 * 128 + 3 * 256])
+        say_ready()
 
         remote(dh, dh, C_DH, C_DH, (0, d, r)).wait_recv()
         upstream(fs.at[1], dh, fs.at[0], g2, b2, mask, 4, 5)
-        sync(2, 4, 2)
+        sync(0, 4, 2)
         s_du, s_dg = both(4), both(5)
         dg[1], dg[9] = s_dg, s_du
         norm_back(d5, 0, fs.at[1], 0, fs.at[0], 0, g2 * inv[1], s_du * (1.0 / total_out), s_dg * (1.0 / total_out))
@@ -1216,7 +1408,7 @@
 
         def first_slopes():
             tx[6], tx[7] = lax.fori_loop(0, 14, slopes, zero_stats)
-            sync(3, 6, 2)
+            sync(1, 6, 2)
             dg[0], dg[8] = both(7), both(6)
 
         def first_back():
@@ -1254,28 +1446,33 @@
             share_out(3)
 
         def compute(t):
-            @pl.when(t < 9)
-            def _():
-                wh[rows(at_row(t), 512), :] = tn(pt[t], d5[...]).astype(BF16)
-
-            @pl.when(t >= 9)
-            def _():
-                block = tn(wx[rows((t - 9) * 1568, 1568), :], u1[0:1568, :])
+            taps = (t < 7) | (t >= 9)
+
+            @pl.when(taps)
+            def _():
+                tap = jnp.where(t < 7, t, t - 2)
+                wh[rows(at_row(t), 512), :] = tn(pt[tap], d5[...]).astype(BF16)
+
+            @pl.when(jnp.logical_not(taps))
+            def _():
+                block = tn(wx[rows((t - 7) * 1568, 1568), :], u1[0:1568, :])
                 wh[rows(at_row(t), 512), :] = block.astype(BF16)
 
         def at_row(t):
-            return jnp.where(t < 2, 5632 + t * 512, t * 512)
+            return jnp.where(t < 2, 5632 + t * 512, jnp.where(t < 9, t * 512, 2048 + t * 512))
 
         sum_gradients(
-            11, compute, at_row, lambda t: lax.rem(t + 2, 11), False, 3136,
+            9, compute, at_row, lambda t: jnp.where(t < 7, t + 2, jnp.where(t < 9, t - 7, t)), False, Z1_ZERO,
             {
-                2: back_conv,
-                3: first_slopes,
-                4: back_and_share,
-                5: lambda: share_out(1),
-                6: lambda: share_out(2),
-                7: lambda: share(r0, 0, 0),
+                2 * SUBS: back_conv,
+                3 * SUBS: first_slopes,
+                4 * SUBS: back_and_share,
+                5 * SUBS: lambda: share_out(1),
+                6 * SUBS: lambda: share_out(2),
+                7 * SUBS: lambda: share(r0, 0, 0),
+                LAST_TURN + 9 * SUBS: final_part,
             },
+            lend=(2, 3), helper=2, helper_turn=lambda t: t - 5,
         )
         for k in (1, 2, 3):
             share_copy(k).wait_send()
@@ -1283,7 +1480,7 @@
     @pl.when(p == 1)
     def _():
         mask = mask_of(1)
-        gate_col = meta[:, 4:5]
+        gate_v = per_row(lambda m: gates[m]).astype(F32)
         cotb[PIX_OUT] = jnp.zeros((8, C_OUT), BF16)
         clear_patch_pad()
         load_weights(plain, 48, 0, 16, put_wide(wh, 0, 512, 0))
@@ -1295,6 +1492,30 @@
             f0[pl.ds(PP + a * 7, 7)] = v[:, :, 512:1024]
             return carry
 
+        other_z = 2 * (1 - lax.rem(r, 2))
+        this_z = 2 * lax.rem(r, 2)
+
+        def pass_own(i):
+            piece_copy(W_OWN, i, quarter, (1, d, r)).wait_recv()
+            piece_copy(W_PEER, i, quarter, peer).start()
+            piece_copy(W_Z, i, quarter, z_dev).start()
+
+        def pass_on(i):
+            piece_copy(W_Z, i, other_z + d, peer).wait_recv()
+            piece_copy(W_ON, i, other_z + d, peer).start()
+
+        def have(i):
+            piece_copy(W_PEER, i, this_z + 1 - d, peer).wait_recv()
+            piece_copy(W_ON, i, other_z + 1 - d, peer).wait_recv()
+
+        def pass_half(i):
+            half_copy(W_OWN, i, d, (1, d, r)).wait_recv()
+            half_copy(W_PEER, i, d, peer).start()
+
+        def have_half(i):
+            half_copy(W_PEER, i, 1 - d, peer).wait_recv()
+
+        pass_own(0)
         over_images(shorten, 0)
         f0[PIX_OUT] = jnp.zeros((8, BLK), F32)
         f0[PP + PIX_OUT] = jnp.zeros((8, BLK), F32)
@@ -1304,61 +1525,42 @@
             z = nn(sx[0:RW, :], wh[rows(2048 + n * 1024, 512), :]) + nn(
                 sx[RW : 2 * RW, :], wh[rows(2560 + n * 1024, 512), :]
             )
-            store_z(f1, n * PP, z, 8 + n, 12 + n)
-            return carry
-
+            store_z(f1, n * PP, z, 4 * n + 2, 4 * n + 3)
+            return carry
+
+        pass_own(1)
         lax.fori_loop(0, 4, shortcut, 0)
 
-        other_z = 2 * (1 - lax.rem(r, 2))
-        this_z = 2 * lax.rem(r, 2)
-
-        def piece(i, q):
-            return wx.at[rows(i * 512 + q * 128, 128)]
-
-        def piece_copy(kind, i, q, device):
-            part = piece(i, q)
-            return pltpu.make_async_remote_copy(
-                src_ref=part, dst_ref=part, send_sem=wss.at[kind, i], recv_sem=wrs.at[kind, i],
-                device_id=device, device_id_type=MESH,
-            )
-
-        def pass_own(i):
-            piece_copy(W_OWN, i, quarter, (1, d, r)).wait_recv()
-            piece_copy(W_PEER, i, quarter, peer).start()
-            piece_copy(W_Z, i, quarter, z_dev).start()
-
-        def pass_on(i):
-            piece_copy(W_Z, i, other_z + d, peer).wait_recv()
-            piece_copy(W_ON, i, other_z + d, peer).start()
-
-        def have(i):
-            piece_copy(W_PEER, i, this_z + 1 - d, peer).wait_recv()
-            piece_copy(W_ON, i, other_z + 1 - d, peer).wait_recv()
-
-        def each(work, first, last):
-            def body(i, carry):
-                work(i)
-                return carry
-
-            lax.fori_loop(first, last, body, 0)
-
-        zero_rest(12)
-        each(pass_own, 0, 7)
-        each(pass_on, 0, 4)
+        pass_own(2)
+        pass_own(VIA)
+        pass_on(0)
+        pass_own(3)
+        pass_on(1)
+        pass_own(VIA + 1)
+        pass_own(4)
+        pl.semaphore_signal(go, inc=1, device_id=(3, d, r), device_id_type=MESH)
+        pass_on(2)
+        pass_own(VIA + 2)
+        pass_own(5)
+        pass_on(VIA)
+        pass_own(6)
+        pass_on(3)
+        pass_own(7)
+        pass_on(VIA + 1)
         remote(h2, h2, C_H2, C_H2, (1, d, r)).wait_recv()
 
         def third_conv(n, carry):
-            store_z(f0, n * PP, nn(h2[...], wh[rows(n * 512, 512), :]), n, 4 + n)
+            store_z(f0, n * PP, nn(h2[...], wh[rows(n * 512, 512), :]), 4 * n, 4 * n + 1)
+            exchange_of(E_WIDE + n, 4 * n, 4).start()
             return carry
 
         lax.fori_loop(0, 4, third_conv, 0)
-        sync(0, 0, 16)
-        pass_own(7)
         pass_on(4)
 
         def join(n, carry):
-            c3, s3 = moments(n, 4 + n, total_out, 2 + n)
-            cp, sp = moments(8 + n, 12 + n, total_out, 6 + n)
+            exchange_of(E_WIDE + n, 4 * n, 4).wait()
+            c3, s3 = moments(4 * n, 4 * n + 1, total_out, 2 + n)
+            cp, sp = moments(4 * n + 2, 4 * n + 3, total_out, 6 + n)
             g3, gp, b = par[n], par[4 + n], par[8 + n] + par[12 + n]
 
             def body(_, i, carry):
@@ -1376,15 +1578,18 @@
             return carry
 
         lax.fori_loop(0, 4, join, 0)
-        pass_own(8)
-        pass_on(5)
+        for n in (1, 2, 3):
+            o1_copy(n, 3).start()
+        pass_half(13)
+        pass_on(VIA + 2)
+        pass_half(HALF)
         each(have, 0, 4)
         zhat4, zhat5 = fs.at[0], fs.at[1]
         z = nn(u0[0:RW, :], wx[0:512, :])
         for n in range(1, 4):
             z += nn(u0[n * RW : (n + 1) * RW, :], wx[n * 512 : (n + 1) * 512, :])
         store_z(zhat4, 0, z, 16, 17)
-        sync(1, 16, 2)
+        sync(0, 16, 2)
         remote(parx.at[0:4], parx.at[0:4], C_PAR2, C_PAR2, (1, d, r)).wait_recv()
         center, scale = moments(16, 17, total_out, 10)
         g4, g5, b4, b5 = parx[0], parx[1], parx[2], parx[3]
@@ -1403,56 +1608,51 @@
         h4_send = remote(h4, h4, C_H4, C_H4, (2, d, r))
         h4_send.start()
 
-        def o1_copy(n):
-            part = u0.at[n * RW : (n + 1) * RW]
-            return remote(part, part, C_O1 + n, C_O1 + n, (2, d, r))
-
-        o1_copy(0).start()
-        o1_copy(1).start()
+        o1_copy(0, 2).start()
+        pass_on(5)
         build_patches(plain_base)
-        each(pass_own, 9, 11)
-        pl.semaphore_signal(go, inc=1, device_id=(3, d, r), device_id_type=MESH)
+        pass_half(14)
         pass_on(6)
-        pass_own(11)
+        pass_half(HALF + 1)
         pass_on(7)
-        pass_own(12)
-        pass_on(8)
         zhat5[...] = jnp.zeros_like(zhat5)
 
         def fifth_conv(t, carry):
-            @pl.when(t >= 5)
-            def _():
-                pass_on(4 + t)
-
-            have(4 + t)
+            @pl.when(t < HALF - 4)
+            def _():
+                have(4 + t)
+
+            @pl.when(t >= HALF - 4)
+            def _():
+                have_half(4 + t)
+
             z = nn(pt[t], wx[rows(2048 + t * 512, 512), :])
             zhat5[...] += z.reshape(PP, 8, BLK)
             return carry
 
         lax.fori_loop(0, 9, fifth_conv, 0)
-        each(pass_own, 13, 17)
+        pass_half(15)
         stats_of_map(zhat5, 18, 19)
-        sync(2, 18, 2)
+        sync(1, 18, 2)
         center, scale = moments(18, 19, total_out, 11)
         act_to(zhat5, h5, center, scale, g5, b5, mask)
-        h5_send = remote(h5, h5, C_H5, C_H5, (3, d, r))
-        h5_send.start()
-        each(pass_on, 13, 17)
+
+        pass_half(16)
 
         def sixth_conv(n, carry):
-            have(13 + n)
-            store_z(f2, n * PP, nn(h5[...], wx[rows(6656 + n * 512, 512), :]), 20 + n, 24 + n)
+            have_half(13 + n)
+            store_z(f2, n * PP, nn(h5[...], wx[rows(6656 + n * 512, 512), :]), 20 + 2 * n, 21 + 2 * n)
+            exchange_of(E_WIDE_NEXT + n, 20 + 2 * n, 2).start()
             return carry
 
         lax.fori_loop(0, 4, sixth_conv, 0)
-        sync(3, 20, 8)
         remote(parx.at[4:12], parx.at[4:12], C_PAR3, C_PAR3, (1, d, r)).wait_recv()
         pltpu.make_async_copy(cot, cotb.at[0:PIX_OUT], ls.at[16]).wait()
 
         def finish(n, carry):
-            center, scale = moments(20 + n, 24 + n, total_out, 12 + n)
+            exchange_of(E_WIDE_NEXT + n, 20 + 2 * n, 2).wait()
+            center, scale = moments(20 + 2 * n, 21 + 2 * n, total_out, 12 + n)
             g6, b6 = parx[4 + n], parx[8 + n]
-            gate_v = jnp.broadcast_to(gate_col, (8, BLK))
 
             def body(c, i, carry):
                 part = pl.ds(n * PP + i * 10, 10)
@@ -1461,7 +1661,7 @@
                 f2[part] = zhat
                 o = u0[part_rows, :].astype(F32).reshape(10, 8, BLK)
                 q = o + zhat * g6 + b6
-                s = jax.nn.sigmoid(q)
+                s = sigmoid(q)
                 merged = gate_v * (q * s) + (1.0 - gate_v) * o
                 pt[n, rows(i * 80, 80), :] = merged.reshape(80, BLK).astype(BF16)
                 ct = cotb[c, :, pl.ds(pl.multiple_of(n * BLK, BLK), BLK)].astype(F32)
@@ -1471,31 +1671,30 @@
                 u2[part_rows, :] = dres.reshape(80, BLK).astype(BF16)
                 return add_stats(carry, dq, dq * zhat)
 
-            tx[28 + n], tx[32 + n] = five(body, zero_stats)
+            tx[28 + 2 * n], tx[29 + 2 * n] = five(body, zero_stats)
+            exchange_of(E_WIDE + n, 28 + 2 * n, 2).start()
             return carry
 
         lax.fori_loop(0, 4, finish, 0)
         ob[...] = pt[1]
 
-        sync(4, 28, 8)
 
         def sixth_back(n, carry):
-            s_du, s_dg = both(28 + n), both(32 + n)
+            exchange_of(E_WIDE + n, 28 + 2 * n, 2).wait()
+            s_du, s_dg = both(28 + 2 * n), both(29 + 2 * n)
             dgx[4 + n] = s_dg
             dgx[8 + n] = s_du
             norm_back(u1, n * RW, f3, n * PP, f2, n * PP, parx[4 + n] * inv[12 + n], s_du * (1.0 / total_out), s_dg * (1.0 / total_out))
             return carry
 
         lax.fori_loop(0, 4, sixth_back, 0)
-        z6_send = remote(u1, u1, C_Z6, C_Z6, (3, d, r))
-        z6_send.start()
         grad = nt(u1[0:RW, :], wx[6656:7168, :])
         for n in range(1, 4):
             grad += nt(u1[n * RW : (n + 1) * RW, :], wx[6656 + n * 512 : 7168 + n * 512, :])
         dh[...] = grad.astype(BF16)
 
         upstream(f2, dh, zhat5, g5, b5, mask, 36, 37)
-        sync(5, 36, 2)
+        sync(0, 36, 2)
         s_du, s_dg = both(36), both(37)
         dgx[1] = s_dg
         dgx[3] = s_du
@@ -1512,7 +1711,7 @@
             return add_stats(carry, du, du * zhat)
 
         tx[38], tx[39] = lax.fori_loop(0, 7, fourth_slopes, zero_stats)
-        sync(6, 38, 2)
+        sync(1, 38, 2)
         s_du, s_dg = both(38), both(39)
         dgx[0] = s_dg
         dgx[2] = s_du
@@ -1531,14 +1730,17 @@
                 s0, s1, s2 = carry
                 return s0 + jnp.sum(dp, axis=0), s1 + jnp.sum(dp * a, axis=0), s2 + jnp.sum(dp * b_, axis=0)
 
-            tx[40 + n], tx[44 + n], tx[48 + n] = five(body, zero_stats + zero_stats[:1])
+            first = 40 + 3 * n
+            tx[first], tx[first + 1], tx[first + 2] = five(body, zero_stats + zero_stats[:1])
+            exchange_of(E_WIDE_NEXT + n, first, 3).start()
             return carry
 
         lax.fori_loop(0, 4, first_block_slopes, 0)
-        sync(7, 40, 12)
 
         def third_back(n, carry):
-            s_du, s_d3, s_dp = both(40 + n), both(44 + n), both(48 + n)
+            first = 40 + 3 * n
+            exchange_of(E_WIDE_NEXT + n, first, 3).wait()
+            s_du, s_d3, s_dp = both(first), both(first + 1), both(first + 2)
             dg[n] = s_d3
             dg[4 + n] = s_dp
             dg[8 + n] = s_du
@@ -1556,27 +1758,22 @@
         dh_send = remote(dh, dh, C_DH, C_DH, (0, d, r))
         dh_send.start()
 
-        d4_send = remote(d4, d4, C_D4, C_D4, (2, d, r))
-        d4_send.start()
-        def drain_pieces(i, carry):
-            piece_copy(W_PEER, i, quarter, peer).wait_send()
-            piece_copy(W_Z, i, quarter, z_dev).wait_send()
-            piece_copy(W_ON, i, other_z + d, peer).wait_send()
-            return carry
-
-        lax.fori_loop(0, N_PIECE, drain_pieces, 0)
+        all_sent(wss.at[W_PEER], wx.at[0 : HALF * 128 + 6 * 256])
+        all_sent(wss.at[W_Z], wx.at[0 : HALF * 128])
+        all_sent(wss.at[W_ON], wx.at[0 : HALF * 128])
         say_ready()
-        o1_copy(2).start()
-        o1_copy(3).start()
-        sends = [d4_send, dh_send, d5_send, h5_send, z6_send] + [o1_copy(n) for n in range(4)]
+
+        late = [remote(d4, d4, C_D4, C_D4, (2, d, r))]
         for first, last, sem, chip in ((0, 4, C_DG2, 2), (4, 12, C_DG3, 3)):
-            copy = remote(dgx.at[first:last], dgx.at[first:last], sem, sem, (chip, d, r))
-            copy.start()
-            sends.append(copy)
-        for slot, k in enumerate((0, 2, 3)):
-            copy = remote(pt.at[k], ob, C_SHARE + slot, C_SHARE, (k, d, r))
-            copy.start()
-            sends.append(copy)
+            late.append(remote(dgx.at[first:last], dgx.at[first:last], sem, sem, (chip, d, r)))
+        later = [
+            remote(pt.at[k], ob, C_SHARE + slot, C_SHARE, (k, d, r)) for slot, k in enumerate((0, 2, 3))
+        ]
+
+        def late_sends():
+            dh_send.wait_send()
+            for copy in late:
+                copy.start()
 
         def shortcut_share(k):
             g = nt(u2[0:RW, :], wh[2048 + k * 256 : 2304 + k * 256, :])
@@ -1590,12 +1787,20 @@
             place, k = places[slot]
             return remote(place, r1, C_GP + slot, C_GP, (k, d, r))
 
-        def shortcut_shares():
-            h4_send.wait_send()
-            for slot, (place, k) in enumerate(places):
-                place[...] = shortcut_share(k)
+        def shortcut_shares(slot):
+            place, k = places[slot]
+            if slot == 0:
+                h4_send.wait_send()
+            place[...] = shortcut_share(k)
+
+        def shortcut_own():
+            r1[...] = shortcut_share(1)
+
+        def late_shares():
+            for copy in later:
+                copy.start()
+            for slot in range(3):
                 share_copy(slot).start()
-            r1[...] = shortcut_share(1)
 
         def compute(t):
             @pl.when(t < 4)
@@ -1604,15 +1809,34 @@
                 for n in range(4):
                     put_chunk(t, n, tn(left, pt[4 + n]))
 
-            @pl.when(t >= 4)
+            @pl.when((t >= 4) & (t < 12))
             def _():
                 m = t - 4
                 left = sx[rows((m // 4) * RW, RW), pl.ds(pl.multiple_of(lax.rem(m, 4) * 128, 128), 128)]
                 for n in range(4):
                     put_chunk(t, n, tn(left, u2[n * RW : (n + 1) * RW, :]))
 
-        sum_gradients(12, compute, lambda t: t * 512, lambda t: t, True, 0, {1: shortcut_shares})
-        for copy in sends:
+            @pl.when(t >= 12)
+            def _():
+                left = h5[:, pl.ds(pl.multiple_of((t - 12) * 128, 128), 128)]
+                for n in range(4):
+                    put_chunk(t, n, tn(left, u1[n * RW : (n + 1) * RW, :]))
+
+        zero_rest(12, sb)
+        sum_gradients(
+            12, compute, lambda t: t * 512, lambda t: t, True, 0,
+            {
+                2: lambda: shortcut_shares(0),
+                4: lambda: shortcut_shares(1),
+                6: lambda: shortcut_shares(2),
+                7: late_sends,
+                8: shortcut_own,
+                10: late_shares,
+                LAST_TURN + 12 * SUBS: final_part,
+            },
+            passed=(3, 5, 7, 9), helper=3, helper_turn=lambda t: t - 7,
+        )
+        for copy in [d5_send, o1_copy(0, 2)] + [o1_copy(n, 3) for n in (1, 2, 3)] + late + later:
             copy.wait_send()
         for slot in range(3):
             share_copy(slot).wait_send()
@@ -1625,28 +1849,30 @@
         par_send = remote(parx.at[0:4], parx.at[0:4], C_PAR2, C_PAR2, (1, d, r))
         par_send.start()
 
-        def piece_copy(i):
-            part = wx.at[rows(i * 512 + quarter * 128, 128)]
-            return pltpu.make_async_remote_copy(
-                src_ref=part, dst_ref=part, send_sem=wss.at[W_OWN, i], recv_sem=wrs.at[W_OWN, i],
-                device_id=(1, d, r), device_id_type=MESH,
-            )
-
-        put_w = put_narrow(wx, lambda i: i * 512 + quarter * 128)
+        put_w = put_narrow(wx, lambda i: own_parts(i) * 128)
 
         def put(i):
             put_w(i)
-            piece_copy(i).start()
-
-        load_weights(every_fourth, 13, 0, 13, put)
+
+            @pl.when(i < VIA)
+            def _():
+                piece_copy(W_OWN, i, quarter, (1, d, r)).start()
+
+            @pl.when((i >= VIA) & (i < HALF))
+            def _():
+                piece_copy(W_VIA, i, quarter, (0, d, r)).start()
+
+            for k in range(HALF, 13):
+                @pl.when(i == HALF + 2 * (k - HALF) + 1)
+                def _(k=k):
+                    half_copy(W_VIA, k, d, (0, d, r)).start()
+
+        load_weights(own_parts, 15, 0, 15, put)
         pb[...] = jnp.zeros_like(pb)
         clear_patch_pad()
 
-        def drain(i, carry):
-            piece_copy(i).wait_send()
-            return carry
-
-        lax.fori_loop(0, 13, drain, 0)
+        all_sent(wss.at[W_OWN], wx.at[0 : VIA * 128])
+        all_sent(wss.at[W_VIA], wx.at[0 : 3 * 128 + 2 * 256])
         say_ready()
         remote(h4, h4, C_H4, C_H4, (2, d, r)).wait_recv()
         pb[1:8, 1:8] = h4[0:RV, :].astype(F32).reshape(7, 7, 8, BLK)
@@ -1654,27 +1880,34 @@
         remote(d5, d5, C_D5, C_D5, (2, d, r)).wait_recv()
 
         def compute(t):
-            @pl.when(t < 9)
-            def _():
-                wh[rows(t * 512, 512), :] = tn(pt[t], d5[...]).astype(BF16)
-
-            @pl.when(t == 9)
+            taps = (t < 4) | (t >= 10)
+
+            @pl.when(taps)
+            def _():
+                tap = jnp.where(t < 4, t + 5, t - 10)
+                wh[rows(t * 512, 512), :] = tn(pt[tap], d5[...]).astype(BF16)
+
+            @pl.when(t == 6)
             def _():
                 remote(d4, d4, C_D4, C_D4, (2, d, r)).wait_recv()
                 for n in range(4):
-                    part = u0.at[n * RW : (n + 1) * RW]
-                    remote(part, part, C_O1 + n, C_O1 + n, (2, d, r)).wait_recv()
-
-            @pl.when(t >= 9)
-            def _():
-                wh[rows(t * 512, 512), :] = tn(u0[rows((t - 9) * RW, RW), :], d4[...]).astype(BF16)
+                    o1_copy(n, 2).wait_recv()
+
+            @pl.when(jnp.logical_not(taps))
+            def _():
+                wh[rows(t * 512, 512), :] = tn(u0[rows((t - 6) * RW, RW), :], d4[...]).astype(BF16)
 
         def norm_grads():
             remote(dgx.at[0:4], dgx.at[0:4], C_DG2, C_DG2, (2, d, r)).wait_recv()
             dg[0], dg[1], dg[8], dg[9] = dgx[0], dgx[1], dgx[2], dgx[3]
 
         sum_gradients(
-            13, compute, lambda t: t * 512, lambda t: lax.rem(t + 4, 13), False, 0, {10: norm_grads}
+            10, compute, lambda t: t * 512, lambda t: jnp.where(t < 4, t + 9, t - 6), False, 0,
+            {7 * SUBS: norm_grads, LAST_TURN + 10 * SUBS: final_part},
+            lend=(2, 3, 4, 5, 6), helper=3, helper_turn=lambda t: t - 10,
+            handed_in=lambda t: (t >= 4) & (t < 6),
+            lent_by=(lambda t: (t >= 4) & (t < 6), lambda t: 0, lambda t: t + 5, 2),
+            computed=(0, 8), packed_here=(0, 8),
         )
         par_send.wait_send()
 
@@ -1690,89 +1923,118 @@
         def put(i):
             for n in range(4):
                 for j in range(4):
-                    wx[rows(6656 + n * 512 + quarter * 128 + i * 32, 32), j * 128 : (j + 1) * 128] = st[
+                    wx[rows(6656 + n * 512 + d * 256 + i * 32, 32), j * 128 : (j + 1) * 128] = st[
                         pl.ds(4 * n + j, 32, stride=16), :
                     ].astype(BF16)
 
-        load_weights(four_rows, 4, 0, 4, put)
-        zero_rest(4)
+        load_weights(half_rows, 8, 0, 8, put)
+        zero_rest(4, sb)
         pl.semaphore_wait(go, 1)
 
-        def piece_copy(n):
-            part = wx.at[rows(6656 + n * 512 + quarter * 128, 128)]
-            return pltpu.make_async_remote_copy(
-                src_ref=part, dst_ref=part, send_sem=wss.at[W_OWN, 13 + n], recv_sem=wrs.at[W_OWN, 13 + n],
-                device_id=(1, d, r), device_id_type=MESH,
-            )
-
-        for n in range(4):
-            piece_copy(n).start()
-        remote(h5, h5, C_H5, C_H5, (3, d, r)).wait_recv()
-        remote(u1, u1, C_Z6, C_Z6, (3, d, r)).wait_recv()
-
-        def compute(t):
-            left = h5[:, pl.ds(pl.multiple_of(t * 128, 128), 128)]
-            for n in range(4):
-                put_chunk(t, n, tn(left, u1[n * RW : (n + 1) * RW, :]))
-
+        half_copy(W_VIA, 16, d, (0, d, r)).start()
+        for i in (13, 14, 15):
+            half_copy(W_OWN, i, d, (1, d, r)).start()
+        for n in (1, 2, 3):
+            o1_copy(n, 3).wait_recv()
+            o1_copy(n, 2).start()
         def norm_grads():
             remote(dgx.at[4:12], dgx.at[4:12], C_DG3, C_DG3, (3, d, r)).wait_recv()
             for k in range(4):
                 dg[k] = dgx[4 + k]
                 dg[8 + k] = dgx[8 + k]
 
-        sum_gradients(4, compute, lambda t: t * 512, lambda t: t, True, 0, {1: norm_grads})
-        for n in range(4):
-            piece_copy(n).wait_send()
+        sum_gradients(
+            9, lambda t: None, lambda t: t * 512, lambda t: t - 5, True, 0,
+            {6 * SUBS: norm_grads, LAST_TURN + 9 * SUBS: final_part},
+            handed_in=lambda t: t >= 0,
+            lent_by=(lambda t: t < 5, lambda t: 2, lambda t: t + 10, 5),
+            computed=(0, 0), packed_here=(5, 4),
+        )
+        for n in (1, 2, 3):
+            o1_copy(n, 2).wait_send()
+        all_sent(wss.at[W_VIA], wx.at[0:256])
+        all_sent(wss.at[W_OWN], wx.at[0 : 3 * 256])
         par_send.wait_send()
 
-    @pl.when(p != 1)
-    def _():
-        remote(ob, ob, C_SHARE, C_SHARE, (p, d, r)).wait_recv()
-        remote(r1, r1, C_GP, C_GP, (p, d, r)).wait_recv()
-
-    @pl.when(p != 0)
-    def _():
-        remote(r0, r0, C_GI, C_GI, (p, d, r)).wait_recv()
-
-    out[...] = ob[0:RV, :].astype(F32).reshape(PIX_OUT, 8, BLK).astype(BF16)
-    f0[0:PP, :, 0:256] = r1[...].astype(F32).reshape(PP, 8, 256)
-
-    def place(a, carry):
-        m = r0[rows(a * 224, 224), :].astype(F32).reshape(28, 8, 256)
-        first = m[0:14].reshape(7, 2, 8, 256)
-        even = first[:, 0] + f0[pl.ds(a * 7, 7), :, 0:256]
-        f3[pl.ds(a * 28, 14), :, 0:256] = jnp.stack([even, first[:, 1]], axis=1).reshape(14, 8, 256)
-        f3[pl.ds(a * 28 + 14, 14), :, 0:256] = m[14:28]
-        return carry
-
-    lax.fori_loop(0, 7, place, 0)
-    gi_copy = pltpu.make_async_copy(f3.at[0:PIX_IN, :, 0:256], gi, ls.at[17])
-    gi_copy.start()
-    gi_copy.wait()
+    gi_copy().wait()
+
+
+def widen_kernel(out_in, gi_in, dw_in, dgb_in, out, gi, dw, gain, bias, v_out, v_gi, v_dw, v_wide, v_dgb, sin, sout):
+    count = v_dw.shape[0] // 2048
+
+    def part(i):
+        return pl.ds(i * 2048, 2048)
+
+    loads = [pltpu.make_async_copy(dw_in.at[part(i)], v_dw.at[part(i)], sin.at[i]) for i in range(count)]
+    others = (
+        (dgb_in, v_dgb, ((v_dgb.at[0:4], gain), (v_dgb.at[4:8], bias))),
+        (out_in, v_out, ((v_out, out),)),
+        (gi_in, v_gi, ((v_gi, gi),)),
+    )
+    more = [pltpu.make_async_copy(a, b, sin.at[count + k]) for k, (a, b, _) in enumerate(others)]
+    for copy in loads + more:
+        copy.start()
+    stores = []
+    for i in range(count):
+        loads[i].wait()
+        v_wide[part(i)] = v_dw[part(i)].astype(F32)
+        stores.append(pltpu.make_async_copy(v_wide.at[part(i)], dw.at[part(i)], sout.at[i]))
+        stores[-1].start()
+    for k, (_, _, ends) in enumerate(others):
+        more[k].wait()
+        for a, b in ends:
+            stores.append(pltpu.make_async_copy(a, b, sout.at[len(stores)]))
+            stores[-1].start()
+    for copy in stores:
+        copy.wait()
+
+
+def widen(out, gi, dw, dgb):
+    count = P_SIZE // 128 // 2048
+    any_space = pl.BlockSpec(memory_space=pl.ANY)
+    return pl.pallas_call(
+        widen_kernel,
+        out_shape=(
+            jax.ShapeDtypeStruct(out.shape, out.dtype),
+            jax.ShapeDtypeStruct(gi.shape, gi.dtype),
+            jax.ShapeDtypeStruct(dw.shape, F32),
+            jax.ShapeDtypeStruct((4, 4096), F32),
+            jax.ShapeDtypeStruct((4, 4096), F32),
+        ),
+        in_specs=[any_space] * 4,
+        out_specs=(any_space,) * 5,
+        scratch_shapes=[
+            pltpu.VMEM(out.shape, out.dtype),
+            pltpu.VMEM(gi.shape, gi.dtype),
+            pltpu.VMEM(dw.shape, BF16),
+            pltpu.VMEM(dw.shape, F32),
+            pltpu.VMEM(dgb.shape, F32),
+            pltpu.SemaphoreType.DMA((count + 3,)),
+            pltpu.SemaphoreType.DMA((count + 4,)),
+        ],
+        compiler_params=pltpu.CompilerParams(vmem_limit_bytes=64 * 1024 * 1024),
+    )(out, gi, dw, dgb)
 
 
 def one_kernel(images, section_weights, bn_gain, bn_bias, width, bn_set, gate, cotangent):
-    meta = jnp.concatenate(
-        [width.astype(F32), bn_set.astype(F32), gate.astype(F32)[:, None], jnp.zeros((MB, 123), F32)], axis=1
-    )
     any_space = pl.BlockSpec(memory_space=pl.ANY)
     vmem = pl.BlockSpec(memory_space=pltpu.VMEM)
+    smem = pl.BlockSpec(memory_space=pltpu.SMEM)
     out, gi, dw, dgb = pl.pallas_call(
         whole_kernel,
         out_shape=(
             jax.ShapeDtypeStruct((PIX_OUT, 8, BLK), BF16),
             jax.ShapeDtypeStruct((PIX_IN, 8, 256), F32),
-            jax.ShapeDtypeStruct((P_SIZE // 128, 128), BF16),
+            jax.ShapeDtypeStruct((P_SIZE // SUB, 512, 128), BF16),
             jax.ShapeDtypeStruct((8, 4096), F32),
         ),
-        in_specs=[any_space, any_space, vmem, vmem, vmem, any_space],
+        in_specs=[any_space, any_space, vmem, vmem, smem, smem, smem, any_space],
         out_specs=(vmem, any_space, any_space, vmem),
         scratch_shapes=[
             pltpu.VMEM((4, 28, 8, 1024), BF16),
             pltpu.VMEM((RING, 1, SUB), BF16),
-            pltpu.VMEM((1024, 128), F32),
-            pltpu.VMEM((6656, BLK), BF16),
+            pltpu.VMEM((512, 128), F32),
+            pltpu.VMEM((8192, BLK), BF16),
             pltpu.VMEM((8768, BLK), BF16),
             pltpu.VMEM((4 * PP, 8, BLK), F32),
             pltpu.VMEM((4 * PP, 8, BLK), F32),
@@ -1802,17 +2064,17 @@
             pltpu.VMEM((12, 8, BLK), F32),
             pltpu.VMEM((16, 8, BLK), F32),
             pltpu.VMEM((12, 8, BLK), F32),
-            pltpu.VMEM((4, 1024, 128), BF16),
-            pltpu.VMEM((3328, BLK), BF16),
+            pltpu.VMEM((4, 512, 128), BF16),
+            pltpu.VMEM((4096, BLK), BF16),
             pltpu.VMEM((2, 8, 4096), F32),
             pltpu.VMEM((8, 4096), F32),
-            pltpu.SemaphoreType.DMA((18,)),
+            pltpu.SemaphoreType.DMA((19,)),
             pltpu.SemaphoreType.DMA((N_SEM,)),
             pltpu.SemaphoreType.DMA((N_SEM,)),
-            pltpu.SemaphoreType.DMA((4, N_PIECE)),
-            pltpu.SemaphoreType.DMA((4, N_PIECE)),
-            pltpu.SemaphoreType.DMA((5, 13)),
-            pltpu.SemaphoreType.DMA((5, 13)),
+            pltpu.SemaphoreType.DMA((5,)),
+            pltpu.SemaphoreType.DMA((62,)),
+            pltpu.SemaphoreType.DMA((N_SUM_SEND,)),
+            pltpu.SemaphoreType.DMA((N_SUM_RECV,)),
             pltpu.SemaphoreType.REGULAR((2,)),
             pltpu.SemaphoreType.REGULAR,
         ],
@@ -1824,16 +2086,18 @@
         section_weights,
         bn_gain[0],
         bn_bias[0],
-        meta,
+        width.T,
+        bn_set.T,
+        gate,
         jnp.transpose(cotangent, (1, 0, 2)),
     )
-    dw = dw.astype(F32).reshape(1, P_SIZE)
+    out, gi, dw, gain_sum, bias_sum = widen(out, gi, dw.reshape(P_SIZE // 128, 128), dgb)
     return (
         jnp.transpose(out, (1, 0, 2)),
         jnp.transpose(gi, (1, 0, 2)),
-        dw,
-        dgb[None, :4],
-        dgb[None, 4:],
+        dw.reshape(1, P_SIZE),
+        gain_sum[None],
+        bias_sum[None],
     )
 
 

time: 217 us -> 176 us (0.81); the launches traced: 213 us -> 176 us
  Pallas kernels: 197 us -> 175 us
  other arithmetic: 9.74 us -> 0 us
  local copies, waits for them, and re-layouts: 5.23 us -> 0 us
    pallas_call x1, Pallas kernels: 197 us -> 166 us  [one_kernel(): pl.pallas_call(whole_kernel, out_shape=(jax.ShapeDtypeStruct((PIX_OUT, 8,...]
    pallas_call x0 -> x1, Pallas kernels: none -> 8.68 us  [widen(): pl.pallas_call(widen_kernel, out_shape=(jax.ShapeDtypeStruct(out.shape, o...]
    reshape x1 -> x0, other arithmetic: 8.4 us -> none  [one_kernel(): dw = dw.astype(F32).reshape(1, P_SIZE)]
    unnamed x8 -> x0, local copies, waits for them, and re-layouts: 3.41 us -> none
where the time goes in v3:
time: 176 us
  Pallas kernels  175 us (99%)
    pallas_call x1, Pallas kernels, one_kernel(): pl.pallas_call(whole_kernel, out_shape=(jax.ShapeDtypeStruct((PIX_OUT, 8,...  166 us
    pallas_call x1, Pallas kernels, widen(): pl.pallas_call(widen_kernel, out_shape=(jax.ShapeDtypeStruct(out.shape, o...  8.68 us

profile of v3, /device:TPU:5, one launch (start us, length us, event | category | flops | bytes accessed | tf_op | source)
XLA Modules:
  0.0 175.5 jit_solution(14903219277113998209)
XLA Ops:
  0.6 166.0 %shard_map.119 = (bf16[49,8,512]{2,1,0:T(8,128)(2,1)}, f32[196,8,256]{2,1,0:T(8,128)}, bf16[52,512,128]{2,1,0:T(8,128)(2,1)}, f32[8,4096]{1,0:T(8,128)}) custom-call(bf16[196,8,1024]{2,1,0:T(8,128)(2,1)} %bitcast.13, bf16[1,3407872]{1,0:T(2,128)(2,1)} %wts.1, f32[4,4096]{1,0:T(4,128)} %bitcast.15, f32[4,4096]{1,0:T(4,128)} %bitcast.16, s32[2,8]{1,0:T(2,128)} %bitcast.17, ...), custom_call_target="tpu_custom_call" | custom-call | tf_op jit(solution)/shard_map/pallas_call | solution.py:2023
  166.7 8.7 %shard_map.120 = (bf16[49,8,512]{2,1,0:T(8,128)(2,1)}, f32[196,8,256]{2,1,0:T(8,128)}, f32[26624,128]{1,0:T(8,128)}, f32[4,4096]{1,0:T(4,128)}, f32[4,4096]{1,0:T(4,128)}) custom-call(bf16[49,8,512]{2,1,0:T(8,128)(2,1)} %get-tuple-element.14.out_in, f32[196,8,256]{2,1,0:T(8,128)} %get-tuple-element.15.gi_in, bf16[26624,128]{1,0:T(8,128)(2,1)} %bitcast.12, ...), custom_call_target="tpu_custom_call" | custom-call | tf_op jit(solution)/shard_map/pallas_call | solution.py:1995

commit v4 on v3

--- a/solution.py
+++ b/solution.py
@@ -647,15 +647,15 @@
 E_WIDE, E_WIDE_NEXT = 2, 6
 C_H2, C_H4, C_D5, C_D4, C_DH = range(10, 15)
 C_O1, C_SHARE, C_GI, C_GP = 15, 19, 22, 25
-C_PAR2, C_PAR3, C_DG2, C_DG3, C_BN1, C_BN2, C_BN3 = range(28, 35)
-N_SEM = 35
+C_PAR2, C_PAR3, C_DG2, C_DG3, C_BN1, C_BN2, C_BN3, C_BN4 = range(28, 36)
+N_SEM = 36
 N_PIECE = 17
 W_OWN, W_PEER, W_Z, W_ON, W_VIA = range(5)
 VIA, HALF = 8, 11
 W_BASE = (0, 17, 34, 45, 56 - VIA)
 S_CORE, S_IN, S_OUT, S_HAND, S_BACK, S_DONE, S_ACROSS, N_SUM_SEND = 0, 1, 2, 3, 4, 5, 9, 17
 R_CORE, R_IN, R_ACROSS, R_OUT, R_GIVE = (0, 8), (8, 12), (20, 8), (28, 12), (40, 4)
-R_DONE, R_BACK, R_HAND, N_SUM_RECV = 44, 45, 46, 64
+R_DONE, R_BACK, R_HAND, N_SUM_RECV = 44, 45, 46, 66
 RING = 8
 SUBS = 2
 SUB_ROWS = 256 // SUBS
@@ -681,14 +681,14 @@
 
 
 def rows(start, size):
-    return pl.ds(pl.multiple_of(start, 16), size)
+    return pl.ds(start if isinstance(start, int) else pl.multiple_of(start, 16), size)
 
 
 def whole_kernel(
     img, wts, gain, bias, width, sets, gates, cot,
-    out, gi, dw, dgb,
+    out, gi, dw, dgb_out,
     imgb, raw, st, wh, wx, f0, f1, f2, f3, fs, pb, pt, u0, u1, u2, sx, cotb,
-    h2, h4, h5, d5, d4, dh, r0, r1, ob, tx, rx, inv, par, parx, dg, dgx, sb, rd, bz, dgs,
+    h2, h4, h5, d5, d4, dh, r0, r1, ob, tx, rx, inv, par, parx, dg, dgx, sb, rd, bz, dgs, dgb, v_out,
     ls, ss, rs, wss, wrs, ass, ars, ready, go,
 ):
     p, d, r = lax.axis_index("pipe"), lax.axis_index("dp"), lax.axis_index("rep")
@@ -726,7 +726,7 @@
 
     def slope(v):
         s = sigmoid(v)
-        return s * (1.0 + v * (1.0 - s))
+        return s + v * s * (1.0 - s)
 
     def clear_pad(ref, first):
         tile = ref[rows(first + RW - 16, 16), :].astype(F32)
@@ -744,7 +744,11 @@
         lane = lax.broadcasted_iota(jnp.int32, (8, BLK), 1)
         return (lane < per_row(lambda m: width[block, m])).astype(F32)
 
-    def five(body, init=0):
+    def five(body, init=0, unrolled=False):
+        if unrolled:
+            for c in range(5):
+                init = body(pl.ds(c * 10, 10), c, init)
+            return init
         return lax.fori_loop(0, 5, lambda c, carry: body(pl.ds(c * 10, 10), c, carry), init)
 
     def add_stats(carry, a, b):
@@ -802,10 +806,10 @@
 
         return put
 
-    def put_chunk(t, n, block):
+    def put_chunk(row, n, block):
         size = SUB_ROWS // 4
         for part in range(2 * SUBS):
-            wh[rows(t * 512 + part * SUB_ROWS + n * size, size), :] = block[part * size : (part + 1) * size].astype(BF16)
+            wh[rows(row + part * SUB_ROWS + n * size, size), :] = block[part * size : (part + 1) * size].astype(BF16)
 
     def plain(turn):
         return turn
@@ -905,14 +909,19 @@
                 dgs[k : k + 1, cols] = jnp.sum(dg[n] * hot, axis=0, keepdims=True)
                 dgs[4 + k : 5 + k, cols] = jnp.sum(dg[8 + n] * hot, axis=0, keepdims=True)
 
+    norm_half = pl.ds(pl.multiple_of(d * 2048, 2048), 2048)
+
     def bn_in():
-        return remote(dgs, bz.at[0], C_BN1, C_BN1, z_dev)
+        return remote(dgs.at[:, norm_half], bz.at[0, :, norm_half], C_BN1, C_BN1, z_dev)
 
     def bn_across():
-        return remote(dgs, bz.at[1], C_BN2, C_BN2, across)
+        return remote(dgs.at[:, norm_half], bz.at[1, :, norm_half], C_BN2, C_BN2, across)
 
     def bn_out():
-        return remote(dgb, bz.at[0], C_BN3, C_BN3, z_dev)
+        return remote(dgb.at[:, norm_half], bz.at[0, :, norm_half], C_BN3, C_BN3, z_dev)
+
+    def bn_core():
+        return remote(dgb.at[:, norm_half], dgb.at[:, norm_half], C_BN4, C_BN4, peer)
 
     def say_ready():
         pl.semaphore_signal(ready.at[0], inc=1, device_id=z_dev, device_id_type=MESH)
@@ -924,6 +933,7 @@
     def sum_gradients(
         count, compute, at_row, chunk_of, wide, z1, extra,
         lend=(), passed=(), helper=0, helper_turn=None, handed_in=None, lent_by=None, computed=None, packed_here=None,
+        norms_at=0,
     ):
         turns = SUBS * count
         last_lent = SUBS * (count + len(lend))
@@ -1040,6 +1050,11 @@
                 add(u, from_core(u))
                 hand(u).start()
 
+        def unit_rows(units):
+            return wh.at[0 : units * SUB_ROWS]
+
+        take_at = turns + OUT_LAG - (last_lent - turns)
+
         def step(it, carry):
             for when, work in extra.items():
                 pl.when(it == when)(work)
@@ -1108,7 +1123,7 @@
                 outwards(u8).wait_recv()
                 finish(u8, from_z(u8))
 
-            @pl.when(it == turns - 2 * SUBS)
+            @pl.when(it == norms_at)
             def _():
                 bn_sums()
 
@@ -1116,43 +1131,49 @@
                 def _():
                     bn_in().start()
 
-            @pl.when(inner & (it == turns))
+            @pl.when(inner & (it == norms_at + 4))
             def _():
                 bn_in().wait_recv()
-                dgs[...] += bz[0]
+                dgs[:, norm_half] += bz[0, :, norm_half]
                 bn_across().start()
 
-            @pl.when(inner & (it == turns + 2 * SUBS))
+            @pl.when(inner & (it == norms_at + 8))
             def _():
                 bn_across().wait()
-                dgb[...] = dgs[...] + bz[1]
+                dgb[:, norm_half] = dgs[:, norm_half] + bz[1, :, norm_half]
                 bn_out().start()
+                bn_core().start()
+
+            @pl.when(outer & (it == norms_at + 14))
+            def _():
+                bn_out().wait_recv()
+                dgb[:, norm_half] = bz[0, :, norm_half]
+                bn_core().start()
+
+            if lend:
+                u_back = turns + it - take_at
+
+                @pl.when(it == take_at)
+                def _():
+                    all_here(ars.at[R_BACK], unit_rows(last_lent - turns))
+
+                @pl.when((u_back >= turns) & (u_back < last_lent))
+                def _():
+                    pack(u_back, own_turns + u_back - turns, from_z(u_back))
 
             return carry
 
         lax.fori_loop(0, turns + OUT_LAG, step, 0)
+
+        bn_core().wait()
 
         @pl.when(outer)
         def _():
             bn_in().wait_send()
-            bn_out().wait_recv()
-            dgb[...] = bz[0]
 
         @pl.when(inner)
         def _():
             bn_out().wait_send()
-
-        def unit_rows(units):
-            return wh.at[0 : units * SUB_ROWS]
-
-        if lend:
-            all_here(ars.at[R_BACK], unit_rows(last_lent - turns))
-
-            def take(u, carry):
-                pack(u, own_turns + u - turns, from_z(u))
-                return carry
-
-            lax.fori_loop(turns, last_lent, take, 0)
 
         @pl.when(outer)
         def _():
@@ -1248,8 +1269,8 @@
 
         lax.fori_loop(0, 9, body, 0)
 
-    def conv_back(dz, ref, first, base):
-        pb[...] = jnp.zeros_like(pb)
+    def conv_back(dz, ref, first, base, side):
+        pb[0:side, 0:side] = jnp.zeros((side, side, 8, BLK), F32)
 
         def body(tap, carry):
             row, col = base(tap)
@@ -1286,7 +1307,7 @@
 
         tx[slot_sum], tx[slot_gain] = five(body, zero_stats)
 
-    def norm_back(target, first, du_ref, du_first, zhat_ref, zhat_first, gscale, mean_du, mean_dg):
+    def norm_back(target, first, du_ref, du_first, zhat_ref, zhat_first, gscale, mean_du, mean_dg, unrolled=False):
         def body(c, i, carry):
             du = du_ref[pl.ds(du_first + i * 10, 10)]
             zhat = zhat_ref[pl.ds(zhat_first + i * 10, 10)]
@@ -1294,11 +1315,17 @@
             target[rows(first + i * 80, 80), :] = dz.reshape(80, BLK).astype(BF16)
             return carry
 
-        five(body)
+        five(body, unrolled=unrolled)
         clear_pad(target, first)
 
     def gi_copy():
         return pltpu.make_async_copy(f3.at[0:PIX_IN, :, 0:256], gi, ls.at[17])
+
+    def out_copy():
+        return pltpu.make_async_copy(v_out, out, ls.at[0])
+
+    def dgb_copy():
+        return pltpu.make_async_copy(dgb, dgb_out, ls.at[1])
 
     def final_part():
         @pl.when(p != 1)
@@ -1310,7 +1337,8 @@
         def _():
             remote(r0, r0, C_GI, C_GI, (p, d, r)).wait_recv()
 
-        out[...] = ob[0:RV, :].astype(F32).reshape(PIX_OUT, 8, BLK).astype(BF16)
+        v_out[...] = ob[0:RV, :].astype(F32).reshape(PIX_OUT, 8, BLK).astype(BF16)
+        out_copy().start()
         f0[0:PP, :, 0:256] = r1[...].astype(F32).reshape(PP, 8, 256)
 
         def place(a, carry):
@@ -1395,7 +1423,7 @@
         dg[1], dg[9] = s_dg, s_du
         norm_back(d5, 0, fs.at[1], 0, fs.at[0], 0, g2 * inv[1], s_du * (1.0 / total_out), s_dg * (1.0 / total_out))
         def back_conv():
-            conv_back(d5, wh, 1024, strided_base)
+            conv_back(d5, wh, 1024, strided_base, 16)
 
         def slopes(i, carry):
             u = i + 1
@@ -1443,7 +1471,7 @@
 
         def back_and_share():
             first_back()
-            share_out(3)
+            share_out(1)
 
         def compute(t):
             taps = (t < 7) | (t >= 9)
@@ -1467,12 +1495,12 @@
                 2 * SUBS: back_conv,
                 3 * SUBS: first_slopes,
                 4 * SUBS: back_and_share,
-                5 * SUBS: lambda: share_out(1),
-                6 * SUBS: lambda: share_out(2),
+                5 * SUBS: lambda: share_out(2),
+                6 * SUBS: lambda: share_out(3),
                 7 * SUBS: lambda: share(r0, 0, 0),
                 LAST_TURN + 9 * SUBS: final_part,
             },
-            lend=(2, 3), helper=2, helper_turn=lambda t: t - 5,
+            lend=(2, 3), helper=2, helper_turn=lambda t: t - 4, norms_at=4 * SUBS,
         )
         for k in (1, 2, 3):
             share_copy(k).wait_send()
@@ -1593,7 +1621,7 @@
         remote(parx.at[0:4], parx.at[0:4], C_PAR2, C_PAR2, (1, d, r)).wait_recv()
         center, scale = moments(16, 17, total_out, 10)
         g4, g5, b4, b5 = parx[0], parx[1], parx[2], parx[3]
-        pb[...] = jnp.zeros_like(pb)
+        pb[0:9, 0:9] = jnp.zeros((9, 9, 8, BLK), F32)
 
         def hidden(a, carry):
             part = pl.ds(a * 7, 7)
@@ -1611,26 +1639,26 @@
         o1_copy(0, 2).start()
         pass_on(5)
         build_patches(plain_base)
+
+        def fifth_conv(taps):
+            left = jnp.concatenate([pt[t] for t in taps], axis=1)
+            right = jnp.concatenate([wx[2048 + t * 512 : 2560 + t * 512, :] for t in taps], axis=0)
+            return nn(left, right).reshape(PP, 8, BLK)
+
+        for i in (4, 5, VIA):
+            have(i)
+        zhat5[...] = fifth_conv((0, 1, 4))
         pass_half(14)
         pass_on(6)
+        for i in (6, VIA + 1, VIA + 2):
+            have(i)
+        zhat5[...] += fifth_conv((2, 5, 6))
         pass_half(HALF + 1)
         pass_on(7)
-        zhat5[...] = jnp.zeros_like(zhat5)
-
-        def fifth_conv(t, carry):
-            @pl.when(t < HALF - 4)
-            def _():
-                have(4 + t)
-
-            @pl.when(t >= HALF - 4)
-            def _():
-                have_half(4 + t)
-
-            z = nn(pt[t], wx[rows(2048 + t * 512, 512), :])
-            zhat5[...] += z.reshape(PP, 8, BLK)
-            return carry
-
-        lax.fori_loop(0, 9, fifth_conv, 0)
+        have(7)
+        have_half(HALF)
+        have_half(HALF + 1)
+        zhat5[...] += fifth_conv((3, 7, 8))
         pass_half(15)
         stats_of_map(zhat5, 18, 19)
         sync(1, 18, 2)
@@ -1639,18 +1667,17 @@
 
         pass_half(16)
 
-        def sixth_conv(n, carry):
+        def sixth_conv(n):
             have_half(13 + n)
-            store_z(f2, n * PP, nn(h5[...], wx[rows(6656 + n * 512, 512), :]), 20 + 2 * n, 21 + 2 * n)
-            exchange_of(E_WIDE_NEXT + n, 20 + 2 * n, 2).start()
-            return carry
-
-        lax.fori_loop(0, 4, sixth_conv, 0)
-        remote(parx.at[4:12], parx.at[4:12], C_PAR3, C_PAR3, (1, d, r)).wait_recv()
-        pltpu.make_async_copy(cot, cotb.at[0:PIX_OUT], ls.at[16]).wait()
-
-        def finish(n, carry):
-            exchange_of(E_WIDE_NEXT + n, 20 + 2 * n, 2).wait()
+            store_z(f2, n * PP, nn(h5[...], wx[6656 + n * 512 : 7168 + n * 512, :]), 20 + 2 * n, 21 + 2 * n)
+
+        def exchange_z6(n):
+            return exchange_of(E_WIDE_NEXT + n, 20 + 2 * n, 2)
+
+        def exchange_d6(n):
+            return exchange_of(E_WIDE + n, 28 + 2 * n, 2)
+
+        def finish(n):
             center, scale = moments(20 + 2 * n, 21 + 2 * n, total_out, 12 + n)
             g6, b6 = parx[4 + n], parx[8 + n]
 
@@ -1662,35 +1689,54 @@
                 o = u0[part_rows, :].astype(F32).reshape(10, 8, BLK)
                 q = o + zhat * g6 + b6
                 s = sigmoid(q)
-                merged = gate_v * (q * s) + (1.0 - gate_v) * o
-                pt[n, rows(i * 80, 80), :] = merged.reshape(80, BLK).astype(BF16)
-                ct = cotb[c, :, pl.ds(pl.multiple_of(n * BLK, BLK), BLK)].astype(F32)
-                dq = ct * gate_v * (s * (1.0 + q * (1.0 - s)))
+                act = q * s
+                pt[n, rows(i * 80, 80), :] = (o + gate_v * (act - o)).reshape(80, BLK).astype(BF16)
+                ct = cotb[c, :, n * BLK : (n + 1) * BLK].astype(F32)
+                through = ct * gate_v
+                dq = through * (s + act * (1.0 - s))
                 f3[part] = dq
-                dres = dq + (1.0 - gate_v) * ct
-                u2[part_rows, :] = dres.reshape(80, BLK).astype(BF16)
+                u2[part_rows, :] = (dq + (ct - through)).reshape(80, BLK).astype(BF16)
                 return add_stats(carry, dq, dq * zhat)
 
-            tx[28 + 2 * n], tx[29 + 2 * n] = five(body, zero_stats)
-            exchange_of(E_WIDE + n, 28 + 2 * n, 2).start()
-            return carry
-
-        lax.fori_loop(0, 4, finish, 0)
+            tx[28 + 2 * n], tx[29 + 2 * n] = five(body, zero_stats, unrolled=True)
+
+        for n in (0, 1):
+            sixth_conv(n)
+            exchange_z6(n).start()
+        remote(parx.at[4:12], parx.at[4:12], C_PAR3, C_PAR3, (1, d, r)).wait_recv()
+        pltpu.make_async_copy(cot, cotb.at[0:PIX_OUT], ls.at[16]).wait()
+        for n in range(4):
+            if n < 2:
+                have_half(15 + n)
+            exchange_z6(n).wait()
+            if n < 2:
+                store_z(
+                    f2, (n + 2) * PP, nn(h5[...], wx[7680 + n * 512 : 8192 + n * 512, :]), 24 + 2 * n, 25 + 2 * n
+                )
+            finish(n)
+            if n < 2:
+                exchange_z6(n + 2).start()
+            exchange_d6(n).start()
         ob[...] = pt[1]
 
 
-        def sixth_back(n, carry):
-            exchange_of(E_WIDE + n, 28 + 2 * n, 2).wait()
+        def sixth_back(n):
             s_du, s_dg = both(28 + 2 * n), both(29 + 2 * n)
             dgx[4 + n] = s_dg
             dgx[8 + n] = s_du
-            norm_back(u1, n * RW, f3, n * PP, f2, n * PP, parx[4 + n] * inv[12 + n], s_du * (1.0 / total_out), s_dg * (1.0 / total_out))
-            return carry
-
-        lax.fori_loop(0, 4, sixth_back, 0)
-        grad = nt(u1[0:RW, :], wx[6656:7168, :])
-        for n in range(1, 4):
-            grad += nt(u1[n * RW : (n + 1) * RW, :], wx[6656 + n * 512 : 7168 + n * 512, :])
+            norm_back(
+                u1, n * RW, f3, n * PP, f2, n * PP, parx[4 + n] * inv[12 + n],
+                s_du * (1.0 / total_out), s_dg * (1.0 / total_out), unrolled=True,
+            )
+
+        for n in range(4):
+            exchange_d6(n).wait()
+        grad = jnp.zeros((RW, BLK), F32)
+        for n in range(5):
+            if n < 4:
+                sixth_back(n)
+            if n > 0:
+                grad += nt(u1[(n - 1) * RW : n * RW, :], wx[6144 + n * 512 : 6656 + n * 512, :])
         dh[...] = grad.astype(BF16)
 
         upstream(f2, dh, zhat5, g5, b5, mask, 36, 37)
@@ -1701,7 +1747,11 @@
         norm_back(d5, 0, f2, 0, zhat5, 0, g5 * inv[11], s_du * (1.0 / total_out), s_dg * (1.0 / total_out))
         d5_send = remote(d5, d5, C_D5, C_D5, (2, d, r))
         d5_send.start()
-        conv_back(d5, wx, 2048, plain_base)
+        pb[0:9, 0:9] = jnp.zeros((9, 9, 8, BLK), F32)
+        for tap in range(9):
+            row, col = tap // 3, tap % 3
+            part = nt(d5[0:RV, :], wx[2048 + tap * 512 : 2560 + tap * 512, :])
+            pb[row : row + 7, col : col + 7] += part.reshape(7, 7, 8, BLK)
 
         def fourth_slopes(a, carry):
             part = pl.ds(a * 7, 7)
@@ -1717,13 +1767,20 @@
         dgx[2] = s_du
         norm_back(d4, 0, f2, 0, zhat4, 0, g4 * inv[10], s_du * (1.0 / total_out), s_dg * (1.0 / total_out))
 
-        def first_block_slopes(n, carry):
-            f3[pl.ds(n * PP, PP)] = nt(d4[...], wx[rows(n * 512, 512), :]).reshape(PP, 8, BLK)
+        def carried_back(n):
+            z = nt(d4[...], wx[n * 512 : (n + 1) * 512, :])
+            f2[(n % 2) * PP : (n % 2 + 1) * PP] = z.reshape(PP, 8, BLK)
+
+        def exchange_d1(n):
+            return exchange_of(E_WIDE_NEXT + n, 40 + 3 * n, 3)
+
+        def first_block_slopes(n):
             g3, gp, b = par[n], par[4 + n], par[8 + n] + par[12 + n]
 
             def body(_, i, carry):
                 part = pl.ds(n * PP + i * 10, 10)
-                do = u2[rows(n * RW + i * 80, 80), :].astype(F32).reshape(10, 8, BLK) + f3[part]
+                do = u2[n * RW + i * 80 : n * RW + (i + 1) * 80, :].astype(F32).reshape(10, 8, BLK)
+                do += f2[pl.ds((n % 2) * PP + i * 10, 10)]
                 a, b_ = f0[part], f1[part]
                 dp = do.astype(BF16).astype(F32) * slope(a * g3 + b_ * gp + b)
                 f3[part] = dp
@@ -1731,33 +1788,46 @@
                 return s0 + jnp.sum(dp, axis=0), s1 + jnp.sum(dp * a, axis=0), s2 + jnp.sum(dp * b_, axis=0)
 
             first = 40 + 3 * n
-            tx[first], tx[first + 1], tx[first + 2] = five(body, zero_stats + zero_stats[:1])
-            exchange_of(E_WIDE_NEXT + n, first, 3).start()
-            return carry
-
-        lax.fori_loop(0, 4, first_block_slopes, 0)
-
-        def third_back(n, carry):
+            tx[first], tx[first + 1], tx[first + 2] = five(body, zero_stats + zero_stats[:1], unrolled=True)
+
+        carried_back(0)
+        for n in range(4):
+            if n < 3:
+                carried_back(n + 1)
+            first_block_slopes(n)
+            exchange_d1(n).start()
+
+        def third_back(n):
             first = 40 + 3 * n
-            exchange_of(E_WIDE_NEXT + n, first, 3).wait()
+            m_du, m_dg = both(first) * (1.0 / total_out), both(first + 1) * (1.0 / total_out)
+            norm_back(
+                pt.at[4 + n], 0, f3, n * PP, f0, n * PP, par[n] * inv[2 + n], m_du, m_dg, unrolled=True
+            )
+
+        for n in range(4):
+            exchange_d1(n).wait()
+        grad = jnp.zeros((RW, BLK), F32)
+        for n in range(5):
+            if n < 4:
+                third_back(n)
+            if n > 0:
+                grad += nt(pt[3 + n], wh[(n - 1) * 512 : n * 512, :])
+        dh[...] = grad.astype(BF16)
+        dh_send = remote(dh, dh, C_DH, C_DH, (0, d, r))
+        dh_send.start()
+
+        def shortcut_back(n, carry):
+            first = 40 + 3 * n
             s_du, s_d3, s_dp = both(first), both(first + 1), both(first + 2)
             dg[n] = s_d3
             dg[4 + n] = s_dp
             dg[8 + n] = s_du
             dg[12 + n] = s_du
-            m_du = s_du * (1.0 / total_out)
-            norm_back(pt.at[4 + n], 0, f3, n * PP, f0, n * PP, par[n] * inv[2 + n], m_du, s_d3 * (1.0 / total_out))
-            norm_back(u2, n * RW, f3, n * PP, f1, n * PP, par[4 + n] * inv[6 + n], m_du, s_dp * (1.0 / total_out))
+            m_du, m_dg = s_du * (1.0 / total_out), s_dp * (1.0 / total_out)
+            norm_back(u2, n * RW, f3, n * PP, f1, n * PP, par[4 + n] * inv[6 + n], m_du, m_dg)
             return carry
 
-        lax.fori_loop(0, 4, third_back, 0)
-        grad = nt(pt[4], wh[0:512, :])
-        for n in range(1, 4):
-            grad += nt(pt[4 + n], wh[n * 512 : (n + 1) * 512, :])
-        dh[...] = grad.astype(BF16)
-        dh_send = remote(dh, dh, C_DH, C_DH, (0, d, r))
-        dh_send.start()
-
+        lax.fori_loop(0, 4, shortcut_back, 0)
         all_sent(wss.at[W_PEER], wx.at[0 : HALF * 128 + 6 * 256])
         all_sent(wss.at[W_Z], wx.at[0 : HALF * 128])
         all_sent(wss.at[W_ON], wx.at[0 : HALF * 128])
@@ -1802,39 +1872,42 @@
             for slot in range(3):
                 share_copy(slot).start()
 
+        def at_row(t):
+            return jnp.where(t < 10, t * 512, jnp.where(t < 15, t * 512 + 1024, 5632))
+
         def compute(t):
             @pl.when(t < 4)
             def _():
                 left = h2[:, pl.ds(pl.multiple_of(t * 128, 128), 128)]
                 for n in range(4):
-                    put_chunk(t, n, tn(left, pt[4 + n]))
+                    put_chunk(at_row(t), n, tn(left, pt[4 + n]))
 
             @pl.when((t >= 4) & (t < 12))
             def _():
                 m = t - 4
                 left = sx[rows((m // 4) * RW, RW), pl.ds(pl.multiple_of(lax.rem(m, 4) * 128, 128), 128)]
                 for n in range(4):
-                    put_chunk(t, n, tn(left, u2[n * RW : (n + 1) * RW, :]))
+                    put_chunk(at_row(t), n, tn(left, u2[n * RW : (n + 1) * RW, :]))
 
             @pl.when(t >= 12)
             def _():
                 left = h5[:, pl.ds(pl.multiple_of((t - 12) * 128, 128), 128)]
                 for n in range(4):
-                    put_chunk(t, n, tn(left, u1[n * RW : (n + 1) * RW, :]))
+                    put_chunk(at_row(t), n, tn(left, u1[n * RW : (n + 1) * RW, :]))
 
         zero_rest(12, sb)
         sum_gradients(
-            12, compute, lambda t: t * 512, lambda t: t, True, 0,
+            10, compute, at_row, lambda t: t, True, 0,
             {
                 2: lambda: shortcut_shares(0),
                 4: lambda: shortcut_shares(1),
+                5: late_sends,
                 6: lambda: shortcut_shares(2),
-                7: late_sends,
                 8: shortcut_own,
-                10: late_shares,
-                LAST_TURN + 12 * SUBS: final_part,
+                14: late_shares,
+                LAST_TURN + 10 * SUBS: final_part,
             },
-            passed=(3, 5, 7, 9), helper=3, helper_turn=lambda t: t - 7,
+            lend=(3, 5), passed=(7, 9, 11, 13), helper=3, helper_turn=lambda t: t - 6, norms_at=2,
         )
         for copy in [d5_send, o1_copy(0, 2)] + [o1_copy(n, 3) for n in (1, 2, 3)] + late + later:
             copy.wait_send()
@@ -1880,14 +1953,14 @@
         remote(d5, d5, C_D5, C_D5, (2, d, r)).wait_recv()
 
         def compute(t):
-            taps = (t < 4) | (t >= 10)
+            taps = (t < 5) | (t >= 11)
 
             @pl.when(taps)
             def _():
-                tap = jnp.where(t < 4, t + 5, t - 10)
+                tap = jnp.where(t < 5, t + 4, t - 11)
                 wh[rows(t * 512, 512), :] = tn(pt[tap], d5[...]).astype(BF16)
 
-            @pl.when(t == 6)
+            @pl.when(t == 7)
             def _():
                 remote(d4, d4, C_D4, C_D4, (2, d, r)).wait_recv()
                 for n in range(4):
@@ -1895,19 +1968,19 @@
 
             @pl.when(jnp.logical_not(taps))
             def _():
-                wh[rows(t * 512, 512), :] = tn(u0[rows((t - 6) * RW, RW), :], d4[...]).astype(BF16)
+                wh[rows(t * 512, 512), :] = tn(u0[rows((t - 7) * RW, RW), :], d4[...]).astype(BF16)
 
         def norm_grads():
             remote(dgx.at[0:4], dgx.at[0:4], C_DG2, C_DG2, (2, d, r)).wait_recv()
             dg[0], dg[1], dg[8], dg[9] = dgx[0], dgx[1], dgx[2], dgx[3]
 
         sum_gradients(
-            10, compute, lambda t: t * 512, lambda t: jnp.where(t < 4, t + 9, t - 6), False, 0,
-            {7 * SUBS: norm_grads, LAST_TURN + 10 * SUBS: final_part},
-            lend=(2, 3, 4, 5, 6), helper=3, helper_turn=lambda t: t - 10,
-            handed_in=lambda t: (t >= 4) & (t < 6),
-            lent_by=(lambda t: (t >= 4) & (t < 6), lambda t: 0, lambda t: t + 5, 2),
-            computed=(0, 8), packed_here=(0, 8),
+            11, compute, lambda t: t * 512, lambda t: jnp.where(t < 5, t + 8, t - 7), False, 0,
+            {6 * SUBS: norm_grads, LAST_TURN + 11 * SUBS: final_part},
+            lend=(2, 3, 4, 6), helper=3, helper_turn=lambda t: t - 11,
+            handed_in=lambda t: (t >= 5) & (t < 7),
+            lent_by=(lambda t: (t >= 5) & (t < 7), lambda t: 0, lambda t: t + 4, 2),
+            computed=(0, 9), packed_here=(0, 9), norms_at=6 * SUBS,
         )
         par_send.wait_send()
 
@@ -1944,11 +2017,11 @@
                 dg[8 + k] = dgx[8 + k]
 
         sum_gradients(
-            9, lambda t: None, lambda t: t * 512, lambda t: t - 5, True, 0,
-            {6 * SUBS: norm_grads, LAST_TURN + 9 * SUBS: final_part},
+            10, lambda t: None, lambda t: t * 512, lambda t: t - 6, True, 0,
+            {5 * SUBS: norm_grads, LAST_TURN + 10 * SUBS: final_part},
             handed_in=lambda t: t >= 0,
-            lent_by=(lambda t: t < 5, lambda t: 2, lambda t: t + 10, 5),
-            computed=(0, 0), packed_here=(5, 4),
+            lent_by=(lambda t: t < 6, lambda t: jnp.where(t < 4, 2, 1), lambda t: jnp.where(t < 4, t + 11, t + 6), 6),
+            computed=(0, 0), packed_here=(6, 4), norms_at=5 * SUBS,
         )
         for n in (1, 2, 3):
             o1_copy(n, 2).wait_send()
@@ -1956,7 +2029,10 @@
         all_sent(wss.at[W_OWN], wx.at[0 : 3 * 256])
         par_send.wait_send()
 
+    dgb_copy().start()
     gi_copy().wait()
+    out_copy().wait()
+    dgb_copy().wait()
 
 
 def widen_kernel(out_in, gi_in, dw_in, dgb_in, out, gi, dw, gain, bias, v_out, v_gi, v_dw, v_wide, v_dgb, sin, sout):
@@ -2029,12 +2105,12 @@
             jax.ShapeDtypeStruct((8, 4096), F32),
         ),
         in_specs=[any_space, any_space, vmem, vmem, smem, smem, smem, any_space],
-        out_specs=(vmem, any_space, any_space, vmem),
+        out_specs=(any_space,) * 4,
         scratch_shapes=[
             pltpu.VMEM((4, 28, 8, 1024), BF16),
             pltpu.VMEM((RING, 1, SUB), BF16),
             pltpu.VMEM((512, 128), F32),
-            pltpu.VMEM((8192, BLK), BF16),
+            pltpu.VMEM((8704, BLK), BF16),
             pltpu.VMEM((8768, BLK), BF16),
             pltpu.VMEM((4 * PP, 8, BLK), F32),
             pltpu.VMEM((4 * PP, 8, BLK), F32),
@@ -2068,6 +2144,8 @@
             pltpu.VMEM((4096, BLK), BF16),
             pltpu.VMEM((2, 8, 4096), F32),
             pltpu.VMEM((8, 4096), F32),
+            pltpu.VMEM((8, 4096), F32),
+            pltpu.VMEM((PIX_OUT, 8, BLK), BF16),
             pltpu.SemaphoreType.DMA((19,)),
             pltpu.SemaphoreType.DMA((N_SEM,)),
             pltpu.SemaphoreType.DMA((N_SEM,)),

time: 176 us -> 168 us (0.955)
  Pallas kernels: 175 us -> 165 us
    pallas_call x1, Pallas kernels: 166 us -> 157 us  [one_kernel(): pl.pallas_call(whole_kernel, out_shape=(jax.ShapeDtypeStruct((PIX_OUT, 8,...]
where the time goes in v4:
time: 168 us; the launch traced here: 166 us
  Pallas kernels  165 us (98%)
    pallas_call x1, Pallas kernels, one_kernel(): pl.pallas_call(whole_kernel, out_shape=(jax.ShapeDtypeStruct((PIX_OUT, 8,...  157 us
    pallas_call x1, Pallas kernels, widen(): pl.pallas_call(widen_kernel, out_shape=(jax.ShapeDtypeStruct(out.shape, o...  8.68 us

profile of v4, /device:TPU:5, one launch (start us, length us, event | category | flops | bytes accessed | tf_op | source)
XLA Modules:
  0.0 166.1 jit_solution(2169202136657686929)
XLA Ops:
  0.6 156.6 %shard_map.119 = (bf16[49,8,512]{2,1,0:T(8,128)(2,1)}, f32[196,8,256]{2,1,0:T(8,128)}, bf16[52,512,128]{2,1,0:T(8,128)(2,1)}, f32[8,4096]{1,0:T(8,128)}) custom-call(bf16[196,8,1024]{2,1,0:T(8,128)(2,1)} %bitcast.13, bf16[1,3407872]{1,0:T(2,128)(2,1)} %wts.1, f32[4,4096]{1,0:T(4,128)} %bitcast.15, f32[4,4096]{1,0:T(4,128)} %bitcast.16, s32[2,8]{1,0:T(2,128)} %bitcast.17, ...), custom_call_target="tpu_custom_call" | custom-call | tf_op jit(solution)/shard_map/pallas_call | solution.py:2099
  157.2 8.7 %shard_map.120 = (bf16[49,8,512]{2,1,0:T(8,128)(2,1)}, f32[196,8,256]{2,1,0:T(8,128)}, f32[26624,128]{1,0:T(8,128)}, f32[4,4096]{1,0:T(4,128)}, f32[4,4096]{1,0:T(4,128)}) custom-call(bf16[49,8,512]{2,1,0:T(8,128)(2,1)} %get-tuple-element.14.out_in, f32[196,8,256]{2,1,0:T(8,128)} %get-tuple-element.15.gi_in, bf16[26624,128]{1,0:T(8,128)(2,1)} %bitcast.12, ...), custom_call_target="tpu_custom_call" | custom-call | tf_op jit(solution)/shard_map/pallas_call | solution.py:2071

commit v5 on v4

--- a/solution.py
+++ b/solution.py
@@ -652,13 +652,16 @@
 N_PIECE = 17
 W_OWN, W_PEER, W_Z, W_ON, W_VIA = range(5)
 VIA, HALF = 8, 11
-W_BASE = (0, 17, 34, 45, 56 - VIA)
-S_CORE, S_IN, S_OUT, S_HAND, S_BACK, S_DONE, S_ACROSS, N_SUM_SEND = 0, 1, 2, 3, 4, 5, 9, 17
-R_CORE, R_IN, R_ACROSS, R_OUT, R_GIVE = (0, 8), (8, 12), (20, 8), (28, 12), (40, 4)
-R_DONE, R_BACK, R_HAND, N_SUM_RECV = 44, 45, 46, 66
+W_BASE = (0, 17, 34, 45, -VIA)
+S_CORE, S_IN, S_OUT, S_HAND, S_BACK, S_DONE, S_ACROSS, N_SUM_SEND = 0, 1, 2, 3, 4, 5, 9, 25
+R_CORE, R_Z, R_ACROSS, R_GIVE = (0, 8), (8, 24), (32, 16), (48, 4)
+R_DONE, R_BACK, R_BACK_HUB, R_HAND, N_SUM_RECV = 52, 53, 54, 55, 75
+HUB_GUEST = 8704
 RING = 8
 SUBS = 2
 SUB_ROWS = 256 // SUBS
+HOPS = 2
+HOP_ROWS = SUB_ROWS // HOPS
 Z1_ZERO = 3136
 ACROSS_LAG, OUT_LAG = 3 * SUBS // 2 + 1, 4 * SUBS
 LAST_TURN = OUT_LAG - 2
@@ -685,11 +688,11 @@
 
 
 def whole_kernel(
-    img, wts, gain, bias, width, sets, gates, cot,
+    img, wts, gain_in, bias_in, width, sets, gates, cot,
     out, gi, dw, dgb_out,
     imgb, raw, st, wh, wx, f0, f1, f2, f3, fs, pb, pt, u0, u1, u2, sx, cotb,
-    h2, h4, h5, d5, d4, dh, r0, r1, ob, tx, rx, inv, par, parx, dg, dgx, sb, rd, bz, dgs, dgb, v_out,
-    ls, ss, rs, wss, wrs, ass, ars, ready, go,
+    h2, h4, h5, d5, d4, dh, r0, r1, ob, tx, rx, inv, par, parx, dg, dgx, sb, rd, bz, dgs, dgb, v_out, gain, bias,
+    ls, ss, rs, wss, ass, ars, ready, go,
 ):
     p, d, r = lax.axis_index("pipe"), lax.axis_index("dp"), lax.axis_index("rep")
     peer = (p, 1 - d, r)
@@ -824,7 +827,7 @@
     def piece_copy(kind, i, q, device):
         part = wx.at[rows(i * 512 + q * 128, 128)]
         return pltpu.make_async_remote_copy(
-            src_ref=part, dst_ref=part, send_sem=wss.at[kind], recv_sem=wrs.at[W_BASE[kind] + i],
+            src_ref=part, dst_ref=part, send_sem=wss.at[kind], recv_sem=ars.at[W_BASE[kind] + i],
             device_id=device, device_id_type=MESH,
         )
 
@@ -832,7 +835,7 @@
         part = wx.at[rows(i * 512 + which * 256, 256)]
         order = min(i, 13) if kind == W_VIA else i
         return pltpu.make_async_remote_copy(
-            src_ref=part, dst_ref=part, send_sem=wss.at[kind], recv_sem=wrs.at[W_BASE[kind] + order],
+            src_ref=part, dst_ref=part, send_sem=wss.at[kind], recv_sem=ars.at[W_BASE[kind] + order],
             device_id=device, device_id_type=MESH,
         )
 
@@ -909,19 +912,20 @@
                 dgs[k : k + 1, cols] = jnp.sum(dg[n] * hot, axis=0, keepdims=True)
                 dgs[4 + k : 5 + k, cols] = jnp.sum(dg[8 + n] * hot, axis=0, keepdims=True)
 
-    norm_half = pl.ds(pl.multiple_of(d * 2048, 2048), 2048)
-
-    def bn_in():
-        return remote(dgs.at[:, norm_half], bz.at[0, :, norm_half], C_BN1, C_BN1, z_dev)
-
-    def bn_across():
-        return remote(dgs.at[:, norm_half], bz.at[1, :, norm_half], C_BN2, C_BN2, across)
-
-    def bn_out():
-        return remote(dgb.at[:, norm_half], bz.at[0, :, norm_half], C_BN3, C_BN3, z_dev)
-
-    def bn_core():
-        return remote(dgb.at[:, norm_half], dgb.at[:, norm_half], C_BN4, C_BN4, peer)
+    def norm_half(channels):
+        return pl.ds(pl.multiple_of(d * (channels // 2), 512), channels // 2)
+
+    def bn_in(cols):
+        return remote(dgs.at[:, cols], bz.at[0, :, cols], C_BN1, C_BN1, z_dev)
+
+    def bn_across(cols):
+        return remote(dgs.at[:, cols], bz.at[1, :, cols], C_BN2, C_BN2, across)
+
+    def bn_out(cols):
+        return remote(dgb.at[:, cols], bz.at[0, :, cols], C_BN3, C_BN3, z_dev)
+
+    def bn_core(cols):
+        return remote(dgb.at[:, cols], dgb.at[:, cols], C_BN4, C_BN4, peer)
 
     def say_ready():
         pl.semaphore_signal(ready.at[0], inc=1, device_id=z_dev, device_id_type=MESH)
@@ -932,14 +936,15 @@
 
     def sum_gradients(
         count, compute, at_row, chunk_of, wide, z1, extra,
-        lend=(), passed=(), helper=0, helper_turn=None, handed_in=None, lent_by=None, computed=None, packed_here=None,
-        norms_at=0,
+        lend=(), passed=(), helper=None, helper_turn=None, helper_row=None, handed_in=None, lent_by=None, computed=None, packed_here=None,
+        norms_at=0, norms=4096, after=None, back=R_BACK, late_back=0,
     ):
         turns = SUBS * count
         last_lent = SUBS * (count + len(lend))
         last_given = last_lent + SUBS * len(passed)
         computed = (0, count) if computed is None else computed
         packed_here = (0, count) if packed_here is None else packed_here
+        cols = norm_half(norms)
         first_own, own_turns = packed_here[0] * SUBS, packed_here[1] * SUBS
         z2 = z1 + last_given * SUB_ROWS
 
@@ -966,11 +971,18 @@
         def half(u, which):
             return wh.at[rows(at_row(u // SUBS) + which * 256 + lax.rem(u, SUBS) * SUB_ROWS, SUB_ROWS)]
 
+        def half_part(u, k):
+            first = at_row(u // SUBS) + d * 256 + lax.rem(u, SUBS) * SUB_ROWS + k * HOP_ROWS
+            return wh.at[rows(first, HOP_ROWS)]
+
         def from_z(u):
             return wx.at[rows(z1 + u * SUB_ROWS, SUB_ROWS)]
 
-        def from_across(u):
-            return wx.at[rows(z2 + u * SUB_ROWS, SUB_ROWS)]
+        def from_z_part(u, k):
+            return wx.at[rows(z1 + u * SUB_ROWS + k * HOP_ROWS, HOP_ROWS)]
+
+        def from_across(u, k):
+            return wx.at[rows(z2 + u * SUB_ROWS + k * HOP_ROWS, HOP_ROWS)]
 
         def from_core(u):
             return rd.at[rows(u * SUB_ROWS, SUB_ROWS)]
@@ -979,14 +991,17 @@
             recv = jnp.where(u < turns, in_turn(R_CORE, u), in_turn(R_GIVE, u))
             return grad_copy(S_CORE, recv, half(u, 1 - d), from_core(u), peer)
 
-        def inwards(u):
-            return grad_copy(S_IN, in_turn(R_IN, u), half(u, d), from_z(u), z_dev)
-
-        def exchange(u):
-            return grad_copy(S_ACROSS + lax.rem(u, 8), in_turn(R_ACROSS, u), half(u, d), from_across(u), across)
-
-        def outwards(u):
-            return grad_copy(S_OUT, in_turn(R_OUT, u), half(u, d), from_z(u), z_dev)
+        def inwards(u, k):
+            return grad_copy(S_IN, in_turn(R_Z, u * HOPS + k), half_part(u, k), from_z_part(u, k), z_dev)
+
+        def exchange(u, k):
+            turn = u * HOPS + k
+            return grad_copy(
+                S_ACROSS + lax.rem(turn, 16), in_turn(R_ACROSS, turn), half_part(u, k), from_across(u, k), across
+            )
+
+        def outwards(u, k):
+            return grad_copy(S_OUT, in_turn(R_Z, u * HOPS + k), half_part(u, k), from_z_part(u, k), z_dev)
 
         def packed(u, which):
             return dw.at[chunk_of(u // SUBS) * 4 + which * 2 + lax.rem(u, SUBS)]
@@ -999,9 +1014,9 @@
             slot = lax.rem(turn, 4)
             return pltpu.make_async_copy(sb.at[slot], packed(u, d), ls.at[4 + slot])
 
-        def add(u, other):
-            sums = half(u, d)[...].astype(F32) + other[...].astype(F32)
-            half(u, d)[...] = sums.astype(BF16)
+        def add(mine, other):
+            sums = mine[...].astype(F32) + other[...].astype(F32)
+            mine[...] = sums.astype(BF16)
 
         def pack(u, turn, ref):
             @pl.when(turn >= 4)
@@ -1023,9 +1038,11 @@
             done_core(u, turn).start()
 
         def hand(u):
-            theirs = helper_turn(u // SUBS) * SUBS + lax.rem(u, SUBS)
-            place = wh.at[rows(theirs * SUB_ROWS + (theirs // SUBS + d) * 256, SUB_ROWS)]
-            return grad_copy(S_HAND, R_HAND + theirs, half(u, d), place, (helper, d, r))
+            t, part = u // SUBS, lax.rem(u, SUBS)
+            theirs = helper_turn(t) * SUBS + part
+            row = helper_turn(t) * 512 if helper_row is None else helper_row(t)
+            place = wh.at[rows(row + d * 256 + part * SUB_ROWS, SUB_ROWS)]
+            return grad_copy(S_HAND, R_HAND + theirs, half(u, d), place, (helper(t), d, r))
 
         def handed(u):
             return grad_copy(S_HAND, R_HAND + u, half(u, d), half(u, d), (p, d, r))
@@ -1034,7 +1051,7 @@
             t = u // SUBS
             theirs = lent_by[2](t) * SUBS + lax.rem(u, SUBS)
             place = wx.at[rows(jnp.where(lent_by[1](t) == 0, Z1_ZERO, 0) + theirs * SUB_ROWS, SUB_ROWS)]
-            return grad_copy(S_BACK, R_BACK, ref, place, (lent_by[1](t), d, r))
+            return grad_copy(S_BACK, back, ref, place, (lent_by[1](t), d, r))
 
         def finish(u, ref):
             when_kept(u, lambda: pack(u, u - first_own, ref))
@@ -1047,7 +1064,7 @@
             for k in range(SUBS):
                 u = t * SUBS + k
                 to_core(u).wait_recv()
-                add(u, from_core(u))
+                add(half(u, d), from_core(u))
                 hand(u).start()
 
         def unit_rows(units):
@@ -1078,7 +1095,7 @@
             def _():
                 def join_cores():
                     to_core(u1).wait_recv()
-                    add(u1, from_core(u1))
+                    add(half(u1, d), from_core(u1))
 
                 when_own(u1, join_cores)
                 when_handed(u1, lambda: handed(u1).wait_recv())
@@ -1089,7 +1106,8 @@
 
                 @pl.when(outer)
                 def _():
-                    inwards(u1).start()
+                    for k in range(HOPS):
+                        inwards(u1, k).start()
 
             u2 = it - 2
 
@@ -1099,9 +1117,10 @@
                 def _():
                     pl.semaphore_wait(ready.at[1], 1)
 
-                inwards(u2).wait_recv()
-                add(u2, from_z(u2))
-                exchange(u2).start()
+                for k in range(HOPS):
+                    inwards(u2, k).wait_recv()
+                    add(half_part(u2, k), from_z_part(u2, k))
+                    exchange(u2, k).start()
 
             u4 = it - ACROSS_LAG
 
@@ -1111,16 +1130,20 @@
                 def _():
                     pl.semaphore_wait(ready.at[0], 1)
 
-                exchange(u4).wait()
-                add(u4, from_across(u4))
-                outwards(u4).start()
+                for k in range(HOPS):
+                    exchange(u4, k).wait()
+                    add(half_part(u4, k), from_across(u4, k))
+                    outwards(u4, k).start()
+
                 finish(u4, half(u4, d))
 
             u8 = it - OUT_LAG
 
             @pl.when(outer & (u8 >= 0) & (u8 < turns))
             def _():
-                outwards(u8).wait_recv()
+                for k in range(HOPS):
+                    outwards(u8, k).wait_recv()
+
                 finish(u8, from_z(u8))
 
             @pl.when(it == norms_at)
@@ -1129,33 +1152,44 @@
 
                 @pl.when(outer)
                 def _():
-                    bn_in().start()
+                    bn_in(cols).start()
 
             @pl.when(inner & (it == norms_at + 4))
             def _():
-                bn_in().wait_recv()
-                dgs[:, norm_half] += bz[0, :, norm_half]
-                bn_across().start()
+                bn_in(cols).wait_recv()
+                dgs[:, cols] += bz[0, :, cols]
+                bn_across(cols).start()
 
             @pl.when(inner & (it == norms_at + 8))
             def _():
-                bn_across().wait()
-                dgb[:, norm_half] = dgs[:, norm_half] + bz[1, :, norm_half]
-                bn_out().start()
-                bn_core().start()
+                bn_across(cols).wait()
+                dgb[:, cols] = dgs[:, cols] + bz[1, :, cols]
+                bn_out(cols).start()
+                bn_core(cols).start()
 
             @pl.when(outer & (it == norms_at + 14))
             def _():
-                bn_out().wait_recv()
-                dgb[:, norm_half] = bz[0, :, norm_half]
-                bn_core().start()
+                bn_out(cols).wait_recv()
+                dgb[:, cols] = bz[0, :, cols]
+                bn_core(cols).start()
+
+            for when, work in (after or {}).items():
+                pl.when(it == when)(work)
 
             if lend:
                 u_back = turns + it - take_at
 
+                late_units = late_back * SUBS
+
                 @pl.when(it == take_at)
                 def _():
-                    all_here(ars.at[R_BACK], unit_rows(last_lent - turns))
+                    all_here(ars.at[R_BACK], unit_rows(last_lent - turns - late_units))
+
+                if late_units:
+
+                    @pl.when(u_back == last_lent - late_units)
+                    def _():
+                        all_here(ars.at[R_BACK_HUB], unit_rows(late_units))
 
                 @pl.when((u_back >= turns) & (u_back < last_lent))
                 def _():
@@ -1165,15 +1199,15 @@
 
         lax.fori_loop(0, turns + OUT_LAG, step, 0)
 
-        bn_core().wait()
+        bn_core(cols).wait()
 
         @pl.when(outer)
         def _():
-            bn_in().wait_send()
+            bn_in(cols).wait_send()
 
         @pl.when(inner)
         def _():
-            bn_out().wait_send()
+            bn_out(cols).wait_send()
 
         @pl.when(outer)
         def _():
@@ -1195,6 +1229,13 @@
             done_here(first_own, jnp.int32(slot)).wait()
             done_core(first_own, jnp.int32(slot)).wait_send()
 
+    tables = [
+        pltpu.make_async_copy(gain_in, gain, ls.at[17]),
+        pltpu.make_async_copy(bias_in, bias, ls.at[18]),
+    ]
+    for copy in tables:
+        copy.start()
+
     @pl.when(p == 0)
     def _():
         open_weights(plain, 44)
@@ -1218,6 +1259,8 @@
     for device in (peer, (p, d, z_pair), (p, d, 3 - r)) + tuple((lax.rem(p + k, 4), d, r) for k in (1, 2, 3)):
         pl.semaphore_signal(barrier, inc=1, device_id=device, device_id_type=MESH)
 
+    for copy in tables:
+        copy.wait()
     block_two = p >= 2
     set_of = per_row(lambda m: jnp.where(block_two, sets[1, m], sets[0, m]))
     for k in range(NSETS):
@@ -1232,6 +1275,7 @@
                 par[n] += g
                 par[8 + n] += b
     dg[...] = jnp.zeros_like(dg)
+    dgb[...] = jnp.zeros_like(dgb)
     pl.semaphore_wait(barrier, 6)
 
     total_in, total_out = 2.0 * PIX_IN, 2.0 * PIX_OUT
@@ -1474,33 +1518,37 @@
             share_out(1)
 
         def compute(t):
-            taps = (t < 7) | (t >= 9)
+            taps = (t < 6) | (t >= 8)
 
             @pl.when(taps)
             def _():
-                tap = jnp.where(t < 7, t, t - 2)
+                tap = jnp.where(t < 6, t, t - 2)
                 wh[rows(at_row(t), 512), :] = tn(pt[tap], d5[...]).astype(BF16)
 
             @pl.when(jnp.logical_not(taps))
             def _():
-                block = tn(wx[rows((t - 7) * 1568, 1568), :], u1[0:1568, :])
+                block = tn(wx[rows((t - 6) * 1568, 1568), :], u1[0:1568, :])
                 wh[rows(at_row(t), 512), :] = block.astype(BF16)
 
         def at_row(t):
-            return jnp.where(t < 2, 5632 + t * 512, jnp.where(t < 9, t * 512, 2048 + t * 512))
+            return jnp.where(t < 2, 5632 + t * 512, jnp.where(t < 8, t * 512, 2560 + t * 512))
+
+        def chunk_of(t):
+            return jnp.where(t < 6, t + 2, jnp.where(t < 8, t - 6, t))
 
         sum_gradients(
-            9, compute, at_row, lambda t: jnp.where(t < 7, t + 2, jnp.where(t < 9, t - 7, t)), False, Z1_ZERO,
-            {
-                2 * SUBS: back_conv,
-                3 * SUBS: first_slopes,
-                4 * SUBS: back_and_share,
-                5 * SUBS: lambda: share_out(2),
-                6 * SUBS: lambda: share_out(3),
-                7 * SUBS: lambda: share(r0, 0, 0),
-                LAST_TURN + 9 * SUBS: final_part,
+            8, compute, at_row, chunk_of, False, Z1_ZERO,
+            {LAST_TURN + 8 * SUBS: final_part},
+            lend=(5, 6, 7), helper=lambda t: jnp.where(t < 10, 2, 1), helper_turn=lambda t: jnp.where(t < 10, t - 1, 8),
+            helper_row=lambda t: jnp.where(t < 10, (t - 1) * 512, HUB_GUEST), norms_at=4 * SUBS, norms=1024, late_back=1,
+            after={
+                1: back_conv,
+                2: first_slopes,
+                3: back_and_share,
+                4: lambda: share(r0, 0, 0),
+                8: lambda: share_out(3),
+                10: lambda: share_out(2),
             },
-            lend=(2, 3), helper=2, helper_turn=lambda t: t - 4, norms_at=4 * SUBS,
         )
         for k in (1, 2, 3):
             share_copy(k).wait_send()
@@ -1719,6 +1767,11 @@
             exchange_d6(n).start()
         ob[...] = pt[1]
 
+        def output_copy(k):
+            return remote(pt.at[k], ob, C_SHARE + k % 3, C_SHARE, (k, d, r))
+
+        output_copy(3).start()
+
 
         def sixth_back(n):
             s_du, s_dg = both(28 + 2 * n), both(29 + 2 * n)
@@ -1827,7 +1880,9 @@
             norm_back(u2, n * RW, f3, n * PP, f1, n * PP, par[4 + n] * inv[6 + n], m_du, m_dg)
             return carry
 
-        lax.fori_loop(0, 4, shortcut_back, 0)
+        def all_shortcut_back():
+            lax.fori_loop(0, 4, shortcut_back, 0)
+
         all_sent(wss.at[W_PEER], wx.at[0 : HALF * 128 + 6 * 256])
         all_sent(wss.at[W_Z], wx.at[0 : HALF * 128])
         all_sent(wss.at[W_ON], wx.at[0 : HALF * 128])
@@ -1836,9 +1891,6 @@
         late = [remote(d4, d4, C_D4, C_D4, (2, d, r))]
         for first, last, sem, chip in ((0, 4, C_DG2, 2), (4, 12, C_DG3, 3)):
             late.append(remote(dgx.at[first:last], dgx.at[first:last], sem, sem, (chip, d, r)))
-        later = [
-            remote(pt.at[k], ob, C_SHARE + slot, C_SHARE, (k, d, r)) for slot, k in enumerate((0, 2, 3))
-        ]
 
         def late_sends():
             dh_send.wait_send()
@@ -1866,14 +1918,14 @@
         def shortcut_own():
             r1[...] = shortcut_share(1)
 
+
         def late_shares():
-            for copy in later:
-                copy.start()
             for slot in range(3):
                 share_copy(slot).start()
 
         def at_row(t):
-            return jnp.where(t < 10, t * 512, jnp.where(t < 15, t * 512 + 1024, 5632))
+            early = jnp.where(t == 8, HUB_GUEST, t * 512)
+            return jnp.where(t < 11, early, jnp.where(t < 16, t * 512 + 512, 5632))
 
         def compute(t):
             @pl.when(t < 4)
@@ -1882,37 +1934,44 @@
                 for n in range(4):
                     put_chunk(at_row(t), n, tn(left, pt[4 + n]))
 
-            @pl.when((t >= 4) & (t < 12))
+            @pl.when((t >= 4) & (t < 13))
             def _():
-                m = t - 4
+                m = jnp.where(t < 8, t - 4, t - 5)
                 left = sx[rows((m // 4) * RW, RW), pl.ds(pl.multiple_of(lax.rem(m, 4) * 128, 128), 128)]
                 for n in range(4):
                     put_chunk(at_row(t), n, tn(left, u2[n * RW : (n + 1) * RW, :]))
 
-            @pl.when(t >= 12)
+            @pl.when(t >= 13)
             def _():
-                left = h5[:, pl.ds(pl.multiple_of((t - 12) * 128, 128), 128)]
+                left = h5[:, pl.ds(pl.multiple_of((t - 13) * 128, 128), 128)]
                 for n in range(4):
                     put_chunk(at_row(t), n, tn(left, u1[n * RW : (n + 1) * RW, :]))
 
         zero_rest(12, sb)
         sum_gradients(
-            10, compute, at_row, lambda t: t, True, 0,
+            11, compute, at_row, lambda t: jnp.where(t < 8, t, t - 1), True, 0,
             {
+                1: all_shortcut_back,
                 2: lambda: shortcut_shares(0),
                 4: lambda: shortcut_shares(1),
                 5: late_sends,
                 6: lambda: shortcut_shares(2),
                 8: shortcut_own,
-                14: late_shares,
-                LAST_TURN + 10 * SUBS: final_part,
+                7: lambda: output_copy(2).start(),
+                11: lambda: output_copy(0).start(),
+                15: late_shares,
+                LAST_TURN + 11 * SUBS: final_part,
             },
-            lend=(3, 5), passed=(7, 9, 11, 13), helper=3, helper_turn=lambda t: t - 6, norms_at=2,
-        )
-        for copy in [d5_send, o1_copy(0, 2)] + [o1_copy(n, 3) for n in (1, 2, 3)] + late + later:
+            lend=(3, 5), passed=(7, 9, 11, 13), helper=lambda t: 3, helper_turn=lambda t: t - 7, norms_at=2,
+            handed_in=lambda t: t == 8, lent_by=(lambda t: t == 8, lambda t: 0, lambda t: t + 2, 1), back=R_BACK_HUB,
+            computed=(0, 10), packed_here=(0, 10),
+        )
+        for copy in [d5_send, o1_copy(0, 2)] + [o1_copy(n, 3) for n in (1, 2, 3)] + late:
             copy.wait_send()
         for slot in range(3):
             share_copy(slot).wait_send()
+        for k in (0, 2, 3):
+            output_copy(k).wait_send()
 
 
     @pl.when(p == 2)
@@ -1960,7 +2019,7 @@
                 tap = jnp.where(t < 5, t + 4, t - 11)
                 wh[rows(t * 512, 512), :] = tn(pt[tap], d5[...]).astype(BF16)
 
-            @pl.when(t == 7)
+            @pl.when(t == 5)
             def _():
                 remote(d4, d4, C_D4, C_D4, (2, d, r)).wait_recv()
                 for n in range(4):
@@ -1968,19 +2027,23 @@
 
             @pl.when(jnp.logical_not(taps))
             def _():
-                wh[rows(t * 512, 512), :] = tn(u0[rows((t - 7) * RW, RW), :], d4[...]).astype(BF16)
+                n = jnp.where(t < 7, t - 5, t - 7)
+                wh[rows(t * 512, 512), :] = tn(u0[rows(n * RW, RW), :], d4[...]).astype(BF16)
+
+        def chunk_of(t):
+            return jnp.where(t < 5, t + 8, jnp.where(t < 7, t - 5, t - 7))
 
         def norm_grads():
             remote(dgx.at[0:4], dgx.at[0:4], C_DG2, C_DG2, (2, d, r)).wait_recv()
             dg[0], dg[1], dg[8], dg[9] = dgx[0], dgx[1], dgx[2], dgx[3]
 
         sum_gradients(
-            11, compute, lambda t: t * 512, lambda t: jnp.where(t < 5, t + 8, t - 7), False, 0,
+            11, compute, lambda t: t * 512, chunk_of, False, 0,
             {6 * SUBS: norm_grads, LAST_TURN + 11 * SUBS: final_part},
-            lend=(2, 3, 4, 6), helper=3, helper_turn=lambda t: t - 11,
-            handed_in=lambda t: (t >= 5) & (t < 7),
-            lent_by=(lambda t: (t >= 5) & (t < 7), lambda t: 0, lambda t: t + 4, 2),
-            computed=(0, 9), packed_here=(0, 9), norms_at=6 * SUBS,
+            lend=(2, 3, 4, 6), helper=lambda t: 3, helper_turn=lambda t: t - 11,
+            handed_in=lambda t: (t >= 7) & (t < 9),
+            lent_by=(lambda t: (t >= 7) & (t < 9), lambda t: 0, lambda t: t + 1, 2),
+            computed=(0, 9), packed_here=(0, 9), norms_at=6 * SUBS, norms=1024,
         )
         par_send.wait_send()
 
@@ -2020,8 +2083,8 @@
             10, lambda t: None, lambda t: t * 512, lambda t: t - 6, True, 0,
             {5 * SUBS: norm_grads, LAST_TURN + 10 * SUBS: final_part},
             handed_in=lambda t: t >= 0,
-            lent_by=(lambda t: t < 6, lambda t: jnp.where(t < 4, 2, 1), lambda t: jnp.where(t < 4, t + 11, t + 6), 6),
-            computed=(0, 0), packed_here=(6, 4), norms_at=5 * SUBS,
+            lent_by=(lambda t: t < 6, lambda t: jnp.where(t < 4, 2, 1), lambda t: jnp.where(t < 4, t + 11, t + 7), 6),
+            computed=(0, 0), packed_here=(6, 4), norms_at=5 * SUBS, norms=2048,
         )
         for n in (1, 2, 3):
             o1_copy(n, 2).wait_send()
@@ -2094,7 +2157,6 @@
 
 def one_kernel(images, section_weights, bn_gain, bn_bias, width, bn_set, gate, cotangent):
     any_space = pl.BlockSpec(memory_space=pl.ANY)
-    vmem = pl.BlockSpec(memory_space=pltpu.VMEM)
     smem = pl.BlockSpec(memory_space=pltpu.SMEM)
     out, gi, dw, dgb = pl.pallas_call(
         whole_kernel,
@@ -2104,13 +2166,13 @@
             jax.ShapeDtypeStruct((P_SIZE // SUB, 512, 128), BF16),
             jax.ShapeDtypeStruct((8, 4096), F32),
         ),
-        in_specs=[any_space, any_space, vmem, vmem, smem, smem, smem, any_space],
+        in_specs=[any_space, any_space, any_space, any_space, smem, smem, smem, any_space],
         out_specs=(any_space,) * 4,
         scratch_shapes=[
             pltpu.VMEM((4, 28, 8, 1024), BF16),
             pltpu.VMEM((RING, 1, SUB), BF16),
             pltpu.VMEM((512, 128), F32),
-            pltpu.VMEM((8704, BLK), BF16),
+            pltpu.VMEM((9216, BLK), BF16),
             pltpu.VMEM((8768, BLK), BF16),
             pltpu.VMEM((4 * PP, 8, BLK), F32),
             pltpu.VMEM((4 * PP, 8, BLK), F32),
@@ -2141,16 +2203,17 @@
             pltpu.VMEM((16, 8, BLK), F32),
             pltpu.VMEM((12, 8, BLK), F32),
             pltpu.VMEM((4, 512, 128), BF16),
-            pltpu.VMEM((4096, BLK), BF16),
+            pltpu.VMEM((4352, BLK), BF16),
             pltpu.VMEM((2, 8, 4096), F32),
             pltpu.VMEM((8, 4096), F32),
             pltpu.VMEM((8, 4096), F32),
             pltpu.VMEM((PIX_OUT, 8, BLK), BF16),
+            pltpu.VMEM((NSETS, 4096), F32),
+            pltpu.VMEM((NSETS, 4096), F32),
             pltpu.SemaphoreType.DMA((19,)),
             pltpu.SemaphoreType.DMA((N_SEM,)),
             pltpu.SemaphoreType.DMA((N_SEM,)),
             pltpu.SemaphoreType.DMA((5,)),
-            pltpu.SemaphoreType.DMA((62,)),
             pltpu.SemaphoreType.DMA((N_SUM_SEND,)),
             pltpu.SemaphoreType.DMA((N_SUM_RECV,)),
             pltpu.SemaphoreType.REGULAR((2,)),

time: 168 us -> 164 us (0.976)
  Pallas kernels: 165 us -> 163 us
    pallas_call x1, Pallas kernels: 157 us -> 154 us  [one_kernel(): pl.pallas_call(whole_kernel, out_shape=(jax.ShapeDtypeStruct((PIX_OUT, 8,...]
where the time goes in v5:
time: 164 us; the launch traced here: 163 us
  Pallas kernels  163 us (99%)
    pallas_call x1, Pallas kernels, one_kernel(): pl.pallas_call(whole_kernel, out_shape=(jax.ShapeDtypeStruct((PIX_OUT, 8,...  154 us
    pallas_call x1, Pallas kernels, widen(): pl.pallas_call(widen_kernel, out_shape=(jax.ShapeDtypeStruct(out.shape, o...  8.68 us

profile of v5, /device:TPU:5, one launch (start us, length us, event | category | flops | bytes accessed | tf_op | source)
XLA Modules:
  0.0 163.5 jit_solution(7894765261271423400)
XLA Ops:
  0.6 154.0 %shard_map.119 = (bf16[49,8,512]{2,1,0:T(8,128)(2,1)}, f32[196,8,256]{2,1,0:T(8,128)}, bf16[52,512,128]{2,1,0:T(8,128)(2,1)}, f32[8,4096]{1,0:T(8,128)}) custom-call(bf16[196,8,1024]{2,1,0:T(8,128)(2,1)} %bitcast.13, bf16[1,3407872]{1,0:T(2,128)(2,1)} %wts.1, f32[4,4096]{1,0:T(4,128)} %bitcast.15, f32[4,4096]{1,0:T(4,128)} %bitcast.16, s32[2,8]{1,0:T(2,128)} %bitcast.17, ...), custom_call_target="tpu_custom_call" | custom-call | tf_op jit(solution)/shard_map/pallas_call | solution.py:2161
  154.6 8.7 %shard_map.120 = (bf16[49,8,512]{2,1,0:T(8,128)(2,1)}, f32[196,8,256]{2,1,0:T(8,128)}, f32[26624,128]{1,0:T(8,128)}, f32[4,4096]{1,0:T(4,128)}, f32[4,4096]{1,0:T(4,128)}) custom-call(bf16[49,8,512]{2,1,0:T(8,128)(2,1)} %get-tuple-element.14.out_in, f32[196,8,256]{2,1,0:T(8,128)} %get-tuple-element.15.gi_in, bf16[26624,128]{1,0:T(8,128)(2,1)} %bitcast.12, ...), custom_call_target="tpu_custom_call" | custom-call | tf_op jit(solution)/shard_map/pallas_call | solution.py:2134

commit v6 on v5

--- a/solution.py
+++ b/solution.py
@@ -760,7 +760,7 @@
     zero_stats = (jnp.zeros((8, BLK), F32), jnp.zeros((8, BLK), F32))
 
     def store_z(ref, first, z, slot_sum, slot_square):
-        z3 = z.reshape(PP, 8, BLK)
+        z3 = z.reshape(PP, 8, BLK) if z.ndim == 2 else z
         ref[pl.ds(first, PP)] = z3
         tx[slot_sum] = jnp.sum(z3, axis=0)
         tx[slot_square] = jnp.sum(z3 * z3, axis=0)
@@ -1687,6 +1687,7 @@
         o1_copy(0, 2).start()
         pass_on(5)
         build_patches(plain_base)
+        pass_on(6)
 
         def fifth_conv(taps):
             left = jnp.concatenate([pt[t] for t in taps], axis=1)
@@ -1696,24 +1697,22 @@
         for i in (4, 5, VIA):
             have(i)
         zhat5[...] = fifth_conv((0, 1, 4))
-        pass_half(14)
-        pass_on(6)
+        pass_half(HALF + 1)
+        pass_on(7)
         for i in (6, VIA + 1, VIA + 2):
             have(i)
         zhat5[...] += fifth_conv((2, 5, 6))
-        pass_half(HALF + 1)
-        pass_on(7)
         have(7)
         have_half(HALF)
         have_half(HALF + 1)
-        zhat5[...] += fifth_conv((3, 7, 8))
-        pass_half(15)
-        stats_of_map(zhat5, 18, 19)
-        sync(1, 18, 2)
+        store_z(zhat5, 0, zhat5[...] + fifth_conv((3, 7, 8)), 18, 19)
+        exchange_z5 = exchange_of(1, 18, 2)
+        exchange_z5.start()
+        pass_half(14)
+        exchange_z5.wait()
         center, scale = moments(18, 19, total_out, 11)
         act_to(zhat5, h5, center, scale, g5, b5, mask)
 
-        pass_half(16)
 
         def sixth_conv(n):
             have_half(13 + n)
@@ -1753,18 +1752,26 @@
             exchange_z6(n).start()
         remote(parx.at[4:12], parx.at[4:12], C_PAR3, C_PAR3, (1, d, r)).wait_recv()
         pltpu.make_async_copy(cot, cotb.at[0:PIX_OUT], ls.at[16]).wait()
-        for n in range(4):
-            if n < 2:
-                have_half(15 + n)
-            exchange_z6(n).wait()
-            if n < 2:
-                store_z(
-                    f2, (n + 2) * PP, nn(h5[...], wx[7680 + n * 512 : 8192 + n * 512, :]), 24 + 2 * n, 25 + 2 * n
-                )
-            finish(n)
-            if n < 2:
-                exchange_z6(n + 2).start()
-            exchange_d6(n).start()
+        pass_half(15)
+        exchange_z6(0).wait()
+        finish(0)
+        exchange_d6(0).start()
+        pass_half(16)
+        exchange_z6(1).wait()
+        finish(1)
+        exchange_d6(1).start()
+        have_half(15)
+        store_z(f2, 2 * PP, nn(h5[...], wx[7680:8192, :]), 24, 25)
+        exchange_z6(2).start()
+        have_half(16)
+        store_z(f2, 3 * PP, nn(h5[...], wx[8192:8704, :]), 26, 27)
+        exchange_z6(3).start()
+        exchange_z6(2).wait()
+        finish(2)
+        exchange_d6(2).start()
+        exchange_z6(3).wait()
+        finish(3)
+        exchange_d6(3).start()
         ob[...] = pt[1]
 
         def output_copy(k):

time: 164 us -> 162 us (0.988)
  Pallas kernels: 163 us -> 161 us
    pallas_call x1, Pallas kernels: 154 us -> 152 us  [one_kernel(): pl.pallas_call(whole_kernel, out_shape=(jax.ShapeDtypeStruct((PIX_OUT, 8,...]
where the time goes in v6:
time: 162 us
  Pallas kernels  161 us (99%)
    pallas_call x1, Pallas kernels, one_kernel(): pl.pallas_call(whole_kernel, out_shape=(jax.ShapeDtypeStruct((PIX_OUT, 8,...  152 us
    pallas_call x1, Pallas kernels, widen(): pl.pallas_call(widen_kernel, out_shape=(jax.ShapeDtypeStruct(out.shape, o...  8.68 us

profile of v6, /device:TPU:5, one launch (start us, length us, event | category | flops | bytes accessed | tf_op | source)
XLA Modules:
  0.0 161.6 jit_solution(13127460310492421656)
XLA Ops:
  0.6 152.1 %shard_map.119 = (bf16[49,8,512]{2,1,0:T(8,128)(2,1)}, f32[196,8,256]{2,1,0:T(8,128)}, bf16[52,512,128]{2,1,0:T(8,128)(2,1)}, f32[8,4096]{1,0:T(8,128)}) custom-call(bf16[196,8,1024]{2,1,0:T(8,128)(2,1)} %bitcast.13, bf16[1,3407872]{1,0:T(2,128)(2,1)} %wts.1, f32[4,4096]{1,0:T(4,128)} %bitcast.15, f32[4,4096]{1,0:T(4,128)} %bitcast.16, s32[2,8]{1,0:T(2,128)} %bitcast.17, ...), custom_call_target="tpu_custom_call" | custom-call | tf_op jit(solution)/shard_map/pallas_call | solution.py:2168
  152.7 8.7 %shard_map.120 = (bf16[49,8,512]{2,1,0:T(8,128)(2,1)}, f32[196,8,256]{2,1,0:T(8,128)}, f32[26624,128]{1,0:T(8,128)}, f32[4,4096]{1,0:T(4,128)}, f32[4,4096]{1,0:T(4,128)}) custom-call(bf16[49,8,512]{2,1,0:T(8,128)(2,1)} %get-tuple-element.14.out_in, f32[196,8,256]{2,1,0:T(8,128)} %get-tuple-element.15.gi_in, bf16[26624,128]{1,0:T(8,128)(2,1)} %bitcast.12, ...), custom_call_target="tpu_custom_call" | custom-call | tf_op jit(solution)/shard_map/pallas_call | solution.py:2141

commit v7 on v6

--- a/solution.py
+++ b/solution.py
@@ -1789,11 +1789,10 @@
                 s_du * (1.0 / total_out), s_dg * (1.0 / total_out), unrolled=True,
             )
 
-        for n in range(4):
-            exchange_d6(n).wait()
         grad = jnp.zeros((RW, BLK), F32)
         for n in range(5):
             if n < 4:
+                exchange_d6(n).wait()
                 sixth_back(n)
             if n > 0:
                 grad += nt(u1[(n - 1) * RW : n * RW, :], wx[6144 + n * 512 : 6656 + n * 512, :])
@@ -1864,11 +1863,10 @@
                 pt.at[4 + n], 0, f3, n * PP, f0, n * PP, par[n] * inv[2 + n], m_du, m_dg, unrolled=True
             )
 
-        for n in range(4):
-            exchange_d1(n).wait()
         grad = jnp.zeros((RW, BLK), F32)
         for n in range(5):
             if n < 4:
+                exchange_d1(n).wait()
                 third_back(n)
             if n > 0:
                 grad += nt(pt[3 + n], wh[(n - 1) * 512 : n * 512, :])
@@ -1926,6 +1924,10 @@
             r1[...] = shortcut_share(1)
 
 
+        def own_and_output():
+            shortcut_own()
+            output_copy(2).start()
+
         def late_shares():
             for slot in range(3):
                 share_copy(slot).start()
@@ -1957,17 +1959,16 @@
         zero_rest(12, sb)
         sum_gradients(
             11, compute, at_row, lambda t: jnp.where(t < 8, t, t - 1), True, 0,
-            {
+            {LAST_TURN + 11 * SUBS: final_part},
+            after={
                 1: all_shortcut_back,
                 2: lambda: shortcut_shares(0),
                 4: lambda: shortcut_shares(1),
                 5: late_sends,
                 6: lambda: shortcut_shares(2),
-                8: shortcut_own,
-                7: lambda: output_copy(2).start(),
+                7: own_and_output,
                 11: lambda: output_copy(0).start(),
                 15: late_shares,
-                LAST_TURN + 11 * SUBS: final_part,
             },
             lend=(3, 5), passed=(7, 9, 11, 13), helper=lambda t: 3, helper_turn=lambda t: t - 7, norms_at=2,
             handed_in=lambda t: t == 8, lent_by=(lambda t: t == 8, lambda t: 0, lambda t: t + 2, 1), back=R_BACK_HUB,
@@ -2106,10 +2107,10 @@
 
 
 def widen_kernel(out_in, gi_in, dw_in, dgb_in, out, gi, dw, gain, bias, v_out, v_gi, v_dw, v_wide, v_dgb, sin, sout):
-    count = v_dw.shape[0] // 2048
+    count = v_dw.shape[0] // 3328
 
     def part(i):
-        return pl.ds(i * 2048, 2048)
+        return pl.ds(i * 3328, 3328)
 
     loads = [pltpu.make_async_copy(dw_in.at[part(i)], v_dw.at[part(i)], sin.at[i]) for i in range(count)]
     others = (
@@ -2118,7 +2119,7 @@
         (gi_in, v_gi, ((v_gi, gi),)),
     )
     more = [pltpu.make_async_copy(a, b, sin.at[count + k]) for k, (a, b, _) in enumerate(others)]
-    for copy in loads + more:
+    for copy in more + loads:
         copy.start()
     stores = []
     for i in range(count):
@@ -2136,7 +2137,7 @@
 
 
 def widen(out, gi, dw, dgb):
-    count = P_SIZE // 128 // 2048
+    count = P_SIZE // 128 // 3328
     any_space = pl.BlockSpec(memory_space=pl.ANY)
     return pl.pallas_call(
         widen_kernel,

time: 162 us -> 161 us (level)
  no operation moved by 1% of the time
where the time goes in v7:
time: 161 us
  Pallas kernels  160 us (99%)
    pallas_call x1, Pallas kernels, one_kernel(): pl.pallas_call(whole_kernel, out_shape=(jax.ShapeDtypeStruct((PIX_OUT, 8,...  152 us
    pallas_call x1, Pallas kernels, widen(): pl.pallas_call(widen_kernel, out_shape=(jax.ShapeDtypeStruct(out.shape, o...  7.9 us

profile of v7, /device:TPU:5, one launch (start us, length us, event | category | flops | bytes accessed | tf_op | source)
XLA Modules:
  0.0 160.8 jit_solution(5360026478492274714)
XLA Ops:
  0.6 152.1 %shard_map.119 = (bf16[49,8,512]{2,1,0:T(8,128)(2,1)}, f32[196,8,256]{2,1,0:T(8,128)}, bf16[52,512,128]{2,1,0:T(8,128)(2,1)}, f32[8,4096]{1,0:T(8,128)}) custom-call(bf16[196,8,1024]{2,1,0:T(8,128)(2,1)} %bitcast.13, bf16[1,3407872]{1,0:T(2,128)(2,1)} %wts.1, f32[4,4096]{1,0:T(4,128)} %bitcast.15, f32[4,4096]{1,0:T(4,128)} %bitcast.16, s32[2,8]{1,0:T(2,128)} %bitcast.17, ...), custom_call_target="tpu_custom_call" | custom-call | tf_op jit(solution)/shard_map/pallas_call | solution.py:2169
  152.7 7.9 %shard_map.120 = (bf16[49,8,512]{2,1,0:T(8,128)(2,1)}, f32[196,8,256]{2,1,0:T(8,128)}, f32[26624,128]{1,0:T(8,128)}, f32[4,4096]{1,0:T(4,128)}, f32[4,4096]{1,0:T(4,128)}) custom-call(bf16[49,8,512]{2,1,0:T(8,128)(2,1)} %get-tuple-element.14.out_in, f32[196,8,256]{2,1,0:T(8,128)} %get-tuple-element.15.gi_in, bf16[26624,128]{1,0:T(8,128)(2,1)} %bitcast.12, ...), custom_call_target="tpu_custom_call" | custom-call | tf_op jit(solution)/shard_map/pallas_call | solution.py:2142

commit v8 on v7

--- a/solution.py
+++ b/solution.py
@@ -1418,10 +1418,14 @@
             z = nn(rows_q, wh[0:1024, :]).reshape(28, 8, BLK)
             f0[pl.ds(q * 28, 28)] = z
             load_weights(plain, 44, 8 + 5 * q, 5, put_w)
+
+            @pl.when(q == 5)
+            def _():
+                relay(VIA)
+
             return add_stats(carry, z, z * z)
 
         tx[0], tx[1] = over_images(first_conv, zero_stats)
-        relay(VIA)
         exchange = remote(tx.at[pl.ds(0, 2)], rx.at[pl.ds(0, 2)], 0, 0, peer)
         exchange.start()
         pb[...] = jnp.zeros_like(pb)
@@ -1855,6 +1859,11 @@
                 carried_back(n + 1)
             first_block_slopes(n)
             exchange_d1(n).start()
+            if n == 2:
+                all_sent(wss.at[W_PEER], wx.at[0 : HALF * 128 + 6 * 256])
+                all_sent(wss.at[W_Z], wx.at[0 : HALF * 128])
+                all_sent(wss.at[W_ON], wx.at[0 : HALF * 128])
+                say_ready()
 
         def third_back(n):
             first = 40 + 3 * n
@@ -1888,10 +1897,6 @@
         def all_shortcut_back():
             lax.fori_loop(0, 4, shortcut_back, 0)
 
-        all_sent(wss.at[W_PEER], wx.at[0 : HALF * 128 + 6 * 256])
-        all_sent(wss.at[W_Z], wx.at[0 : HALF * 128])
-        all_sent(wss.at[W_ON], wx.at[0 : HALF * 128])
-        say_ready()
 
         late = [remote(d4, d4, C_D4, C_D4, (2, d, r))]
         for first, last, sem, chip in ((0, 4, C_DG2, 2), (4, 12, C_DG3, 3)):

time: 161 us -> 161 us (level)
  no operation moved by 1% of the time
where the time goes in v8:
time: 161 us
  Pallas kernels  160 us (99%)
    pallas_call x1, Pallas kernels, one_kernel(): pl.pallas_call(whole_kernel, out_shape=(jax.ShapeDtypeStruct((PIX_OUT, 8,...  152 us
    pallas_call x1, Pallas kernels, widen(): pl.pallas_call(widen_kernel, out_shape=(jax.ShapeDtypeStruct(out.shape, o...  7.9 us

profile of v8, /device:TPU:5, one launch (start us, length us, event | category | flops | bytes accessed | tf_op | source)
XLA Modules:
  0.0 160.8 jit_solution(8535624540295131978)
XLA Ops:
  0.6 152.1 %shard_map.119 = (bf16[49,8,512]{2,1,0:T(8,128)(2,1)}, f32[196,8,256]{2,1,0:T(8,128)}, bf16[52,512,128]{2,1,0:T(8,128)(2,1)}, f32[8,4096]{1,0:T(8,128)}) custom-call(bf16[196,8,1024]{2,1,0:T(8,128)(2,1)} %bitcast.13, bf16[1,3407872]{1,0:T(2,128)(2,1)} %wts.1, f32[4,4096]{1,0:T(4,128)} %bitcast.15, f32[4,4096]{1,0:T(4,128)} %bitcast.16, s32[2,8]{1,0:T(2,128)} %bitcast.17, ...), custom_call_target="tpu_custom_call" | custom-call | tf_op jit(solution)/shard_map/pallas_call | solution.py:2174
  152.7 7.9 %shard_map.120 = (bf16[49,8,512]{2,1,0:T(8,128)(2,1)}, f32[196,8,256]{2,1,0:T(8,128)}, f32[26624,128]{1,0:T(8,128)}, f32[4,4096]{1,0:T(4,128)}, f32[4,4096]{1,0:T(4,128)}) custom-call(bf16[49,8,512]{2,1,0:T(8,128)(2,1)} %get-tuple-element.14.out_in, f32[196,8,256]{2,1,0:T(8,128)} %get-tuple-element.15.gi_in, bf16[26624,128]{1,0:T(8,128)(2,1)} %bitcast.12, ...), custom_call_target="tpu_custom_call" | custom-call | tf_op jit(solution)/shard_map/pallas_call | solution.py:2147

commit v9 on v7

--- a/solution.py
+++ b/solution.py
@@ -1841,7 +1841,7 @@
                 do = u2[n * RW + i * 80 : n * RW + (i + 1) * 80, :].astype(F32).reshape(10, 8, BLK)
                 do += f2[pl.ds((n % 2) * PP + i * 10, 10)]
                 a, b_ = f0[part], f1[part]
-                dp = do.astype(BF16).astype(F32) * slope(a * g3 + b_ * gp + b)
+                dp = do * slope(a * g3 + b_ * gp + b)
                 f3[part] = dp
                 s0, s1, s2 = carry
                 return s0 + jnp.sum(dp, axis=0), s1 + jnp.sum(dp * a, axis=0), s2 + jnp.sum(dp * b_, axis=0)

time: 161 us -> 161 us (level)
  no operation moved by 1% of the time
where the time goes in v9:
time: 161 us
  Pallas kernels  160 us (99%)
    pallas_call x1, Pallas kernels, one_kernel(): pl.pallas_call(whole_kernel, out_shape=(jax.ShapeDtypeStruct((PIX_OUT, 8,...  152 us
    pallas_call x1, Pallas kernels, widen(): pl.pallas_call(widen_kernel, out_shape=(jax.ShapeDtypeStruct(out.shape, o...  7.9 us

profile of v9, /device:TPU:5, one launch (start us, length us, event | category | flops | bytes accessed | tf_op | source)
XLA Modules:
  0.0 160.8 jit_solution(8076271457703973180)
XLA Ops:
  0.6 152.1 %shard_map.119 = (bf16[49,8,512]{2,1,0:T(8,128)(2,1)}, f32[196,8,256]{2,1,0:T(8,128)}, bf16[52,512,128]{2,1,0:T(8,128)(2,1)}, f32[8,4096]{1,0:T(8,128)}) custom-call(bf16[196,8,1024]{2,1,0:T(8,128)(2,1)} %bitcast.13, bf16[1,3407872]{1,0:T(2,128)(2,1)} %wts.1, f32[4,4096]{1,0:T(4,128)} %bitcast.15, f32[4,4096]{1,0:T(4,128)} %bitcast.16, s32[2,8]{1,0:T(2,128)} %bitcast.17, ...), custom_call_target="tpu_custom_call" | custom-call | tf_op jit(solution)/shard_map/pallas_call | solution.py:2169
  152.7 7.9 %shard_map.120 = (bf16[49,8,512]{2,1,0:T(8,128)(2,1)}, f32[196,8,256]{2,1,0:T(8,128)}, f32[26624,128]{1,0:T(8,128)}, f32[4,4096]{1,0:T(4,128)}, f32[4,4096]{1,0:T(4,128)}) custom-call(bf16[49,8,512]{2,1,0:T(8,128)(2,1)} %get-tuple-element.14.out_in, f32[196,8,256]{2,1,0:T(8,128)} %get-tuple-element.15.gi_in, bf16[26624,128]{1,0:T(8,128)(2,1)} %bitcast.12, ...), custom_call_target="tpu_custom_call" | custom-call | tf_op jit(solution)/shard_map/pallas_call | solution.py:2142
